TPU v7x, 32 devices: a whole 2x2x4 slice. The times are simulated.
32 devices in a mesh: prime: 4 (over z), row: 8 (over y, x, core).
Axes of the slice: x: 2, y: 2, z: 4, core: 2. Of those that a mesh axis runs over, the one named last changes fastest.
Arguments:
- tile_data: bfloat16 [4, 32, 5, 128, 128], P('prime', 'row'), may hold values from -0.25 to 0.25
- tile_slots: int32 [4, 32, 5], P('prime', 'row'), may hold values from 0 to 19, as said below
- requests: int32 [4, 8, 8, 2], P('prime'), may hold values from 0 to 3, as said below
- start_panel: bfloat16 [4, 4096, 128], P('prime', 'row'), may hold values from -6 to 6
- projectors: bfloat16 [4, 4096, 128], P('prime', 'row'), may hold values from -0.125 to 0.125
- combine_weights: float32 [4, 4], replicated, may hold values from -3 to 3
Outputs:
- projections_mixed: float32 [4, 6, 128, 128], P(None, None, 'row', 'prime')
- final_panel: bfloat16 [4, 4096, 128], P('prime', 'row')
Inputs may be any that keep to these rules, and one draw needn't show every extreme that they name: `tile_slots`: for each system and each device of row, the last slot of each of its 4 block rows is 16 plus the row's index among them, and the other slots of its rows together name each of 0 to 15 exactly once. `requests`: for each system, taking device and source device, the 2 entries are different.
All inputs are finite; a program needn't handle non-finite values.
Results may differ from a plain program's by a relative error of at most 0.02.
Values may be sent and summed in bfloat16 or wider, within the bound.
No kernel may reach another device: no remote copies, remote signals or barrier semaphores. Data moves between devices by JAX's collectives and lax.ppermute only.
A program may use at most 64 MiB of HBM per device.

v0:
```python
import jax
import jax.numpy as jnp
from jax import lax
from jax.sharding import PartitionSpec as P

ITERS = 6


def select_blocks(blocks, positions):
    return blocks[positions]


def shards(tile_data, tile_slots, requests, start_panel, projectors, combine_weights):
    rank_count = lax.axis_size("row")
    my_index = lax.axis_index("row")
    local_primes, local_blocks, stored_tiles, tile_rows, tile_cols = tile_data.shape
    vec_width = start_panel.shape[2]
    fetched = requests.shape[3]
    exchanged = rank_count * fetched
    pick_rows = jax.vmap(select_blocks)
    own_wants = lax.dynamic_index_in_dim(requests, my_index, 1, keepdims=False)
    flat_wants = own_wants.reshape(local_primes, exchanged)
    inside = jnp.clip(tile_slots, 0, exchanged - 1).reshape(local_primes, -1)
    picked = jnp.take_along_axis(flat_wants, inside, axis=1).reshape(tile_slots.shape)
    columns = jnp.where(
        tile_slots < exchanged,
        tile_slots // fetched * local_blocks + picked,
        my_index * local_blocks + tile_slots - exchanged,
    )
    current_panel = start_panel
    projections = []
    for iteration in range(ITERS):
        partial_sum = jnp.einsum(
            "prw,prv->pwv", projectors, current_panel, preferred_element_type=jnp.float32
        )
        projections.append(
            lax.psum_scatter(
                partial_sum.astype(jnp.bfloat16), "row", scatter_dimension=1, tiled=True
            ).astype(jnp.float32)
        )
        gathered = lax.all_gather(current_panel, "row", axis=1, tiled=True)
        gathered = gathered.reshape(local_primes, rank_count * local_blocks, tile_rows, vec_width)
        needed_blocks = pick_rows(gathered, columns)
        product = jnp.einsum(
            "pikab,pikbw->piaw", tile_data, needed_blocks, preferred_element_type=jnp.float32
        )
        current_panel = product.astype(jnp.bfloat16).reshape(
            local_primes, local_blocks * tile_rows, vec_width
        )
    stacked = jnp.stack(projections, axis=1)
    regrouped = lax.all_to_all(stacked, "prime", split_axis=3, concat_axis=0, tiled=True)
    combined = jnp.einsum(
        "qp,pkab->qkab", combine_weights, regrouped, precision=lax.Precision.HIGHEST
    )
    return (combined, current_panel)


def solution(mesh):
    return jax.shard_map(
        shards,
        mesh=mesh,
        in_specs=(
            P("prime", "row", None, None, None),
            P("prime", "row", None),
            P("prime", None, None, None),
            P("prime", "row", None),
            P("prime", "row", None),
            P(),
        ),
        out_specs=(P(None, None, "row", "prime"), P("prime", "row", None)),
        check_vma=False,
    )
```

profile of v0, /device:TPU:0, one launch (start us, length us, event | category | flops | bytes accessed | tf_op | source)
XLA Modules:
  0.0 385.0 jit_solution(10033671958579856215)
XLA Ops:
  7.2 0.7 all-gather.7.cloned.1.call-update
  8.0 0.7 constant_dynamic-slice_fusion
  8.6 0.1 copy.31
  8.7 0.1 reshape.239
  8.8 0.6 copy-done.8
  9.4 0.1 reshape.215
  9.5 0.7 gather_fusion
  10.2 0.1 gather.25
  10.4 0.1 reshape.251
  10.4 25.7 %all-gather.7.cloned.1.call-done = bf16[1,4096,128]{2,1,0:T(8,128)(2,1)} async-done(((bf16[1,512,128]{2,1,0:T(8,128)(2,1)}), bf16[1,4096,128]{2,1,0:T(8,128)(2,1)}) %all-gather.7.cloned.1.call-update) | async-done | bytes 1048592 | tf_op jit(solution)/shard_map/all_gather | solution.py:41
  36.1 1.9 gather_fusion.1
  38.1 1.0 fusion
  39.1 23.6 %all-gather.9.cloned.1.call-done = bf16[1,4096,128]{2,1,0:T(8,128)(2,1)} async-done(((bf16[1,512,128]{2,1,0:T(8,128)(2,1)}), bf16[1,4096,128]{2,1,0:T(8,128)(2,1)}) %all-gather.9.cloned.1.call-update) | async-done | bytes 1048592 | tf_op jit(solution)/shard_map/all_gather | solution.py:41
  62.7 1.9 gather_fusion.2
  64.7 1.0 fusion.1
  65.7 0.0 all-gather.13.cloned.1.call-start
  65.7 23.6 %all-gather.11.cloned.1.call-done = bf16[1,4096,128]{2,1,0:T(8,128)(2,1)} async-done(((bf16[1,512,128]{2,1,0:T(8,128)(2,1)}), bf16[1,4096,128]{2,1,0:T(8,128)(2,1)}) %all-gather.11.cloned.1.call-update) | async-done | bytes 1048592 | tf_op jit(solution)/shard_map/all_gather | solution.py:41
  89.3 1.9 gather_fusion.3
  91.2 1.0 fusion.2
  92.3 0.0 all-gather.15.cloned.1.call-start
  92.3 23.6 %all-gather.13.cloned.1.call-done = bf16[1,4096,128]{2,1,0:T(8,128)(2,1)} async-done(((bf16[1,512,128]{2,1,0:T(8,128)(2,1)}), bf16[1,4096,128]{2,1,0:T(8,128)(2,1)}) %all-gather.13.cloned.1.call-update) | async-done | bytes 1048592 | tf_op jit(solution)/shard_map/all_gather | solution.py:41
  115.9 1.9 gather_fusion.4
  117.8 1.0 fusion.3
  118.9 0.8 copy-done.1
  119.8 0.8 fusion.6
  120.7 0.8 fusion.7
  121.6 0.0 reduce-scatter.11.cloned.1.call-start
  121.6 0.8 fusion.8
  122.5 0.0 reduce-scatter.13.cloned.1.call-start
  122.6 0.8 fusion.9
  123.5 0.8 fusion.10
  124.4 18.1 %all-gather.15.cloned.1.call-done = bf16[1,4096,128]{2,1,0:T(8,128)(2,1)} async-done(((bf16[1,512,128]{2,1,0:T(8,128)(2,1)}), bf16[1,4096,128]{2,1,0:T(8,128)(2,1)}) %all-gather.15.cloned.1.call-update) | async-done | bytes 1048592 | tf_op jit(solution)/shard_map/all_gather | solution.py:41
  142.5 1.9 gather_fusion.5
  144.4 0.3 fusion.4
  144.8 0.8 fusion.11
  145.7 0.0 all-gather.17.cloned.1.call-start
  145.7 0.5 all-gather.17.cloned.1.call-update
  146.2 30.4 %reduce-scatter.7.cloned.1.call-done = bf16[1,16,128]{2,1,0:T(8,128)(2,1)} async-done(((bf16[1,128,128]{2,1,0:T(8,128)(2,1)}), bf16[1,16,128]{2,1,0:T(8,128)(2,1)}) %reduce-scatter.7.cloned.1.call-update) | async-done | bytes 4112 | tf_op jit(solution)/shard_map/reduce_scatter | solution.py:37
  176.7 0.7 constant_dynamic-update-slice_fusion.5
  177.3 33.9 %reduce-scatter.9.cloned.1.call-done = bf16[1,16,128]{2,1,0:T(8,128)(2,1)} async-done(((bf16[1,128,128]{2,1,0:T(8,128)(2,1)}), bf16[1,16,128]{2,1,0:T(8,128)(2,1)}) %reduce-scatter.9.cloned.1.call-update) | async-done | bytes 4112 | tf_op jit(solution)/shard_map/reduce_scatter | solution.py:37
  211.2 0.7 constant_dynamic-update-slice_fusion.4
  211.9 34.2 %reduce-scatter.11.cloned.1.call-done = bf16[1,16,128]{2,1,0:T(8,128)(2,1)} async-done(((bf16[1,128,128]{2,1,0:T(8,128)(2,1)}), bf16[1,16,128]{2,1,0:T(8,128)(2,1)}) %reduce-scatter.11.cloned.1.call-update) | async-done | bytes 4112 | tf_op jit(solution)/shard_map/reduce_scatter | solution.py:37
  246.1 0.7 constant_dynamic-update-slice_fusion.3
  246.8 33.9 %reduce-scatter.13.cloned.1.call-done = bf16[1,16,128]{2,1,0:T(8,128)(2,1)} async-done(((bf16[1,128,128]{2,1,0:T(8,128)(2,1)}), bf16[1,16,128]{2,1,0:T(8,128)(2,1)}) %reduce-scatter.13.cloned.1.call-update) | async-done | bytes 4112 | tf_op jit(solution)/shard_map/reduce_scatter | solution.py:37
  280.7 0.7 constant_dynamic-update-slice_fusion.2
  281.4 33.5 %reduce-scatter.15.cloned.1.call-done = bf16[1,16,128]{2,1,0:T(8,128)(2,1)} async-done(((bf16[1,128,128]{2,1,0:T(8,128)(2,1)}), bf16[1,16,128]{2,1,0:T(8,128)(2,1)}) %reduce-scatter.15.cloned.1.call-update) | async-done | bytes 4112 | tf_op jit(solution)/shard_map/reduce_scatter | solution.py:37
  314.8 0.7 constant_dynamic-update-slice_fusion.1
  315.5 33.9 %reduce-scatter.17.cloned.1.call-done = bf16[1,16,128]{2,1,0:T(8,128)(2,1)} async-done(((bf16[1,128,128]{2,1,0:T(8,128)(2,1)}), bf16[1,16,128]{2,1,0:T(8,128)(2,1)}) %reduce-scatter.17.cloned.1.call-update) | async-done | bytes 4112 | tf_op jit(solution)/shard_map/reduce_scatter | solution.py:37
  349.4 0.7 constant_dynamic-update-slice_fusion
  350.1 0.3 copy.37
  350.4 0.5 broadcast.183
  350.9 1.6 reduce
  352.6 0.2 reshape.318
  352.8 10.1 %all_to_all.18 = f32[4,1,3072]{2,1,0:T(1,128)S(1)} all-to-all(f32[4,1,3072]{2,1,0:T(1,128)S(1)} %reshape.318), channel_id=1, replica_groups=mesh['prime'=4,'row'=8] {'prime'}, dimensions={0} | all-to-all | bytes 98304 | tf_op jit(solution)/shard_map/all_to_all | solution.py:51
  362.9 0.8 reduce.1
  363.7 0.7 reshape.319
  364.4 0.3 copy.38
  364.7 0.1 all_to_all.14
  364.9 0.5 copy-done.9
  365.4 0.5 convolution_bitcast_fusion.6
  365.8 0.7 copy.39
  366.5 8.7 %all-gather.17.cloned.1.call-done = bf16[1,4096,128]{2,1,0:T(8,128)(2,1)} async-done(((bf16[1,512,128]{2,1,0:T(8,128)(2,1)}), bf16[1,4096,128]{2,1,0:T(8,128)(2,1)}) %all-gather.17.cloned.1.call-update) | async-done | bytes 1048592 | tf_op jit(solution)/shard_map/all_gather | solution.py:41
  375.3 1.9 gather_fusion.6
  377.2 1.0 fusion.5
  (40 shorter events, 0.5 us)
Async XLA Ops:
  7.2 30.9 %copy-start = (bf16[1,4,5,128,128]{4,3,2,1,0:T(8,128)(2,1)S(1)}, bf16[1,4,5,128,128]{4,3,2,1,0:T(8,128)(2,1)}, u32[]{:S(2)}) copy-start(bf16[1,4,5,128,128]{4,3,2,1,0:T(8,128)(2,1)} %param.6) | copy-start | bytes 1966084
  7.2 28.9 %all-gather.7.cloned.1.call-start = ((), (), s32[]{:S(2)}) async-start(), calls=%async_computation.8 | async-start | bytes 1179648 | tf_op jit(solution)/shard_map/all_gather | solution.py:41
  7.9 54.8 %all-gather.9.cloned.1.call-start = ((), (), s32[]{:S(2)}) async-start(), calls=%async_computation.10 | async-start | bytes 1179648 | tf_op jit(solution)/shard_map/all_gather | solution.py:41
  8.7 0.7 copy-start.8
  39.1 50.2 %all-gather.11.cloned.1.call-start = ((), (), s32[]{:S(2)}) async-start(), calls=%async_computation.12 | async-start | bytes 1179648 | tf_op jit(solution)/shard_map/all_gather | solution.py:41
  65.7 50.2 %all-gather.13.cloned.1.call-start = ((), (), s32[]{:S(2)}) async-start(), calls=%async_computation.14 | async-start | bytes 1179648 | tf_op jit(solution)/shard_map/all_gather | solution.py:41
  92.3 50.3 %all-gather.15.cloned.1.call-start = ((), (), s32[]{:S(2)}) async-start(), calls=%async_computation.16 | async-start | bytes 1179648 | tf_op jit(solution)/shard_map/all_gather | solution.py:41
  117.8 1.1 copy-start.7
  118.8 0.9 copy-start.1
  118.9 1.8 copy-start.3
  118.9 57.8 %reduce-scatter.7.cloned.1.call-start = ((), (), s32[]{:S(2)}) async-start(), calls=%async_computation.7 | async-start | bytes 36864 | tf_op jit(solution)/shard_map/reduce_scatter | solution.py:37
  120.6 90.6 %reduce-scatter.9.cloned.1.call-start = ((), (), s32[]{:S(2)}) async-start(), calls=%async_computation.9 | async-start | bytes 36864 | tf_op jit(solution)/shard_map/reduce_scatter | solution.py:37
  120.7 0.9 copy-start.4
  121.6 124.5 %reduce-scatter.11.cloned.1.call-start = ((), (), s32[]{:S(2)}) async-start(), calls=%async_computation.11 | async-start | bytes 36864 | tf_op jit(solution)/shard_map/reduce_scatter | solution.py:37
  121.6 0.9 copy-start.6
  122.5 158.2 %reduce-scatter.13.cloned.1.call-start = ((), (), s32[]{:S(2)}) async-start(), calls=%async_computation.13 | async-start | bytes 36864 | tf_op jit(solution)/shard_map/reduce_scatter | solution.py:37
  122.6 0.9 copy-start.5
  123.4 191.4 %reduce-scatter.15.cloned.1.call-start = ((), (), s32[]{:S(2)}) async-start(), calls=%async_computation.15 | async-start | bytes 36864 | tf_op jit(solution)/shard_map/reduce_scatter | solution.py:37
  124.4 225.1 %reduce-scatter.17.cloned.1.call-start = ((), (), s32[]{:S(2)}) async-start(), calls=%async_computation.17 | async-start | bytes 36864 | tf_op jit(solution)/shard_map/reduce_scatter | solution.py:37
  144.8 0.9 copy-start.2
  145.7 229.6 %all-gather.17.cloned.1.call-start = ((), (), s32[]{:S(2)}) async-start(), calls=%async_computation.18 | async-start | bytes 1179648 | tf_op jit(solution)/shard_map/all_gather | solution.py:41
  364.7 0.7 copy-start.9
Sparse Core Ops, SparseCore 0:
  9.9 26.1 all-gather.6
  39.2 23.4 all-gather.8
  65.8 23.4 all-gather.10
  92.4 23.4 all-gather.12
  119.0 23.4 all-gather.14
  145.4 31.2 reduce-scatter.6
  179.9 31.2 reduce-scatter.8
  214.8 31.2 reduce-scatter.10
  249.4 31.2 reduce-scatter.12
  283.5 31.2 reduce-scatter.14
  318.1 31.2 reduce-scatter.16
  351.7 23.4 all-gather.16
where the time goes:
time: 386 us; the launch traced here: 385 us
  waiting for transfers between devices  324 us (84%)
  local copies, waits for them, and re-layouts  22.3 us (6%)
  between operations  14.5 us (4%)
  matrix products  10.8 us (3%)
  blocking collectives  10.1 us (3%)
    reduce_scatter x6, waiting for transfers between devices, shards(): lax.psum_scatter(partial_sum.astype(jnp.bfloat16), 'row', scatter_dimensi...  200 us
    all_gather x6, waiting for transfers between devices, shards(): gathered = lax.all_gather(current_panel, 'row', axis=1, tiled=True)  123 us
    gather x8, local copies, waits for them, and re-layouts, select_blocks(): return blocks[positions]  11.6 us
    all_to_all x1, blocking collectives, shards(): lax.all_to_all(stacked, 'prime', split_axis=3, concat_axis=0, tiled=True)  10.1 us
  transfers between devices with their start and end apart: 12, of which 12 were waited for; matrix products, arithmetic and copies ran while one was open for 5% of the time, Pallas kernels for 0%

commit v1 on v0

v1 whole, which is shorter than its diff:
```python
import functools

import jax
import jax.numpy as jnp
from jax import lax
from jax.experimental import pallas as pl
from jax.experimental.pallas import tpu as pltpu
from jax.sharding import PartitionSpec as P

ITERS = 6
WHOLE_BYTES = 12 << 20
VMEM_BYTES = 48 << 20


def bits_apart(ranks, distance):
    return [(rank, rank ^ distance) for rank in range(ranks)]


def column_order(shape, my_row, ranks, primes):
    width = shape[0]
    each = width // (ranks * primes)
    held = lax.broadcasted_iota(jnp.int32, shape, 0)
    column = lax.broadcasted_iota(jnp.int32, shape, 1)
    distance = lax.rem(column // each, ranks) ^ my_row
    place = distance * (primes * each) + column // (ranks * each) * each + lax.rem(column, each)
    return (held == place).astype(jnp.bfloat16)


def split_columns(ranks, primes, row_ref, panel_ref, *out_refs):
    rows, width = panel_ref.shape
    held = width // ranks
    order = column_order((width, width), row_ref[0], ranks, primes)
    turned = lax.dot_general(
        order, panel_ref[...], (((1,), (1,)), ((), ())), preferred_element_type=jnp.float32
    ).astype(jnp.bfloat16)
    size = out_refs[0].shape[3]
    for distance in range(ranks):
        for block in range(rows // size):
            out_refs[distance // 2][distance % 2, block] = turned[
                distance * held : (distance + 1) * held, block * size : (block + 1) * size
            ]


def apply_blocks(columns_ref, tile_refs, load, store):
    first = 0
    for tiles in tile_refs:
        blocks, stored, size, _ = tiles.shape
        for at in range(0, blocks, 2):
            panels, matrices = [], []
            for row in (at, at + 1):
                slots = [(first + row) * stored + k for k in range(stored)]
                panels.append(jnp.concatenate([load(columns_ref[s]) for s in slots], axis=1))
                matrices.append(jnp.concatenate([tiles[row, k] for k in range(stored)], axis=1))
            held = panels[0].shape[0]
            product = lax.dot_general(
                jnp.concatenate(panels, axis=0),
                jnp.concatenate(matrices, axis=0),
                (((1,), (1,)), ((), ())),
                preferred_element_type=jnp.float32,
            ).astype(jnp.bfloat16)
            store(first + at, product[:held, :size])
            store(first + at + 1, product[held:, size:])
        first += blocks


def first_steps(ranks, primes, columns_ref, *refs):
    chips = ranks // 2
    start_near, start_far = refs[:chips], refs[chips : 2 * chips]
    tiles = refs[2 * chips : 2 * chips + ranks]
    projectors = refs[2 * chips + ranks : 2 * chips + 2 * ranks]
    terms_ref, last_ref, history = refs[2 * chips + 2 * ranks :]
    _, blocks, held, size = start_near[0].shape
    for chip in range(chips):
        for block in range(blocks):
            history[2 * chip * blocks + block, :held] = start_near[chip][0, block]
            history[(2 * chip + 1) * blocks + block, :held] = start_far[chip][1, block]
    for step in range(ITERS - 1):
        old, new = slice(step * held, (step + 1) * held), slice((step + 1) * held, (step + 2) * held)

        def load(position):
            return history[position, old]

        def store(position, value):
            history[position, new] = value
            if step == ITERS - 2:
                last_ref[position] = value

        apply_blocks(columns_ref, tiles, load, store)
    total = None
    for rank in range(ranks):
        panels = jnp.concatenate([history[rank * blocks + b] for b in range(blocks)], axis=1)
        part = jnp.dot(panels, projectors[rank][...], preferred_element_type=jnp.float32)
        total = part if total is None else total + part
    each = held // primes
    for prime in range(primes):
        for step in range(ITERS):
            terms_ref[prime, step * each : (step + 1) * each] = total[
                step * held + prime * each : step * held + (prime + 1) * each
            ]


def last_step(columns_ref, panel_ref, *refs):
    tiles, out_ref = refs[:-1], refs[-1]

    def load(position):
        return panel_ref[position]

    def store(position, value):
        out_ref[position] = value

    apply_blocks(columns_ref, tiles, load, store)


def mix_terms(ranks, primes, place_ref, weights_ref, panel_ref, own_ref, *refs):
    others, out_refs = refs[: primes - 1], refs[primes - 1 : -1]
    turned = refs[-1]
    my_prime, my_row = place_ref[0], place_ref[1]
    parts = [own_ref[my_prime]] + [other[...] for other in others]
    rows, width = parts[0].shape
    mixed = []
    for prime in range(primes):
        mixed.append(sum(weights_ref[prime, my_prime ^ bits] * part for bits, part in enumerate(parts)))
    mixed.append(jnp.zeros((width - primes * rows, width), jnp.float32))
    turned[...] = jnp.concatenate(mixed, axis=0).T.astype(jnp.bfloat16).reshape(turned.shape)
    blocks = panel_ref.shape[0] // ranks
    held = panel_ref.shape[1]
    for distance in range(ranks):
        out = out_refs[distance // 2]
        for block in range(blocks):
            out[distance % 2, block * held : (block + 1) * held] = panel_ref[distance * blocks + block]
        out[distance % 2, blocks * held :] = turned[my_row ^ distance]


def join_columns(ranks, primes, row_ref, *refs):
    chips = ranks // 2
    near, far = refs[:chips], refs[chips : 2 * chips]
    mixed_ref, panel_ref = refs[2 * chips :]
    my_row = row_ref[0]
    width = panel_ref.shape[1]
    held = width // ranks
    each = held // primes
    order = column_order((width, width), my_row, ranks, primes)
    pieces = [(near, far)[d % 2][d // 2][d % 2] for d in range(ranks)]
    size = pieces[0].shape[1]
    blocks = panel_ref.shape[0] // size
    for block in range(blocks):
        turned = jnp.concatenate([p[block * held : (block + 1) * held] for p in pieces], axis=0)
        panel_ref[block * size : (block + 1) * size] = lax.dot_general(
            turned, order, (((0,), (0,)), ((), ())), preferred_element_type=jnp.float32
        ).astype(jnp.bfloat16)
    terms = jnp.concatenate([p[blocks * held :] for p in pieces], axis=1)
    part = ranks * each
    together = width // part
    shape = (ranks * width, width)
    source = lax.broadcasted_iota(jnp.int32, shape, 0)
    target = lax.broadcasted_iota(jnp.int32, shape, 1)
    distance = lax.rem(target // each, ranks) ^ my_row
    wanted = distance * width + target // part * each + lax.rem(target, each)
    for group in range(primes * ITERS // together):
        pick = (source == wanted + group * together * each).astype(jnp.bfloat16)
        placed = jnp.dot(terms, pick, preferred_element_type=jnp.float32)
        for at in range(together):
            entry = group * together + at
            mixed_ref[entry // ITERS, entry % ITERS] = placed[:, at * part : (at + 1) * part]


def on_chip(kernel, out_shape, smem, vmem, scratch=(), flops=0, name=None):
    space = [pl.BlockSpec(memory_space=pltpu.SMEM)] * len(smem) + [pl.BlockSpec(memory_space=pltpu.VMEM)] * len(vmem)
    return pl.pallas_call(
        kernel,
        out_shape=out_shape,
        in_specs=space,
        out_specs=jax.tree.map(lambda _: pl.BlockSpec(memory_space=pltpu.VMEM), out_shape),
        scratch_shapes=list(scratch),
        compiler_params=pltpu.CompilerParams(vmem_limit_bytes=VMEM_BYTES),
        cost_estimate=pl.CostEstimate(flops=flops, bytes_accessed=sum(v.size * v.dtype.itemsize for v in vmem), transcendentals=0),
        name=name,
    )(*smem, *vmem)


def own_columns(tile_slots, requests, my_row, ranks):
    blocks, stored = tile_slots.shape
    fetched = requests.shape[2]
    exchanged = ranks * fetched
    wants = lax.dynamic_index_in_dim(requests, my_row, 0, keepdims=False).reshape(exchanged)
    named = tile_slots[..., None] == lax.broadcasted_iota(jnp.int32, (1, 1, exchanged), 2)
    picked = jnp.sum(jnp.where(named, wants[None, None], 0), axis=2)
    return jnp.where(
        tile_slots < exchanged,
        tile_slots // fetched * blocks + picked,
        my_row * blocks + tile_slots - exchanged,
    )


def whole_system(tile_data, tile_slots, requests, start_panel, projectors, combine_weights):
    ranks, primes = lax.axis_size("row"), lax.axis_size("prime")
    chips = ranks // 2
    my_row, my_prime = lax.axis_index("row"), lax.axis_index("prime")
    row_word = my_row.reshape(1)
    tiles, panel, projector = tile_data[0], start_panel[0], projectors[0]
    blocks, stored, size, _ = tiles.shape
    width = panel.shape[1]
    held = width // ranks
    each = held // primes

    def from_chips(own):
        return [own] + [lax.ppermute(own, "row", bits_apart(ranks, 2 * chip)) for chip in range(1, chips)]

    def from_core(arrays):
        return [lax.ppermute(array, "row", bits_apart(ranks, 1)) for array in arrays]

    def by_distance(near, far):
        return [array for pair in zip(near, far) for array in pair]

    tiles_near = from_chips(tiles)
    tiles_far = from_core(tiles_near)
    pieces = on_chip(
        functools.partial(split_columns, ranks, primes),
        [jax.ShapeDtypeStruct((2, blocks, held, size), jnp.bfloat16)] * chips,
        [row_word],
        [panel],
        name="split_columns",
    )
    start_near = [pieces[0]] + [
        lax.ppermute(pieces[chip], "row", bits_apart(ranks, 2 * chip)) for chip in range(1, chips)
    ]
    start_far = from_core(start_near)
    columns = own_columns(tile_slots[0], requests[0], my_row, ranks)
    columns_near = jnp.stack(from_chips(columns))
    columns_far = lax.ppermute(columns_near, "row", bits_apart(ranks, 1))
    columns = jnp.stack([columns_near, columns_far], axis=1).reshape(-1)
    columns = (columns // blocks ^ my_row) * blocks + columns % blocks
    projectors_near = from_chips(projector)
    projectors_far = from_core(projectors_near)

    every_tile = by_distance(tiles_near, tiles_far)
    every_projector = by_distance(projectors_near, projectors_far)
    step_flops = 2 * ranks * tiles.size * held
    terms, panel = on_chip(
        functools.partial(first_steps, ranks, primes),
        [
            jax.ShapeDtypeStruct((primes, ITERS * each, width), jnp.float32),
            jax.ShapeDtypeStruct((ranks * blocks, held, size), jnp.bfloat16),
        ],
        [columns],
        [*start_near, *start_far, *every_tile, *every_projector],
        scratch=[pltpu.VMEM((ranks * blocks, ITERS * held, size), jnp.bfloat16)],
        flops=(ITERS - 1) * step_flops,
        name="first_steps",
    )
    others = [
        lax.ppermute(
            lax.dynamic_index_in_dim(terms, my_prime ^ bits, 0, keepdims=False), "prime", bits_apart(primes, bits)
        )
        for bits in range(1, primes)
    ]
    panel = on_chip(
        last_step,
        jax.ShapeDtypeStruct(panel.shape, jnp.bfloat16),
        [columns],
        [panel, *every_tile],
        flops=step_flops,
        name="last_step",
    )
    pieces = on_chip(
        functools.partial(mix_terms, ranks, primes),
        [jax.ShapeDtypeStruct((2, (blocks + 1) * held, size), jnp.bfloat16)] * chips,
        [jnp.stack([my_prime, my_row]), combine_weights],
        [panel, terms, *others],
        scratch=[pltpu.VMEM((ranks, width // ranks, width), jnp.bfloat16)],
        name="mix_terms",
    )
    near = [pieces[0]] + [lax.ppermute(pieces[chip], "row", bits_apart(ranks, 2 * chip)) for chip in range(1, chips)]
    far = from_core(near)
    mixed, panel = on_chip(
        functools.partial(join_columns, ranks, primes),
        [
            jax.ShapeDtypeStruct((primes, ITERS, width // ranks, width // primes), jnp.float32),
            jax.ShapeDtypeStruct((blocks * size, width), jnp.bfloat16),
        ],
        [row_word],
        [*near, *far],
        name="join_columns",
    )
    return mixed, panel[None]


def split_system(tile_data, tile_slots, requests, start_panel, projectors, combine_weights):
    ranks = lax.axis_size("row")
    my_row = lax.axis_index("row")
    blocks, stored, size, _ = tile_data.shape[1:]
    width = start_panel.shape[2]
    columns = own_columns(tile_slots[0], requests[0], my_row, ranks)
    panel, projector = start_panel[0], projectors[0]
    partial_sums = []
    for step in range(ITERS):
        partial_sums.append(
            jnp.dot(projector.T, panel, preferred_element_type=jnp.float32).astype(jnp.bfloat16)
        )
        gathered = lax.all_gather(panel, "row", axis=0, tiled=True)
        needed = gathered.reshape(ranks * blocks, size, width)[columns]
        product = jnp.einsum("ikab,ikbw->iaw", tile_data[0], needed, preferred_element_type=jnp.float32)
        panel = product.astype(jnp.bfloat16).reshape(blocks * size, width)
    terms = lax.psum_scatter(jnp.stack(partial_sums), "row", scatter_dimension=1, tiled=True).astype(jnp.float32)
    regrouped = lax.all_to_all(terms[None], "prime", split_axis=3, concat_axis=0, tiled=True)
    mixed = jnp.einsum("qp,pkab->qkab", combine_weights, regrouped, precision=lax.Precision.HIGHEST)
    return mixed, panel[None]


def shards(tile_data, *others):
    ranks, primes = lax.axis_size("row"), lax.axis_size("prime")
    whole_bytes = ranks * tile_data.size * tile_data.dtype.itemsize
    fits = whole_bytes <= WHOLE_BYTES and ranks == 8 and primes == 4 and tile_data.shape[3:] == (128, 128)
    return (whole_system if fits else split_system)(tile_data, *others)


def solution(mesh):
    return jax.shard_map(
        shards,
        mesh=mesh,
        in_specs=(
            P("prime", "row", None, None, None),
            P("prime", "row", None),
            P("prime", None, None, None),
            P("prime", "row", None),
            P("prime", "row", None),
            P(),
        ),
        out_specs=(P(None, None, "row", "prime"), P("prime", "row", None)),
        check_vma=False,
    )
```

time: 386 us -> 121 us (0.31)
  waiting for transfers between devices: 324 us -> 46.7 us
  starting transfers between devices: 0.49 us -> 28.2 us
  Pallas kernels: 0 us -> 24.7 us
  between operations: 14.5 us -> 0.85 us
  matrix products: 10.8 us -> 0 us
  blocking collectives: 10.1 us -> 0 us
  local copies, waits for them, and re-layouts: 22.3 us -> 18.4 us
    reduce_scatter x6 -> x0, waiting for transfers between devices: 200 us -> none  [shards(): lax.psum_scatter(partial_sum.astype(jnp.bfloat16), 'row', scatter_dimensi...]
    all_gather x6 -> x0, waiting for transfers between devices: 123 us -> none  [shards(): gathered = lax.all_gather(current_panel, 'row', axis=1, tiled=True)]
    ppermute x0 -> x35, waiting for transfers between devices: none -> 46.7 us  [the longest x9 29.3 us: from_chips(): lax.ppermute(own, 'row', bits_apart(ranks, 2 * chip))]
    ppermute x0 -> x35, starting transfers between devices: none -> 28.2 us  [the longest x9 14.2 us: from_chips(): lax.ppermute(own, 'row', bits_apart(ranks, 2 * chip))]
    pallas_call x0 -> x5, Pallas kernels: none -> 24.7 us  [on_chip(): pl.pallas_call(kernel, out_shape=out_shape, in_specs=space, out_specs=jax...]
    gather x10 -> x0, local copies, waits for them, and re-layouts: 12.4 us -> none  [the longest x8 11.6 us: select_blocks(): return blocks[positions]]
    dot_general x13 -> x0, matrix products: 10.8 us -> none  [the longest x6 5.3 us: shards(): jnp.einsum('pikab,pikbw->piaw', tile_data, needed_blocks, preferred_eleme...]
    all_to_all x1 -> x0, blocking collectives: 10.1 us -> none  [shards(): lax.all_to_all(stacked, 'prime', split_axis=3, concat_axis=0, tiled=True)]
  transfers between devices with their start and end apart: 12 -> 35, of which waited for: 12 -> 16; matrix products, arithmetic and copies ran while one was open for 5% -> 3% of each run, Pallas kernels for 0% -> 3%
where the time goes in v1:
time: 121 us; the launch traced here: 120 us
  waiting for transfers between devices  46.7 us (39%)
  starting transfers between devices  28.2 us (23%)
  Pallas kernels  24.7 us (20%)
  local copies, waits for them, and re-layouts  18.4 us (15%)
    ppermute x9, waiting for transfers between devices, from_chips(): lax.ppermute(own, 'row', bits_apart(ranks, 2 * chip))  29.3 us
    pallas_call x5, Pallas kernels, on_chip(): pl.pallas_call(kernel, out_shape=out_shape, in_specs=space, out_specs=jax...  24.7 us
    unnamed x60, local copies, waits for them, and re-layouts  16.4 us
    ppermute x9, starting transfers between devices, from_chips(): lax.ppermute(own, 'row', bits_apart(ranks, 2 * chip))  14.2 us
    ppermute x16, waiting for transfers between devices, from_core(): lax.ppermute(array, 'row', bits_apart(ranks, 1))  7.25 us
    ppermute x6, starting transfers between devices, whole_system(): lax.ppermute(pieces[chip], 'row', bits_apart(ranks, 2 * chip))  7.04 us
    ppermute x6, waiting for transfers between devices, whole_system(): lax.ppermute(pieces[chip], 'row', bits_apart(ranks, 2 * chip))  6.78 us
    ppermute x3, starting transfers between devices, whole_system(): lax.ppermute(lax.dynamic_index_in_dim(terms, my_prime ^ bits, 0, keepdims...  4.45 us
  transfers between devices with their start and end apart: 35, of which 16 were waited for; matrix products, arithmetic and copies ran while one was open for 3% of the time, Pallas kernels for 3%

profile of v1, /device:TPU:0, one launch (start us, length us, event | category | flops | bytes accessed | tf_op | source)
XLA Modules:
  0.0 120.0 jit_solution(11416332146921298148)
XLA Ops:
  0.7 3.0 %collective-permute-start.12 = (bf16[4,5,128,128]{3,2,1,0:T(8,128)(2,1)}, bf16[4,5,128,128]{3,2,1,0:T(8,128)(2,1)S(1)}, u32[]{:S(2)}, u32[]{:S(2)}) collective-permute-start(bf16[4,5,128,128]{3,2,1,0:T(8,128)(2,1)} %bitcast.23), channel_id=1, source_target_pairs={{0,2},{1,3},{2,0},{3,1},{4,6},{5,7},{6,4},{7,5},{8,10},{9,11},{10,... | collective-permute-start | bytes 1966088 | tf_op jit(solution)/shard_map/ppermute | solution.py:207
  3.7 1.5 %collective-permute-start.14 = (bf16[4,5,128,128]{3,2,1,0:T(8,128)(2,1)}, bf16[4,5,128,128]{3,2,1,0:T(8,128)(2,1)S(1)}, u32[]{:S(2)}, u32[]{:S(2)}) collective-permute-start(bf16[4,5,128,128]{3,2,1,0:T(8,128)(2,1)} %bitcast.24), channel_id=1, source_target_pairs={{0,4},{1,5},{2,6},{3,7},{4,0},{5,1},{6,2},{7,3},{8,12},{9,13},{10,... | collective-permute-start | bytes 1966088 | tf_op jit(solution)/shard_map/ppermute | solution.py:207
  5.7 2.0 %collective-permute-start = (s32[4,5]{0,1:T(8,128)S(1)}, s32[4,5]{0,1:T(8,128)S(1)}, u32[]{:S(2)}, u32[]{:S(2)}) collective-permute-start(s32[4,5]{0,1:T(8,128)S(1)} %fusion.3), channel_id=1, source_target_pairs={{0,2},{1,3},{2,0},{3,1},{4,6},{5,7},{6,4},{7,5},{8,10},{9,11},{10,... | collective-permute-start | bytes 248 | tf_op jit(solution)/shard_map/ppermute | solution.py:207
  7.8 1.5 %collective-permute-start.1 = (s32[4,5]{0,1:T(8,128)S(1)}, s32[4,5]{0,1:T(8,128)S(1)}, u32[]{:S(2)}, u32[]{:S(2)}) collective-permute-start(s32[4,5]{0,1:T(8,128)S(1)} %fusion.3), channel_id=1, source_target_pairs={{0,4},{1,5},{2,6},{3,7},{4,0},{5,1},{6,2},{7,3},{8,12},{9,13},{10,... | collective-permute-start | bytes 248 | tf_op jit(solution)/shard_map/ppermute | solution.py:207
  9.4 0.9 copy-done.10
  10.5 22.3 %collective-permute-done = s32[4,5]{0,1:T(8,128)S(1)} collective-permute-done((s32[4,5]{0,1:T(8,128)S(1)}, s32[4,5]{0,1:T(8,128)S(1)}, u32[]{:S(2)}, u32[]{:S(2)}) %collective-permute-start) | collective-permute-done | bytes 112 | tf_op jit(solution)/shard_map/ppermute | solution.py:207
  32.8 2.6 %collective-permute-start.2 = (s32[4,5]{0,1:T(8,128)S(1)}, s32[4,5]{0,1:T(8,128)S(1)}, u32[]{:S(2)}, u32[]{:S(2)}) collective-permute-start(s32[4,5]{0,1:T(8,128)S(1)} %fusion.3), channel_id=1, source_target_pairs={{0,6},{1,7},{2,4},{3,5},{4,2},{5,3},{6,0},{7,1},{8,14},{9,15},{10,... | collective-permute-start | bytes 248 | tf_op jit(solution)/shard_map/ppermute | solution.py:207
  35.9 1.4 %collective-permute-done.2 = s32[4,5]{0,1:T(8,128)S(1)} collective-permute-done((s32[4,5]{0,1:T(8,128)S(1)}, s32[4,5]{0,1:T(8,128)S(1)}, u32[]{:S(2)}, u32[]{:S(2)}) %collective-permute-start.2) | collective-permute-done | bytes 112 | tf_op jit(solution)/shard_map/ppermute | solution.py:207
  37.5 1.2 collective-permute-done.3
  38.6 1.7 %collective-permute-start.4 = (bf16[2,4,16,128]{3,2,1,0:T(8,128)(2,1)S(1)}, bf16[2,4,16,128]{3,2,1,0:T(8,128)(2,1)S(1)}, u32[]{:S(2)}, u32[]{:S(2)}) collective-permute-start(bf16[2,4,16,128]{3,2,1,0:T(8,128)(2,1)S(1)} %get-tuple-element.15), channel_id=1, source_target_pairs={{0,2},{1,3},{2,0},{3,1},{4,6},{5,7},{6,4},{7,5},{8,10},{9,11},{10,... | collective-permute-start | bytes 98312 | tf_op jit(solution)/shard_map/ppermute | solution.py:225
  40.4 1.5 %collective-permute-start.5 = (bf16[2,4,16,128]{3,2,1,0:T(8,128)(2,1)S(1)}, bf16[2,4,16,128]{3,2,1,0:T(8,128)(2,1)S(1)}, u32[]{:S(2)}, u32[]{:S(2)}) collective-permute-start(bf16[2,4,16,128]{3,2,1,0:T(8,128)(2,1)S(1)} %get-tuple-element.16), channel_id=1, source_target_pairs={{0,4},{1,5},{2,6},{3,7},{4,0},{5,1},{6,2},{7,3},{8,12},{9,13},{10,... | collective-permute-start | bytes 98312 | tf_op jit(solution)/shard_map/ppermute | solution.py:225
  41.8 0.7 collective-permute-done.4.refs_1_
  42.5 1.7 %collective-permute-done.5.refs_2_ = bf16[2,4,16,128]{3,2,1,0:T(8,128)(2,1)S(1)} collective-permute-done((bf16[2,4,16,128]{3,2,1,0:T(8,128)(2,1)S(1)}, bf16[2,4,16,128]{3,2,1,0:T(8,128)(2,1)S(1)}, u32[]{:S(2)}, u32[]{:S(2)}) %collective-permute-start.5) | collective-permute-done | bytes 32800 | tf_op jit(solution)/shard_map/ppermute | solution.py:225
  44.3 0.6 copy-done.13
  44.9 0.6 copy-done.19
  45.5 0.6 collective-permute-start.19
  46.1 0.6 copy-done.21
  46.9 0.6 copy-done.15
  47.5 0.4 collective-permute-done.8.refs_5_
  47.9 0.6 copy-done.23
  48.7 0.6 copy-done.17
  49.4 0.4 collective-permute-done.9.refs_6_
  49.7 0.6 copy-done.25
  50.3 1.5 %collective-permute-start.21 = (bf16[512,128]{1,0:T(8,128)(2,1)S(1)}, bf16[512,128]{1,0:T(8,128)(2,1)}, u32[]{:S(2)}, u32[]{:S(2)}) collective-permute-start(bf16[512,128]{1,0:T(8,128)(2,1)S(1)} %bitcast.30), channel_id=1, source_target_pairs={{0,4},{1,5},{2,6},{3,7},{4,0},{5,1},{6,2},{7,3},{8,12},{9,13},{10,... | collective-permute-start | bytes 393224 | tf_op jit(solution)/shard_map/ppermute | solution.py:207
  51.8 1.4 %collective-permute-start.23 = (bf16[512,128]{1,0:T(8,128)(2,1)S(1)}, bf16[512,128]{1,0:T(8,128)(2,1)S(1)}, u32[]{:S(2)}, u32[]{:S(2)}) collective-permute-start(bf16[512,128]{1,0:T(8,128)(2,1)S(1)} %bitcast.31), channel_id=1, source_target_pairs={{0,6},{1,7},{2,4},{3,5},{4,2},{5,3},{6,0},{7,1},{8,14},{9,15},{10,... | collective-permute-start | bytes 393224 | tf_op jit(solution)/shard_map/ppermute | solution.py:207
  53.3 5.6 %collective-permute-done.21.refs_20_ = bf16[512,128]{1,0:T(8,128)(2,1)} collective-permute-done((bf16[512,128]{1,0:T(8,128)(2,1)S(1)}, bf16[512,128]{1,0:T(8,128)(2,1)}, u32[]{:S(2)}, u32[]{:S(2)}) %collective-permute-start.21) | collective-permute-done | bytes 131104 | tf_op jit(solution)/shard_map/ppermute | solution.py:207
  58.9 0.5 collective-permute-start.13
  59.5 0.4 collective-permute-start.17
  60.0 2.9 %collective-permute-done.18.refs_17_ = bf16[512,128]{1,0:T(8,128)(2,1)S(1)} collective-permute-done((bf16[512,128]{1,0:T(8,128)(2,1)S(1)}, bf16[512,128]{1,0:T(8,128)(2,1)S(1)}, u32[]{:S(2)}, u32[]{:S(2)}) %collective-permute-start.18) | collective-permute-done | bytes 131104 | tf_op jit(solution)/shard_map/ppermute | solution.py:210
  62.8 0.7 copy-done.6
  63.5 0.4 collective-permute-start.20
  63.9 1.0 collective-permute-done.20.refs_19_
  64.9 0.7 copy-done.8
  65.5 0.4 collective-permute-start.22
  65.9 0.7 pad_add_fusion
  66.6 0.6 copy.23
  67.2 0.8 reshape.17
  68.2 1.4 %collective-permute-done.24.refs_23_ = bf16[512,128]{1,0:T(8,128)(2,1)S(1)} collective-permute-done((bf16[512,128]{1,0:T(8,128)(2,1)}, bf16[512,128]{1,0:T(8,128)(2,1)S(1)}, u32[]{:S(2)}, u32[]{:S(2)}) %collective-permute-start.24) | collective-permute-done | bytes 131104 | tf_op jit(solution)/shard_map/ppermute | solution.py:210
  69.7 1.1 copy-done.1
  70.8 0.9 copy-done.5
  71.7 0.9 copy-done.7
  72.6 0.9 copy-done.9
  73.5 0.8 copy-done.12
  74.2 0.8 copy-done.14
  75.0 0.8 copy-done.16
  75.7 0.8 copy-done.18
  76.5 0.8 copy-done.20
  77.3 0.8 copy-done.22
  78.0 0.8 copy-done.24
  78.8 0.8 copy-done.26
  79.5 19.6 %first_steps.1 = (f32[4,24,128]{2,1,0:T(8,128)S(1)}, bf16[32,16,128]{2,1,0:T(8,128)(2,1)S(1)}) custom-call(s32[160]{0:T(256)S(1)} %fusion.10.columns_ref, bf16[2,4,16,128]{3,2,1,0:T(8,128)(2,1)S(1)} %copy-done.12, bf16[2,4,16,128]{3,2,1,0:T(8,128)(2,1)S(1)} %copy-done.16, bf16[2,4,16,128]{3,2,1,0:T(8,128)(2,1)S(1)} %copy-done.18, ...), custom_call_target="tpu_custom_call" | custom-call | flops 419430400 | bytes 6553600 | tf_op jit(solution)/shard_map/first_steps/pallas_call | solution.py:169
  99.2 1.6 %collective-permute-start.25 = (f32[24,128]{1,0:T(8,128)S(1)}, f32[24,128]{1,0:T(8,128)S(1)}, u32[]{:S(2)}, u32[]{:S(2)}) collective-permute-start(f32[24,128]{1,0:T(8,128)S(1)} %get-tuple-element.28), channel_id=1, source_target_pairs={{0,8},{8,0},{16,24},{24,16},{1,9},{9,1},{17,25},{25,17},{2,10},{10... | collective-permute-start | bytes 36872 | tf_op jit(solution)/shard_map/ppermute | solution.py:252
  100.9 2.6 %collective-permute-start.26 = (f32[24,128]{1,0:T(8,128)S(1)}, f32[24,128]{1,0:T(8,128)S(1)}, u32[]{:S(2)}, u32[]{:S(2)}) collective-permute-start(f32[24,128]{1,0:T(8,128)S(1)} %get-tuple-element.27), channel_id=1, source_target_pairs={{0,16},{8,24},{16,0},{24,8},{1,17},{9,25},{17,1},{25,9},{2,18},{10... | collective-permute-start | bytes 36872 | tf_op jit(solution)/shard_map/ppermute | solution.py:252
  103.8 2.9 %last_step.1.panel_ref = bf16[32,16,128]{2,1,0:T(8,128)(2,1)S(1)} custom-call(s32[160]{0:T(256)S(1)} %fusion.10.columns_ref, bf16[32,16,128]{2,1,0:T(8,128)(2,1)S(1)} %get-tuple-element.18.panel_ref, bf16[4,5,128,128]{3,2,1,0:T(8,128)(2,1)S(1)} %bitcast.28, bf16[4,5,128,128]{3,2,1,0:T(8,128)(2,1)S(1)} %collective-permute-done.11.refs_9_.refs_1_, ...), custom_call_target="tpu_custom_call" | custom-call | flops 83886080 | bytes 5373952 | tf_op jit(solution)/shard_map/last_step/pallas_call | solution.py:169
  106.7 2.2 %collective-permute-done.27.refs_2_ = f32[24,128]{1,0:T(8,128)S(1)} collective-permute-done((f32[24,128]{1,0:T(8,128)S(1)}, f32[24,128]{1,0:T(8,128)S(1)}, u32[]{:S(2)}, u32[]{:S(2)}) %collective-permute-start.27) | collective-permute-done | bytes 12320 | tf_op jit(solution)/shard_map/ppermute | solution.py:252
  109.0 0.7 mix_terms.1
  109.6 1.5 %collective-permute-start.28 = (bf16[2,80,128]{2,1,0:T(8,128)(2,1)S(1)}, bf16[2,80,128]{2,1,0:T(8,128)(2,1)S(1)}, u32[]{:S(2)}, u32[]{:S(2)}) collective-permute-start(bf16[2,80,128]{2,1,0:T(8,128)(2,1)S(1)} %get-tuple-element.21), channel_id=1, source_target_pairs={{0,2},{1,3},{2,0},{3,1},{4,6},{5,7},{6,4},{7,5},{8,10},{9,11},{10,... | collective-permute-start | bytes 122888 | tf_op jit(solution)/shard_map/ppermute | solution.py:273
  111.2 1.5 %collective-permute-start.29 = (bf16[2,80,128]{2,1,0:T(8,128)(2,1)S(1)}, bf16[2,80,128]{2,1,0:T(8,128)(2,1)S(1)}, u32[]{:S(2)}, u32[]{:S(2)}) collective-permute-start(bf16[2,80,128]{2,1,0:T(8,128)(2,1)S(1)} %get-tuple-element.22), channel_id=1, source_target_pairs={{0,4},{1,5},{2,6},{3,7},{4,0},{5,1},{6,2},{7,3},{8,12},{9,13},{10,... | collective-permute-start | bytes 122888 | tf_op jit(solution)/shard_map/ppermute | solution.py:273
  112.6 0.6 collective-permute-start.30
  113.2 0.8 collective-permute-done.28.refs_1_
  114.0 1.2 collective-permute-done.29.refs_2_
  115.2 2.4 %collective-permute-done.30.refs_3_ = bf16[2,80,128]{2,1,0:T(8,128)(2,1)S(1)} collective-permute-done((bf16[2,80,128]{2,1,0:T(8,128)(2,1)S(1)}, bf16[2,80,128]{2,1,0:T(8,128)(2,1)S(1)}, u32[]{:S(2)}, u32[]{:S(2)}) %collective-permute-start.30) | collective-permute-done | bytes 40992 | tf_op jit(solution)/shard_map/ppermute | solution.py:273
  117.6 1.2 collective-permute-done.34.refs_7_
  118.8 1.2 %join_columns.1 = (f32[4,6,16,32]{3,2,1,0:T(8,128)}, bf16[512,128]{1,0:T(8,128)(2,1)}) custom-call(s32[1]{0:T(128)} %bitcast.row_ref, bf16[2,80,128]{2,1,0:T(8,128)(2,1)S(1)} %get-tuple-element.20.refs_0_, bf16[2,80,128]{2,1,0:T(8,128)(2,1)S(1)} %collective-permute-done.28.refs_1_, bf16[2,80,128]{2,1,0:T(8,128)(2,1)S(1)} %collective-permute-done.29.refs_2_, ...), custom_call_target="tpu_custom_call" | custom-call | bytes 327680 | tf_op jit(solution)/shard_map/join_columns/pallas_call | solution.py:169
  (89 shorter events, 2.7 us)
Async XLA Ops:
  0.6 4.6 %copy-start = (s32[1,8,8,2]{2,3,1,0:T(2,128)S(1)}, s32[1,8,8,2]{2,3,1,0:T(2,128)}, u32[]{:S(2)}) copy-start(s32[1,8,8,2]{2,3,1,0:T(2,128)} %param.8) | copy-start | bytes 1540
  0.6 4.7 %copy-start.28 = (s32[1,4,5]{2,1,0:T(4,128)S(1)}, s32[1,4,5]{2,1,0:T(4,128)}, u32[]{:S(2)}) copy-start(s32[1,4,5]{2,1,0:T(4,128)} %param.7) | copy-start | bytes 244
  0.7 58.2 %collective-permute-start.12 = (bf16[4,5,128,128]{3,2,1,0:T(8,128)(2,1)}, bf16[4,5,128,128]{3,2,1,0:T(8,128)(2,1)S(1)}, u32[]{:S(2)}, u32[]{:S(2)}) collective-permute-start(bf16[4,5,128,128]{3,2,1,0:T(8,128)(2,1)} %bitcast.23), channel_id=1, source_target_pairs={{0,2},{1,3},{2,0},{3,1},{4,6},{5,7},{6,4},{7,5},{8,10},{9,11},{10,... | collective-permute-start | bytes 1966088 | tf_op jit(solution)/shard_map/ppermute | solution.py:207
  3.7 55.7 %collective-permute-start.14 = (bf16[4,5,128,128]{3,2,1,0:T(8,128)(2,1)}, bf16[4,5,128,128]{3,2,1,0:T(8,128)(2,1)S(1)}, u32[]{:S(2)}, u32[]{:S(2)}) collective-permute-start(bf16[4,5,128,128]{3,2,1,0:T(8,128)(2,1)} %bitcast.24), channel_id=1, source_target_pairs={{0,4},{1,5},{2,6},{3,7},{4,0},{5,1},{6,2},{7,3},{8,12},{9,13},{10,... | collective-permute-start | bytes 1966088 | tf_op jit(solution)/shard_map/ppermute | solution.py:207
  5.2 54.3 %collective-permute-start.16 = (bf16[4,5,128,128]{3,2,1,0:T(8,128)(2,1)}, bf16[4,5,128,128]{3,2,1,0:T(8,128)(2,1)S(1)}, u32[]{:S(2)}, u32[]{:S(2)}) collective-permute-start(bf16[4,5,128,128]{3,2,1,0:T(8,128)(2,1)} %bitcast.25), channel_id=1, source_target_pairs={{0,6},{1,7},{2,4},{3,5},{4,2},{5,3},{6,0},{7,1},{8,14},{9,15},{10,... | collective-permute-start | bytes 1966088 | tf_op jit(solution)/shard_map/ppermute | solution.py:207
  5.2 40.3 %copy-start.3 = (bf16[1,512,128]{2,1,0:T(8,128)(2,1)S(1)}, bf16[1,512,128]{2,1,0:T(8,128)(2,1)}, u32[]{:S(2)}) copy-start(bf16[1,512,128]{2,1,0:T(8,128)(2,1)} %param.10) | copy-start | bytes 393220
  5.7 27.0 %collective-permute-start = (s32[4,5]{0,1:T(8,128)S(1)}, s32[4,5]{0,1:T(8,128)S(1)}, u32[]{:S(2)}, u32[]{:S(2)}) collective-permute-start(s32[4,5]{0,1:T(8,128)S(1)} %fusion.3), channel_id=1, source_target_pairs={{0,2},{1,3},{2,0},{3,1},{4,6},{5,7},{6,4},{7,5},{8,10},{9,11},{10,... | collective-permute-start | bytes 248 | tf_op jit(solution)/shard_map/ppermute | solution.py:207
  7.8 27.8 %collective-permute-start.1 = (s32[4,5]{0,1:T(8,128)S(1)}, s32[4,5]{0,1:T(8,128)S(1)}, u32[]{:S(2)}, u32[]{:S(2)}) collective-permute-start(s32[4,5]{0,1:T(8,128)S(1)} %fusion.3), channel_id=1, source_target_pairs={{0,4},{1,5},{2,6},{3,7},{4,0},{5,1},{6,2},{7,3},{8,12},{9,13},{10,... | collective-permute-start | bytes 248 | tf_op jit(solution)/shard_map/ppermute | solution.py:207
  9.4 0.9 copy-start.10
  10.5 42.8 %copy-start.11 = (bf16[2,4,16,128]{3,2,1,0:T(8,128)(2,1)}, bf16[2,4,16,128]{3,2,1,0:T(8,128)(2,1)S(1)}, u32[]{:S(2)}) copy-start(bf16[2,4,16,128]{3,2,1,0:T(8,128)(2,1)S(1)} %get-tuple-element.14.refs_0_) | copy-start | bytes 98308
  32.8 4.5 %collective-permute-start.2 = (s32[4,5]{0,1:T(8,128)S(1)}, s32[4,5]{0,1:T(8,128)S(1)}, u32[]{:S(2)}, u32[]{:S(2)}) collective-permute-start(s32[4,5]{0,1:T(8,128)S(1)} %fusion.3), channel_id=1, source_target_pairs={{0,6},{1,7},{2,4},{3,5},{4,2},{5,3},{6,0},{7,1},{8,14},{9,15},{10,... | collective-permute-start | bytes 248 | tf_op jit(solution)/shard_map/ppermute | solution.py:207
  35.5 4.8 %collective-permute-start.6 = (bf16[2,4,16,128]{3,2,1,0:T(8,128)(2,1)S(1)}, bf16[2,4,16,128]{3,2,1,0:T(8,128)(2,1)S(1)}, u32[]{:S(2)}, u32[]{:S(2)}) collective-permute-start(bf16[2,4,16,128]{3,2,1,0:T(8,128)(2,1)S(1)} %get-tuple-element.17), channel_id=1, source_target_pairs={{0,6},{1,7},{2,4},{3,5},{4,2},{5,3},{6,0},{7,1},{8,14},{9,15},{10,... | collective-permute-start | bytes 98312 | tf_op jit(solution)/shard_map/ppermute | solution.py:225
  37.4 1.2 %collective-permute-start.3 = (s32[4,4,5]{2,1,0:T(4,128)S(1)}, s32[4,4,5]{2,1,0:T(4,128)S(1)}, u32[]{:S(2)}, u32[]{:S(2)}) collective-permute-start(s32[4,4,5]{2,1,0:T(4,128)S(1)} %get-tuple-element.30), channel_id=1, source_target_pairs={{0,1},{1,0},{2,3},{3,2},{4,5},{5,4},{6,7},{7,6},{8,9},{9,8},{10,11... | collective-permute-start | bytes 968 | tf_op jit(solution)/shard_map/ppermute | solution.py:230
  38.6 13.2 %copy-start.29 = (s32[4,4,5]{2,1,0:T(4,128)}, s32[4,4,5]{2,1,0:T(4,128)S(1)}, u32[]{:S(2)}) copy-start(s32[4,4,5]{2,1,0:T(4,128)S(1)} %collective-permute-done.3) | copy-start | bytes 964
  38.6 3.9 %collective-permute-start.4 = (bf16[2,4,16,128]{3,2,1,0:T(8,128)(2,1)S(1)}, bf16[2,4,16,128]{3,2,1,0:T(8,128)(2,1)S(1)}, u32[]{:S(2)}, u32[]{:S(2)}) collective-permute-start(bf16[2,4,16,128]{3,2,1,0:T(8,128)(2,1)S(1)} %get-tuple-element.15), channel_id=1, source_target_pairs={{0,2},{1,3},{2,0},{3,1},{4,6},{5,7},{6,4},{7,5},{8,10},{9,11},{10,... | collective-permute-start | bytes 98312 | tf_op jit(solution)/shard_map/ppermute | solution.py:225
  40.4 3.9 %collective-permute-start.5 = (bf16[2,4,16,128]{3,2,1,0:T(8,128)(2,1)S(1)}, bf16[2,4,16,128]{3,2,1,0:T(8,128)(2,1)S(1)}, u32[]{:S(2)}, u32[]{:S(2)}) collective-permute-start(bf16[2,4,16,128]{3,2,1,0:T(8,128)(2,1)S(1)} %get-tuple-element.16), channel_id=1, source_target_pairs={{0,4},{1,5},{2,6},{3,7},{4,0},{5,1},{6,2},{7,3},{8,12},{9,13},{10,... | collective-permute-start | bytes 98312 | tf_op jit(solution)/shard_map/ppermute | solution.py:225
  42.5 2.4 %collective-permute-start.7 = (bf16[2,4,16,128]{3,2,1,0:T(8,128)(2,1)S(1)}, bf16[2,4,16,128]{3,2,1,0:T(8,128)(2,1)S(1)}, u32[]{:S(2)}, u32[]{:S(2)}) collective-permute-start(bf16[2,4,16,128]{3,2,1,0:T(8,128)(2,1)S(1)} %get-tuple-element.14.refs_0_), channel_id=1, source_target_pairs={{0,1},{1,0},{2,3},{3,2},{4,5},{5,4},{6,7},{7,6},{8,9},{9,8},{10,11... | collective-permute-start | bytes 98312 | tf_op jit(solution)/shard_map/ppermute | solution.py:210
  44.3 1.8 %collective-permute-start.10 = (bf16[2,4,16,128]{3,2,1,0:T(8,128)(2,1)S(1)}, bf16[2,4,16,128]{3,2,1,0:T(8,128)(2,1)S(1)}, u32[]{:S(2)}, u32[]{:S(2)}) collective-permute-start(bf16[2,4,16,128]{3,2,1,0:T(8,128)(2,1)S(1)} %collective-permute-done.6.refs_3_), channel_id=1, source_target_pairs={{0,1},{1,0},{2,3},{3,2},{4,5},{5,4},{6,7},{7,6},{8,9},{9,8},{10,11... | collective-permute-start | bytes 98312 | tf_op jit(solution)/shard_map/ppermute | solution.py:210
  44.3 0.6 copy-start.13
  44.9 0.6 copy-start.19
  45.5 6.3 %collective-permute-start.19 = (bf16[512,128]{1,0:T(8,128)(2,1)S(1)}, bf16[512,128]{1,0:T(8,128)(2,1)S(1)}, u32[]{:S(2)}, u32[]{:S(2)}) collective-permute-start(bf16[512,128]{1,0:T(8,128)(2,1)S(1)} %bitcast.29), channel_id=1, source_target_pairs={{0,2},{1,3},{2,0},{3,1},{4,6},{5,7},{6,4},{7,5},{8,10},{9,11},{10,... | collective-permute-start | bytes 393224 | tf_op jit(solution)/shard_map/ppermute | solution.py:207
  46.1 0.6 copy-start.21
  46.7 1.2 %collective-permute-start.8 = (bf16[2,4,16,128]{3,2,1,0:T(8,128)(2,1)S(1)}, bf16[2,4,16,128]{3,2,1,0:T(8,128)(2,1)S(1)}, u32[]{:S(2)}, u32[]{:S(2)}) collective-permute-start(bf16[2,4,16,128]{3,2,1,0:T(8,128)(2,1)S(1)} %collective-permute-done.4.refs_1_), channel_id=1, source_target_pairs={{0,1},{1,0},{2,3},{3,2},{4,5},{5,4},{6,7},{7,6},{8,9},{9,8},{10,11... | collective-permute-start | bytes 98312 | tf_op jit(solution)/shard_map/ppermute | solution.py:210
  46.9 0.6 copy-start.15
  47.9 0.6 copy-start.23
  48.5 1.2 %collective-permute-start.9 = (bf16[2,4,16,128]{3,2,1,0:T(8,128)(2,1)S(1)}, bf16[2,4,16,128]{3,2,1,0:T(8,128)(2,1)S(1)}, u32[]{:S(2)}, u32[]{:S(2)}) collective-permute-start(bf16[2,4,16,128]{3,2,1,0:T(8,128)(2,1)S(1)} %collective-permute-done.5.refs_2_), channel_id=1, source_target_pairs={{0,1},{1,0},{2,3},{3,2},{4,5},{5,4},{6,7},{7,6},{8,9},{9,8},{10,11... | collective-permute-start | bytes 98312 | tf_op jit(solution)/shard_map/ppermute | solution.py:210
  48.7 0.6 copy-start.17
  50.3 8.5 %collective-permute-start.21 = (bf16[512,128]{1,0:T(8,128)(2,1)S(1)}, bf16[512,128]{1,0:T(8,128)(2,1)}, u32[]{:S(2)}, u32[]{:S(2)}) collective-permute-start(bf16[512,128]{1,0:T(8,128)(2,1)S(1)} %bitcast.30), channel_id=1, source_target_pairs={{0,4},{1,5},{2,6},{3,7},{4,0},{5,1},{6,2},{7,3},{8,12},{9,13},{10,... | collective-permute-start | bytes 393224 | tf_op jit(solution)/shard_map/ppermute | solution.py:207
  51.8 8.1 %collective-permute-start.23 = (bf16[512,128]{1,0:T(8,128)(2,1)S(1)}, bf16[512,128]{1,0:T(8,128)(2,1)S(1)}, u32[]{:S(2)}, u32[]{:S(2)}) collective-permute-start(bf16[512,128]{1,0:T(8,128)(2,1)S(1)} %bitcast.31), channel_id=1, source_target_pairs={{0,6},{1,7},{2,4},{3,5},{4,2},{5,3},{6,0},{7,1},{8,14},{9,15},{10,... | collective-permute-start | bytes 393224 | tf_op jit(solution)/shard_map/ppermute | solution.py:207
  58.9 10.8 %collective-permute-start.11 = (bf16[4,5,128,128]{3,2,1,0:T(8,128)(2,1)}, bf16[4,5,128,128]{3,2,1,0:T(8,128)(2,1)S(1)}, u32[]{:S(2)}, u32[]{:S(2)}) collective-permute-start(bf16[4,5,128,128]{3,2,1,0:T(8,128)(2,1)} %bitcast.26), channel_id=1, source_target_pairs={{0,1},{1,0},{2,3},{3,2},{4,5},{5,4},{6,7},{7,6},{8,9},{9,8},{10,11... | collective-permute-start | bytes 1966088 | tf_op jit(solution)/shard_map/ppermute | solution.py:210
  58.9 10.8 %collective-permute-start.13 = (bf16[4,5,128,128]{3,2,1,0:T(8,128)(2,1)S(1)}, bf16[4,5,128,128]{3,2,1,0:T(8,128)(2,1)S(1)}, u32[]{:S(2)}, u32[]{:S(2)}) collective-permute-start(bf16[4,5,128,128]{3,2,1,0:T(8,128)(2,1)S(1)} %collective-permute-done.12.refs_10_.refs_2_), channel_id=1, source_target_pairs={{0,1},{1,0},{2,3},{3,2},{4,5},{5,4},{6,7},{7,6},{8,9},{9,8},{10,11... | collective-permute-start | bytes 1966088 | tf_op jit(solution)/shard_map/ppermute | solution.py:210
  59.4 10.3 %collective-permute-start.15 = (bf16[4,5,128,128]{3,2,1,0:T(8,128)(2,1)S(1)}, bf16[4,5,128,128]{3,2,1,0:T(8,128)(2,1)}, u32[]{:S(2)}, u32[]{:S(2)}) collective-permute-start(bf16[4,5,128,128]{3,2,1,0:T(8,128)(2,1)S(1)} %collective-permute-done.14.refs_12_.refs_4_), channel_id=1, source_target_pairs={{0,1},{1,0},{2,3},{3,2},{4,5},{5,4},{6,7},{7,6},{8,9},{9,8},{10,11... | collective-permute-start | bytes 1966088 | tf_op jit(solution)/shard_map/ppermute | solution.py:210
  59.5 10.2 %collective-permute-start.17 = (bf16[4,5,128,128]{3,2,1,0:T(8,128)(2,1)S(1)}, bf16[4,5,128,128]{3,2,1,0:T(8,128)(2,1)}, u32[]{:S(2)}, u32[]{:S(2)}) collective-permute-start(bf16[4,5,128,128]{3,2,1,0:T(8,128)(2,1)S(1)} %collective-permute-done.16.refs_14_.refs_6_), channel_id=1, source_target_pairs={{0,1},{1,0},{2,3},{3,2},{4,5},{5,4},{6,7},{7,6},{8,9},{9,8},{10,11... | collective-permute-start | bytes 1966088 | tf_op jit(solution)/shard_map/ppermute | solution.py:210
  59.9 5.0 %copy-start.4 = (bf16[512,128]{1,0:T(8,128)(2,1)}, bf16[512,128]{1,0:T(8,128)(2,1)S(1)}, u32[]{:S(2)}) copy-start(bf16[512,128]{1,0:T(8,128)(2,1)S(1)} %collective-permute-done.23.refs_22_) | copy-start | bytes 393220
  59.9 2.9 %collective-permute-start.18 = (bf16[512,128]{1,0:T(8,128)(2,1)S(1)}, bf16[512,128]{1,0:T(8,128)(2,1)S(1)}, u32[]{:S(2)}, u32[]{:S(2)}) collective-permute-start(bf16[512,128]{1,0:T(8,128)(2,1)S(1)} %bitcast.32), channel_id=1, source_target_pairs={{0,1},{1,0},{2,3},{3,2},{4,5},{5,4},{6,7},{7,6},{8,9},{9,8},{10,11... | collective-permute-start | bytes 393224 | tf_op jit(solution)/shard_map/ppermute | solution.py:210
  62.8 0.7 copy-start.6
  63.5 1.4 %collective-permute-start.20 = (bf16[512,128]{1,0:T(8,128)(2,1)S(1)}, bf16[512,128]{1,0:T(8,128)(2,1)S(1)}, u32[]{:S(2)}, u32[]{:S(2)}) collective-permute-start(bf16[512,128]{1,0:T(8,128)(2,1)S(1)} %collective-permute-done.19.refs_18_), channel_id=1, source_target_pairs={{0,1},{1,0},{2,3},{3,2},{4,5},{5,4},{6,7},{7,6},{8,9},{9,8},{10,11... | collective-permute-start | bytes 393224 | tf_op jit(solution)/shard_map/ppermute | solution.py:210
  64.9 0.7 copy-start.8
  65.5 2.5 %collective-permute-start.22 = (bf16[512,128]{1,0:T(8,128)(2,1)}, bf16[512,128]{1,0:T(8,128)(2,1)}, u32[]{:S(2)}, u32[]{:S(2)}) collective-permute-start(bf16[512,128]{1,0:T(8,128)(2,1)} %collective-permute-done.21.refs_20_), channel_id=1, source_target_pairs={{0,1},{1,0},{2,3},{3,2},{4,5},{5,4},{6,7},{7,6},{8,9},{9,8},{10,11... | collective-permute-start | bytes 393224 | tf_op jit(solution)/shard_map/ppermute | solution.py:210
  68.0 1.6 %collective-permute-start.24 = (bf16[512,128]{1,0:T(8,128)(2,1)}, bf16[512,128]{1,0:T(8,128)(2,1)S(1)}, u32[]{:S(2)}, u32[]{:S(2)}) collective-permute-start(bf16[512,128]{1,0:T(8,128)(2,1)} %copy-done.4), channel_id=1, source_target_pairs={{0,1},{1,0},{2,3},{3,2},{4,5},{5,4},{6,7},{7,6},{8,9},{9,8},{10,11... | collective-permute-start | bytes 393224 | tf_op jit(solution)/shard_map/ppermute | solution.py:210
  69.7 1.1 copy-start.1
  70.8 0.9 copy-start.5
  71.7 0.9 copy-start.7
  72.6 0.9 copy-start.9
  73.5 0.8 copy-start.12
  74.2 0.8 copy-start.14
  75.0 0.8 copy-start.16
  75.7 0.8 copy-start.18
  76.5 0.8 copy-start.20
  77.3 0.8 copy-start.22
  78.0 0.8 copy-start.24
  78.8 0.8 copy-start.26
  79.5 24.2 %copy-start.2 = (bf16[1,4,5,128,128]{4,3,2,1,0:T(8,128)(2,1)S(1)}, bf16[1,4,5,128,128]{4,3,2,1,0:T(8,128)(2,1)}, u32[]{:S(2)}) copy-start(bf16[1,4,5,128,128]{4,3,2,1,0:T(8,128)(2,1)} %param.6) | copy-start | bytes 1966084
  99.2 7.5 %collective-permute-start.25 = (f32[24,128]{1,0:T(8,128)S(1)}, f32[24,128]{1,0:T(8,128)S(1)}, u32[]{:S(2)}, u32[]{:S(2)}) collective-permute-start(f32[24,128]{1,0:T(8,128)S(1)} %get-tuple-element.28), channel_id=1, source_target_pairs={{0,8},{8,0},{16,24},{24,16},{1,9},{9,1},{17,25},{25,17},{2,10},{10... | collective-permute-start | bytes 36872 | tf_op jit(solution)/shard_map/ppermute | solution.py:252
  100.9 5.9 %collective-permute-start.26 = (f32[24,128]{1,0:T(8,128)S(1)}, f32[24,128]{1,0:T(8,128)S(1)}, u32[]{:S(2)}, u32[]{:S(2)}) collective-permute-start(f32[24,128]{1,0:T(8,128)S(1)} %get-tuple-element.27), channel_id=1, source_target_pairs={{0,16},{8,24},{16,0},{24,8},{1,17},{9,25},{17,1},{25,9},{2,18},{10... | collective-permute-start | bytes 36872 | tf_op jit(solution)/shard_map/ppermute | solution.py:252
  103.5 5.5 %collective-permute-start.27 = (f32[24,128]{1,0:T(8,128)S(1)}, f32[24,128]{1,0:T(8,128)S(1)}, u32[]{:S(2)}, u32[]{:S(2)}) collective-permute-start(f32[24,128]{1,0:T(8,128)S(1)} %get-tuple-element.26), channel_id=1, source_target_pairs={{0,24},{8,16},{16,8},{24,0},{1,25},{9,17},{17,9},{25,1},{2,26},{10... | collective-permute-start | bytes 36872 | tf_op jit(solution)/shard_map/ppermute | solution.py:252
  103.7 5.2 %copy-start.27 = (f32[4,4]{1,0:T(4,128)S(1)}, f32[4,4]{1,0:T(4,128)}, u32[]{:S(2)}) copy-start(f32[4,4]{1,0:T(4,128)} %weights_ref.1) | copy-start | bytes 196
  109.6 4.3 %collective-permute-start.28 = (bf16[2,80,128]{2,1,0:T(8,128)(2,1)S(1)}, bf16[2,80,128]{2,1,0:T(8,128)(2,1)S(1)}, u32[]{:S(2)}, u32[]{:S(2)}) collective-permute-start(bf16[2,80,128]{2,1,0:T(8,128)(2,1)S(1)} %get-tuple-element.21), channel_id=1, source_target_pairs={{0,2},{1,3},{2,0},{3,1},{4,6},{5,7},{6,4},{7,5},{8,10},{9,11},{10,... | collective-permute-start | bytes 122888 | tf_op jit(solution)/shard_map/ppermute | solution.py:273
  111.2 4.0 %collective-permute-start.29 = (bf16[2,80,128]{2,1,0:T(8,128)(2,1)S(1)}, bf16[2,80,128]{2,1,0:T(8,128)(2,1)S(1)}, u32[]{:S(2)}, u32[]{:S(2)}) collective-permute-start(bf16[2,80,128]{2,1,0:T(8,128)(2,1)S(1)} %get-tuple-element.22), channel_id=1, source_target_pairs={{0,4},{1,5},{2,6},{3,7},{4,0},{5,1},{6,2},{7,3},{8,12},{9,13},{10,... | collective-permute-start | bytes 122888 | tf_op jit(solution)/shard_map/ppermute | solution.py:273
  112.6 4.9 %collective-permute-start.30 = (bf16[2,80,128]{2,1,0:T(8,128)(2,1)S(1)}, bf16[2,80,128]{2,1,0:T(8,128)(2,1)S(1)}, u32[]{:S(2)}, u32[]{:S(2)}) collective-permute-start(bf16[2,80,128]{2,1,0:T(8,128)(2,1)S(1)} %get-tuple-element.23), channel_id=1, source_target_pairs={{0,6},{1,7},{2,4},{3,5},{4,2},{5,3},{6,0},{7,1},{8,14},{9,15},{10,... | collective-permute-start | bytes 122888 | tf_op jit(solution)/shard_map/ppermute | solution.py:273
  113.2 4.3 %collective-permute-start.31 = (bf16[2,80,128]{2,1,0:T(8,128)(2,1)S(1)}, bf16[2,80,128]{2,1,0:T(8,128)(2,1)S(1)}, u32[]{:S(2)}, u32[]{:S(2)}) collective-permute-start(bf16[2,80,128]{2,1,0:T(8,128)(2,1)S(1)} %get-tuple-element.20.refs_0_), channel_id=1, source_target_pairs={{0,1},{1,0},{2,3},{3,2},{4,5},{5,4},{6,7},{7,6},{8,9},{9,8},{10,11... | collective-permute-start | bytes 122888 | tf_op jit(solution)/shard_map/ppermute | solution.py:210
  114.0 3.6 %collective-permute-start.32 = (bf16[2,80,128]{2,1,0:T(8,128)(2,1)S(1)}, bf16[2,80,128]{2,1,0:T(8,128)(2,1)S(1)}, u32[]{:S(2)}, u32[]{:S(2)}) collective-permute-start(bf16[2,80,128]{2,1,0:T(8,128)(2,1)S(1)} %collective-permute-done.28.refs_1_), channel_id=1, source_target_pairs={{0,1},{1,0},{2,3},{3,2},{4,5},{5,4},{6,7},{7,6},{8,9},{9,8},{10,11... | collective-permute-start | bytes 122888 | tf_op jit(solution)/shard_map/ppermute | solution.py:210
  115.2 2.4 %collective-permute-start.33 = (bf16[2,80,128]{2,1,0:T(8,128)(2,1)S(1)}, bf16[2,80,128]{2,1,0:T(8,128)(2,1)S(1)}, u32[]{:S(2)}, u32[]{:S(2)}) collective-permute-start(bf16[2,80,128]{2,1,0:T(8,128)(2,1)S(1)} %collective-permute-done.29.refs_2_), channel_id=1, source_target_pairs={{0,1},{1,0},{2,3},{3,2},{4,5},{5,4},{6,7},{7,6},{8,9},{9,8},{10,11... | collective-permute-start | bytes 122888 | tf_op jit(solution)/shard_map/ppermute | solution.py:210
  117.5 1.2 %collective-permute-start.34 = (bf16[2,80,128]{2,1,0:T(8,128)(2,1)S(1)}, bf16[2,80,128]{2,1,0:T(8,128)(2,1)S(1)}, u32[]{:S(2)}, u32[]{:S(2)}) collective-permute-start(bf16[2,80,128]{2,1,0:T(8,128)(2,1)S(1)} %collective-permute-done.30.refs_3_), channel_id=1, source_target_pairs={{0,1},{1,0},{2,3},{3,2},{4,5},{5,4},{6,7},{7,6},{8,9},{9,8},{10,11... | collective-permute-start | bytes 122888 | tf_op jit(solution)/shard_map/ppermute | solution.py:210
  (1 other events, 0.6 us)

commit v2 on v0

v2 whole, which is shorter than its diff:
```python
import functools

import jax
import jax.numpy as jnp
from jax import lax
from jax.experimental import pallas as pl
from jax.experimental.pallas import tpu as pltpu
from jax.sharding import PartitionSpec as P

ITERS = 6
WHOLE_BYTES = 12 << 20
VMEM_BYTES = 24 << 20


def bits_apart(ranks, distance):
    return [(rank, rank ^ distance) for rank in range(ranks)]


def pack_pieces(projectors_ref, columns_ref, out_ref):
    ranks = out_ref.shape[0]
    rows, width = projectors_ref.shape
    blocks, held = rows // width, width // ranks
    for block in range(blocks):
        turned = projectors_ref[block * width : (block + 1) * width].T
        for device in range(ranks):
            out_ref[device, block * held : (block + 1) * held] = turned[device * held : (device + 1) * held]
    for device in range(ranks):
        out_ref[device, blocks * held :] = columns_ref[...]


def cut_halves(first_ref, second_ref, after_ref, low_ref, high_ref):
    low_ref[...] = first_ref[: low_ref.shape[0]]
    high_ref[...] = second_ref[low_ref.shape[0] :]


def all_steps(ranks, primes, stored, columns_ref, place_ref, pieces_ref, *refs):
    refs, panels = refs[:-ITERS], refs[-ITERS:]
    refs, terms_refs, last_ref, terms = refs[: -primes - 2], refs[-primes - 2 : -2], refs[-2], refs[-1]
    middle = refs[-1].shape[0]
    refs = [whole.at[part] for whole in refs[:-4] for part in (slice(middle), slice(middle, 2 * middle))] + [*refs[-4:]]
    count, size, width = panels[0].shape
    blocks = count // ranks
    half = blocks // 2
    depth = half * stored * size
    first_of = [(place_ref[1] ^ distance) * blocks for distance in range(ranks)]
    for distance, first in enumerate(first_of):
        for row in range(blocks):
            source = refs[2 * distance + row // half]
            at = depth + row % half * size
            panels[0][first + row] = source[at : at + size]

    def apply_row(old, distance, row):
        source = refs[2 * distance + row // half]
        at = row % half * stored * size
        tiles = [source[at + k * size : at + (k + 1) * size] for k in range(stored)]
        slot = (first_of[distance] + row) * stored
        needed = [old[columns_ref[slot + k]] for k in range(stored)]
        return jnp.dot(
            jnp.concatenate(tiles, axis=1), jnp.concatenate(needed, axis=0), preferred_element_type=jnp.float32
        ).astype(jnp.bfloat16)

    for old, new in zip(panels[:-1], panels[1:]):
        for distance, first in enumerate(first_of):
            for row in range(blocks):
                new[first + row] = apply_row(old, distance, row)
    for row in range(blocks):
        last_ref[row * size : (row + 1) * size] = apply_row(panels[-1], 0, row)

    held = width // ranks
    parts = []
    for step in range(0, ITERS, 2):
        total = None
        for device in range(ranks):
            turned = [pieces_ref[device, block * held : (block + 1) * held] for block in range(blocks)]
            seen = [
                jnp.concatenate([panels[step + j][device * blocks + block] for j in range(2)], axis=1)
                for block in range(blocks)
            ]
            part = jnp.dot(
                jnp.concatenate(turned, axis=1), jnp.concatenate(seen, axis=0), preferred_element_type=jnp.float32
            )
            total = part if total is None else total + part
        parts += [total[:, :width], total[:, width:]]
    every_term = jnp.concatenate(parts, axis=0)
    rows, part = ITERS * held // primes, width // primes
    for prime in range(primes):
        terms[prime] = jnp.concatenate(
            [
                every_term[group * rows : (group + 1) * rows, prime * part : (prime + 1) * part]
                for group in range(primes)
            ],
            axis=1,
        )
    for bits in range(primes):
        terms_refs[bits][...] = terms[place_ref[0] ^ bits]


def mix_terms(place_ref, weights_ref, *refs):
    terms_refs, out_ref = refs[:-1], refs[-1]
    primes, steps, held, part = out_ref.shape
    parts = [terms[...] for terms in terms_refs]
    for prime in range(primes):
        mixed = sum(weights_ref[prime, place_ref[0] ^ bits] * terms for bits, terms in enumerate(parts))
        groups = [mixed[:, group * part : (group + 1) * part] for group in range(primes)]
        out_ref[prime] = jnp.concatenate(groups, axis=0).reshape(steps, held, part)


def on_chip(kernel, out_shape, smem, vmem, after=(), scratch=(), flops=0, name=None):
    spaces = [pltpu.SMEM] * len(smem) + [pltpu.VMEM] * len(vmem) + [pl.ANY] * len(after)
    return pl.pallas_call(
        kernel,
        out_shape=out_shape,
        in_specs=[pl.BlockSpec(memory_space=space) for space in spaces],
        out_specs=jax.tree.map(lambda _: pl.BlockSpec(memory_space=pltpu.VMEM), out_shape),
        scratch_shapes=list(scratch),
        compiler_params=pltpu.CompilerParams(vmem_limit_bytes=VMEM_BYTES),
        cost_estimate=pl.CostEstimate(flops=flops, bytes_accessed=sum(v.size * v.dtype.itemsize for v in vmem), transcendentals=0),
        name=name,
    )(*smem, *vmem, *after)


def own_columns(tile_slots, requests, my_row, ranks):
    blocks, stored = tile_slots.shape
    fetched = requests.shape[2]
    exchanged = ranks * fetched
    wants = lax.dynamic_index_in_dim(requests, my_row, 0, keepdims=False).reshape(exchanged)
    named = tile_slots[..., None] == lax.broadcasted_iota(jnp.int32, (1, 1, exchanged), 2)
    picked = jnp.sum(jnp.where(named, wants[None, None], 0), axis=2)
    return jnp.where(
        tile_slots < exchanged,
        tile_slots // fetched * blocks + picked,
        my_row * blocks + tile_slots - exchanged,
    )


def whole_system(tile_data, tile_slots, requests, start_panel, projectors, combine_weights):
    ranks, primes = lax.axis_size("row"), lax.axis_size("prime")
    my_row, my_prime = lax.axis_index("row"), lax.axis_index("prime")
    place = jnp.stack([my_prime, my_row])
    tiles, panel = tile_data[0], start_panel[0]
    blocks, stored, size, _ = tiles.shape
    width = panel.shape[1]
    held = width // ranks

    def to_chip(array, chip):
        return lax.ppermute(array, "row", bits_apart(ranks, 2 * chip))

    def to_core(array):
        return lax.ppermute(array, "row", bits_apart(ranks, 1))

    half = blocks // 2
    by_row = [tiles.reshape(blocks, stored * size, size), panel.reshape(blocks, size, width)]
    own = jnp.concatenate(
        [array[rows].reshape(-1, width) for rows in (slice(half), slice(half, blocks)) for array in by_row]
    )
    middle = own.shape[0] // 2
    from_x, from_y = to_chip(own, 1), to_chip(own, 2)
    columns = own_columns(tile_slots[0], requests[0], my_row, ranks)
    columns = jnp.pad(columns.astype(jnp.bfloat16), ((0, held - blocks), (0, width - stored)))
    pieces = on_chip(
        pack_pieces,
        jax.ShapeDtypeStruct((ranks, (blocks + 1) * held, width), jnp.bfloat16),
        [],
        [projectors[0], columns],
        name="pack_pieces",
    )
    pieces = lax.all_to_all(pieces, "row", split_axis=0, concat_axis=0, tiled=True)
    columns = pieces[:, blocks * held :][:, :blocks, :stored].astype(jnp.int32).reshape(-1)
    low, high = on_chip(
        cut_halves,
        [jax.ShapeDtypeStruct((middle, width), jnp.bfloat16)] * 2,
        [],
        [from_x, from_y],
        after=[pieces],
        name="cut_halves",
    )
    diagonal = [to_chip(low, 2), to_chip(high, 1)]
    whole = [array for near in (own, from_x, from_y) for array in (near, to_core(near))]
    halves = diagonal + [to_core(array) for array in diagonal]
    piece = jax.ShapeDtypeStruct((ITERS * held // primes, width), jnp.float32)
    *terms, last = on_chip(
        functools.partial(all_steps, ranks, primes, stored),
        [piece] * primes + [jax.ShapeDtypeStruct((blocks * size, width), jnp.bfloat16)],
        [columns, place],
        [pieces, *whole, *halves],
        scratch=[pltpu.VMEM((primes, *piece.shape), jnp.float32)]
        + [pltpu.VMEM((ranks * blocks, size, width), jnp.bfloat16)] * ITERS,
        flops=2 * ITERS * ranks * tiles.size * width,
        name="all_steps",
    )
    terms = [terms[0]] + [
        lax.ppermute(terms[bits], "prime", bits_apart(primes, bits)) for bits in range(1, primes)
    ]
    mixed = on_chip(
        mix_terms,
        jax.ShapeDtypeStruct((primes, ITERS, held, width // primes), jnp.float32),
        [place, combine_weights],
        terms,
        name="mix_terms",
    )
    return mixed, last[None]


def split_system(tile_data, tile_slots, requests, start_panel, projectors, combine_weights):
    ranks = lax.axis_size("row")
    my_row = lax.axis_index("row")
    blocks, stored, size, _ = tile_data.shape[1:]
    width = start_panel.shape[2]
    columns = own_columns(tile_slots[0], requests[0], my_row, ranks)
    panel, projector = start_panel[0], projectors[0]
    partial_sums = []
    for step in range(ITERS):
        partial_sums.append(
            jnp.dot(projector.T, panel, preferred_element_type=jnp.float32).astype(jnp.bfloat16)
        )
        gathered = lax.all_gather(panel, "row", axis=0, tiled=True)
        needed = gathered.reshape(ranks * blocks, size, width)[columns]
        product = jnp.einsum("ikab,ikbw->iaw", tile_data[0], needed, preferred_element_type=jnp.float32)
        panel = product.astype(jnp.bfloat16).reshape(blocks * size, width)
    terms = lax.psum_scatter(jnp.stack(partial_sums), "row", scatter_dimension=1, tiled=True).astype(jnp.float32)
    regrouped = lax.all_to_all(terms[None], "prime", split_axis=3, concat_axis=0, tiled=True)
    mixed = jnp.einsum("qp,pkab->qkab", combine_weights, regrouped, precision=lax.Precision.HIGHEST)
    return mixed, panel[None]


def shards(tile_data, *others):
    ranks, primes = lax.axis_size("row"), lax.axis_size("prime")
    whole_bytes = ranks * tile_data.size * tile_data.dtype.itemsize
    fits = whole_bytes <= WHOLE_BYTES and ranks == 8 and primes == 4 and tile_data.shape[3:] == (128, 128)
    return (whole_system if fits else split_system)(tile_data, *others)


def solution(mesh):
    return jax.shard_map(
        shards,
        mesh=mesh,
        in_specs=(
            P("prime", "row", None, None, None),
            P("prime", "row", None),
            P("prime", None, None, None),
            P("prime", "row", None),
            P("prime", "row", None),
            P(),
        ),
        out_specs=(P(None, None, "row", "prime"), P("prime", "row", None)),
        check_vma=False,
    )
```

time: 386 us -> 65.2 us (0.17)
  waiting for transfers between devices: 324 us -> 31.1 us
  local copies, waits for them, and re-layouts: 22.3 us -> 2.5 us
  starting transfers between devices: 0.49 us -> 15.9 us
  Pallas kernels: 0 us -> 14.3 us
  between operations: 14.5 us -> 0.76 us
  matrix products: 10.8 us -> 0 us
  blocking collectives: 10.1 us -> 0 us
    reduce_scatter x6 -> x0, waiting for transfers between devices: 200 us -> none  [shards(): lax.psum_scatter(partial_sum.astype(jnp.bfloat16), 'row', scatter_dimensi...]
    all_gather x6 -> x0, waiting for transfers between devices: 123 us -> none  [shards(): gathered = lax.all_gather(current_panel, 'row', axis=1, tiled=True)]
    ppermute x0 -> x12, waiting for transfers between devices: none -> 17.2 us  [the longest x4 10.1 us: to_chip(): return lax.ppermute(array, 'row', bits_apart(ranks, 2 * chip))]
    pallas_call x0 -> x4, Pallas kernels: none -> 14.3 us  [on_chip(): pl.pallas_call(kernel, out_shape=out_shape, in_specs=[pl.BlockSpec(memory...]
    all_to_all x0 -> x1, waiting for transfers between devices: none -> 13.9 us  [whole_system(): lax.all_to_all(pieces, 'row', split_axis=0, concat_axis=0, tiled=True)]
    ppermute x0 -> x12, starting transfers between devices: none -> 12.6 us  [the longest x4 7.53 us: to_chip(): return lax.ppermute(array, 'row', bits_apart(ranks, 2 * chip))]
    gather x10 -> x0, local copies, waits for them, and re-layouts: 12.4 us -> none  [the longest x8 11.6 us: select_blocks(): return blocks[positions]]
    dot_general x13 -> x0, matrix products: 10.8 us -> none  [the longest x6 5.3 us: shards(): jnp.einsum('pikab,pikbw->piaw', tile_data, needed_blocks, preferred_eleme...]
  transfers between devices with their start and end apart: 12 -> 13, of which waited for: 12 -> 6; matrix products, arithmetic and copies ran while one was open for 5% -> 1% of each run, Pallas kernels for 0% -> 1%
where the time goes in v2:
time: 65.2 us; the launch traced here: 64.9 us
  waiting for transfers between devices  31.1 us (48%)
  starting transfers between devices  15.9 us (24%)
  Pallas kernels  14.3 us (22%)
  local copies, waits for them, and re-layouts  2.5 us (4%)
  between operations  0.76 us (1%)
    pallas_call x4, Pallas kernels, on_chip(): pl.pallas_call(kernel, out_shape=out_shape, in_specs=[pl.BlockSpec(memory...  14.3 us
    all_to_all x1, waiting for transfers between devices, whole_system(): lax.all_to_all(pieces, 'row', split_axis=0, concat_axis=0, tiled=True)  13.9 us
    ppermute x4, waiting for transfers between devices, to_chip(): return lax.ppermute(array, 'row', bits_apart(ranks, 2 * chip))  10.1 us
    ppermute x4, starting transfers between devices, to_chip(): return lax.ppermute(array, 'row', bits_apart(ranks, 2 * chip))  7.53 us
    ppermute x3, waiting for transfers between devices, whole_system(): lax.ppermute(terms[bits], 'prime', bits_apart(primes, bits))  5.27 us
    ppermute x3, starting transfers between devices, whole_system(): lax.ppermute(terms[bits], 'prime', bits_apart(primes, bits))  4.39 us
    all_to_all x1, starting transfers between devices, whole_system(): lax.all_to_all(pieces, 'row', split_axis=0, concat_axis=0, tiled=True)  3.38 us
    ppermute x5, waiting for transfers between devices, to_core(): return lax.ppermute(array, 'row', bits_apart(ranks, 1))  1.83 us
  transfers between devices with their start and end apart: 13, of which 6 were waited for; matrix products, arithmetic and copies ran while one was open for 1% of the time, Pallas kernels for 1%

profile of v2, /device:TPU:0, one launch (start us, length us, event | category | flops | bytes accessed | tf_op | source)
XLA Modules:
  0.0 64.9 jit_solution(3749098548730584274)
XLA Ops:
  0.6 0.0 copy-start
  0.6 0.9 %slice_bitcast_fusion.1 = (bf16[256,128]{1,0:T(8,128)(2,1)S(1)}, bf16[256,128]{1,0:T(8,128)(2,1)S(1)}) fusion(bf16[1,512,128]{2,1,0:T(8,128)(2,1)} %param.9), kind=kLoop, calls=%fused_computation.2 | loop fusion | bytes 262144 | tf_op jit(solution)/shard_map/reshape | solution.py:154
  1.5 1.1 %fusion.6 = (bf16[1,2,5,128,128]{4,3,2,1,0:T(8,128)(2,1)S(1)}, bf16[1,2,5,128,128]{4,3,2,1,0:T(8,128)(2,1)S(1)}) fusion(bf16[1,4,5,128,128]{4,3,2,1,0:T(8,128)(2,1)} %param.6), kind=kLoop, calls=%fused_computation.19 | loop fusion | bytes 1310720 | tf_op jit(solution)/shard_map/slice | solution.py:154
  2.7 0.0 copy-start.3
  2.7 0.0 copy-start.1
  2.7 0.1 pad_maximum_fusion.refs_0_
  2.7 3.0 %collective-permute-start.3 = (bf16[3072,128]{1,0:T(8,128)(2,1)S(1)}, bf16[3072,128]{1,0:T(8,128)(2,1)S(1)}, u32[]{:S(2)}, u32[]{:S(2)}) collective-permute-start(bf16[3072,128]{1,0:T(8,128)(2,1)S(1)} %pad_maximum_fusion.refs_0_), channel_id=1, source_target_pairs={{0,4},{1,5},{2,6},{3,7},{4,0},{5,1},{6,2},{7,3},{8,12},{9,13},{10,... | collective-permute-start | bytes 2359304 | tf_op jit(solution)/shard_map/ppermute | solution.py:146
  5.8 1.5 %collective-permute-start.1 = (bf16[3072,128]{1,0:T(8,128)(2,1)S(1)}, bf16[3072,128]{1,0:T(8,128)(2,1)S(1)}, u32[]{:S(2)}, u32[]{:S(2)}) collective-permute-start(bf16[3072,128]{1,0:T(8,128)(2,1)S(1)} %pad_maximum_fusion.refs_0_), channel_id=1, source_target_pairs={{0,2},{1,3},{2,0},{3,1},{4,6},{5,7},{6,4},{7,5},{8,10},{9,11},{10,... | collective-permute-start | bytes 2359304 | tf_op jit(solution)/shard_map/ppermute | solution.py:146
  7.3 0.0 copy-done
  7.3 0.1 copy.11
  7.4 0.1 broadcast_in_dim.17
  7.4 0.0 copy-done.3
  7.4 0.1 copy.10
  7.5 0.2 select_reduce_fusion
  7.8 0.1 copy.12
  7.9 0.0 copy-done.1
  7.9 0.8 %pack_pieces.1 = bf16[8,80,128]{2,1,0:T(8,128)(2,1)} custom-call(bf16[512,128]{1,0:T(8,128)(2,1)S(1)} %bitcast.14, bf16[16,128]{1,0:T(8,128)(2,1)S(1)} %pad.4.columns_ref), custom_call_target="tpu_custom_call" | custom-call | bytes 135168 | tf_op jit(solution)/shard_map/pack_pieces/pallas_call | solution.py:110
  8.7 3.4 %all-to-all-start = ((bf16[8,80,128]{2,1,0:T(8,128)(2,1)}), bf16[8,80,128]{2,1,0:T(8,128)(2,1)S(1)}, u32[]{:S(2)}, u32[]{:S(2)}) async-start(bf16[8,80,128]{2,1,0:T(8,128)(2,1)} %pack_pieces.1), calls=%async_computation | async-start | bytes 327680 | tf_op jit(solution)/shard_map/all_to_all | solution.py:167
  12.1 0.4 collective-permute-start
  12.5 13.9 %all-to-all-done.after_ref.pieces_ref = bf16[8,80,128]{2,1,0:T(8,128)(2,1)S(1)} async-done(((bf16[8,80,128]{2,1,0:T(8,128)(2,1)}), bf16[8,80,128]{2,1,0:T(8,128)(2,1)S(1)}, u32[]{:S(2)}, u32[]{:S(2)}) %all-to-all-start) | async-done | bytes 163872 | tf_op jit(solution)/shard_map/all_to_all | solution.py:167
  26.3 0.0 collective-permute-done.3.second_ref.refs_4_
  26.3 0.0 collective-permute-done.1.first_ref.refs_2_
  26.3 0.1 cut_halves.1
  26.4 1.7 %collective-permute-start.5 = (bf16[1536,128]{1,0:T(8,128)(2,1)S(1)}, bf16[1536,128]{1,0:T(8,128)(2,1)}, u32[]{:S(2)}, u32[]{:S(2)}) collective-permute-start(bf16[1536,128]{1,0:T(8,128)(2,1)S(1)} %get-tuple-element.9), channel_id=1, source_target_pairs={{0,4},{1,5},{2,6},{3,7},{4,0},{5,1},{6,2},{7,3},{8,12},{9,13},{10,... | collective-permute-start | bytes 1179656 | tf_op jit(solution)/shard_map/ppermute | solution.py:146
  28.1 0.0 collective-permute-start.4
  28.1 1.3 %collective-permute-start.6 = (bf16[1536,128]{1,0:T(8,128)(2,1)S(1)}, bf16[1536,128]{1,0:T(8,128)(2,1)}, u32[]{:S(2)}, u32[]{:S(2)}) collective-permute-start(bf16[1536,128]{1,0:T(8,128)(2,1)S(1)} %get-tuple-element.10), channel_id=1, source_target_pairs={{0,2},{1,3},{2,0},{3,1},{4,6},{5,7},{6,4},{7,5},{8,10},{9,11},{10,... | collective-permute-start | bytes 1179656 | tf_op jit(solution)/shard_map/ppermute | solution.py:146
  29.4 0.2 collective-permute-start.2
  29.6 7.4 %collective-permute-done.5.refs_6_ = bf16[1536,128]{1,0:T(8,128)(2,1)} collective-permute-done((bf16[1536,128]{1,0:T(8,128)(2,1)S(1)}, bf16[1536,128]{1,0:T(8,128)(2,1)}, u32[]{:S(2)}, u32[]{:S(2)}) %collective-permute-start.5) | collective-permute-done | bytes 393248 | tf_op jit(solution)/shard_map/ppermute | solution.py:146
  37.0 0.0 collective-permute-start.7
  37.0 2.7 %collective-permute-done.6.refs_7_ = bf16[1536,128]{1,0:T(8,128)(2,1)} collective-permute-done((bf16[1536,128]{1,0:T(8,128)(2,1)S(1)}, bf16[1536,128]{1,0:T(8,128)(2,1)}, u32[]{:S(2)}, u32[]{:S(2)}) %collective-permute-start.6) | collective-permute-done | bytes 393248 | tf_op jit(solution)/shard_map/ppermute | solution.py:146
  39.8 0.0 collective-permute-start.8
  39.8 0.1 pad_add_fusion.place_ref
  39.8 0.1 reshape.41.columns_ref
  40.0 0.0 copy-start.2
  40.0 0.0 collective-permute-done.refs_1_
  40.0 0.0 collective-permute-done.4.refs_5_
  40.0 0.0 collective-permute-done.7.refs_8_
  40.0 1.8 %collective-permute-done.8.refs_9_ = bf16[1536,128]{1,0:T(8,128)(2,1)} collective-permute-done((bf16[1536,128]{1,0:T(8,128)(2,1)}, bf16[1536,128]{1,0:T(8,128)(2,1)}, u32[]{:S(2)}, u32[]{:S(2)}) %collective-permute-start.8) | collective-permute-done | bytes 393248 | tf_op jit(solution)/shard_map/ppermute | solution.py:149
  41.8 0.0 collective-permute-done.2.refs_3_
  41.8 12.1 %all_steps.1 = (f32[24,128]{1,0:T(8,128)S(1)}, f32[24,128]{1,0:T(8,128)S(1)}, f32[24,128]{1,0:T(8,128)S(1)}, f32[24,128]{1,0:T(8,128)S(1)}, bf16[512,128]{1,0:T(8,128)(2,1)}) custom-call(s32[160]{0:T(256)S(1)} %reshape.41.columns_ref, s32[2]{0:T(128)S(1)} %pad_add_fusion.place_ref, bf16[8,80,128]{2,1,0:T(8,128)(2,1)S(1)} %all-to-all-done.after_ref.pieces_ref, ...), custom_call_target="tpu_custom_call" | custom-call | flops 4026531840 | bytes 6455296 | tf_op jit(solution)/shard_map/all_steps/pallas_call | solution.py:110
  53.9 1.6 %collective-permute-start.9 = (f32[24,128]{1,0:T(8,128)S(1)}, f32[24,128]{1,0:T(8,128)S(1)}, u32[]{:S(2)}, u32[]{:S(2)}) collective-permute-start(f32[24,128]{1,0:T(8,128)S(1)} %get-tuple-element.12), channel_id=1, source_target_pairs={{0,8},{8,0},{16,24},{24,16},{1,9},{9,1},{17,25},{25,17},{2,10},{10... | collective-permute-start | bytes 36872 | tf_op jit(solution)/shard_map/ppermute | solution.py:192
  55.5 2.6 %collective-permute-start.10 = (f32[24,128]{1,0:T(8,128)S(1)}, f32[24,128]{1,0:T(8,128)S(1)}, u32[]{:S(2)}, u32[]{:S(2)}) collective-permute-start(f32[24,128]{1,0:T(8,128)S(1)} %get-tuple-element.13), channel_id=1, source_target_pairs={{0,16},{8,24},{16,0},{24,8},{1,17},{9,25},{17,1},{25,9},{2,18},{10... | collective-permute-start | bytes 36872 | tf_op jit(solution)/shard_map/ppermute | solution.py:192
  58.1 0.2 collective-permute-start.11
  58.3 0.0 collective-permute-done.9.refs_1_
  58.3 1.8 %collective-permute-done.10.refs_2_ = f32[24,128]{1,0:T(8,128)S(1)} collective-permute-done((f32[24,128]{1,0:T(8,128)S(1)}, f32[24,128]{1,0:T(8,128)S(1)}, u32[]{:S(2)}, u32[]{:S(2)}) %collective-permute-start.10) | collective-permute-done | bytes 12320 | tf_op jit(solution)/shard_map/ppermute | solution.py:192
  60.1 3.5 %collective-permute-done.11.refs_3_ = f32[24,128]{1,0:T(8,128)S(1)} collective-permute-done((f32[24,128]{1,0:T(8,128)S(1)}, f32[24,128]{1,0:T(8,128)S(1)}, u32[]{:S(2)}, u32[]{:S(2)}) %collective-permute-start.11) | collective-permute-done | bytes 12320 | tf_op jit(solution)/shard_map/ppermute | solution.py:192
  63.6 0.0 copy-done.2
  63.6 1.4 %mix_terms.1 = f32[4,6,16,32]{3,2,1,0:T(8,128)} custom-call(s32[2]{0:T(128)S(1)} %pad_add_fusion.place_ref, f32[4,4]{1,0:T(4,128)S(1)} %copy-done.2, f32[24,128]{1,0:T(8,128)S(1)} %get-tuple-element.11.refs_0_, f32[24,128]{1,0:T(8,128)S(1)} %collective-permute-done.9.refs_1_, f32[24,128]{1,0:T(8,128)S(1)} %collective-permute-done.10.refs_2_, ...), custom_call_target="tpu_custom_call" | custom-call | bytes 49152 | tf_op jit(solution)/shard_map/mix_terms/pallas_call | solution.py:110
  (4 shorter events, 0.0 us)
Async XLA Ops:
  0.6 6.6 %copy-start = (s32[1,8,8,2]{2,3,1,0:T(2,128)S(1)}, s32[1,8,8,2]{2,3,1,0:T(2,128)}, u32[]{:S(2)}) copy-start(s32[1,8,8,2]{2,3,1,0:T(2,128)} %param.8) | copy-start | bytes 1540
  2.7 4.8 %copy-start.3 = (s32[1,4,5]{2,1,0:T(4,128)S(1)}, s32[1,4,5]{2,1,0:T(4,128)}, u32[]{:S(2)}) copy-start(s32[1,4,5]{2,1,0:T(4,128)} %param.7) | copy-start | bytes 244
  2.7 5.2 %copy-start.1 = (bf16[1,512,128]{2,1,0:T(8,128)(2,1)S(1)}, bf16[1,512,128]{2,1,0:T(8,128)(2,1)}, u32[]{:S(2)}) copy-start(bf16[1,512,128]{2,1,0:T(8,128)(2,1)} %param.10) | copy-start | bytes 393220
  2.7 23.6 %collective-permute-start.3 = (bf16[3072,128]{1,0:T(8,128)(2,1)S(1)}, bf16[3072,128]{1,0:T(8,128)(2,1)S(1)}, u32[]{:S(2)}, u32[]{:S(2)}) collective-permute-start(bf16[3072,128]{1,0:T(8,128)(2,1)S(1)} %pad_maximum_fusion.refs_0_), channel_id=1, source_target_pairs={{0,4},{1,5},{2,6},{3,7},{4,0},{5,1},{6,2},{7,3},{8,12},{9,13},{10,... | collective-permute-start | bytes 2359304 | tf_op jit(solution)/shard_map/ppermute | solution.py:146
  5.8 20.6 %collective-permute-start.1 = (bf16[3072,128]{1,0:T(8,128)(2,1)S(1)}, bf16[3072,128]{1,0:T(8,128)(2,1)S(1)}, u32[]{:S(2)}, u32[]{:S(2)}) collective-permute-start(bf16[3072,128]{1,0:T(8,128)(2,1)S(1)} %pad_maximum_fusion.refs_0_), channel_id=1, source_target_pairs={{0,2},{1,3},{2,0},{3,1},{4,6},{5,7},{6,4},{7,5},{8,10},{9,11},{10,... | collective-permute-start | bytes 2359304 | tf_op jit(solution)/shard_map/ppermute | solution.py:146
  8.7 17.6 %all-to-all-start = ((bf16[8,80,128]{2,1,0:T(8,128)(2,1)}), bf16[8,80,128]{2,1,0:T(8,128)(2,1)S(1)}, u32[]{:S(2)}, u32[]{:S(2)}) async-start(bf16[8,80,128]{2,1,0:T(8,128)(2,1)} %pack_pieces.1), calls=%async_computation | async-start | bytes 327680 | tf_op jit(solution)/shard_map/all_to_all | solution.py:167
  12.1 27.9 %collective-permute-start = (bf16[3072,128]{1,0:T(8,128)(2,1)S(1)}, bf16[3072,128]{1,0:T(8,128)(2,1)S(1)}, u32[]{:S(2)}, u32[]{:S(2)}) collective-permute-start(bf16[3072,128]{1,0:T(8,128)(2,1)S(1)} %pad_maximum_fusion.refs_0_), channel_id=1, source_target_pairs={{0,1},{1,0},{2,3},{3,2},{4,5},{5,4},{6,7},{7,6},{8,9},{9,8},{10,11... | collective-permute-start | bytes 2359304 | tf_op jit(solution)/shard_map/ppermute | solution.py:149
  26.4 10.6 %collective-permute-start.5 = (bf16[1536,128]{1,0:T(8,128)(2,1)S(1)}, bf16[1536,128]{1,0:T(8,128)(2,1)}, u32[]{:S(2)}, u32[]{:S(2)}) collective-permute-start(bf16[1536,128]{1,0:T(8,128)(2,1)S(1)} %get-tuple-element.9), channel_id=1, source_target_pairs={{0,4},{1,5},{2,6},{3,7},{4,0},{5,1},{6,2},{7,3},{8,12},{9,13},{10,... | collective-permute-start | bytes 1179656 | tf_op jit(solution)/shard_map/ppermute | solution.py:146
  28.1 11.9 %collective-permute-start.4 = (bf16[3072,128]{1,0:T(8,128)(2,1)S(1)}, bf16[3072,128]{1,0:T(8,128)(2,1)}, u32[]{:S(2)}, u32[]{:S(2)}) collective-permute-start(bf16[3072,128]{1,0:T(8,128)(2,1)S(1)} %collective-permute-done.3.second_ref.refs_4_), channel_id=1, source_target_pairs={{0,1},{1,0},{2,3},{3,2},{4,5},{5,4},{6,7},{7,6},{8,9},{9,8},{10,11... | collective-permute-start | bytes 2359304 | tf_op jit(solution)/shard_map/ppermute | solution.py:149
  28.1 11.6 %collective-permute-start.6 = (bf16[1536,128]{1,0:T(8,128)(2,1)S(1)}, bf16[1536,128]{1,0:T(8,128)(2,1)}, u32[]{:S(2)}, u32[]{:S(2)}) collective-permute-start(bf16[1536,128]{1,0:T(8,128)(2,1)S(1)} %get-tuple-element.10), channel_id=1, source_target_pairs={{0,2},{1,3},{2,0},{3,1},{4,6},{5,7},{6,4},{7,5},{8,10},{9,11},{10,... | collective-permute-start | bytes 1179656 | tf_op jit(solution)/shard_map/ppermute | solution.py:146
  29.4 12.4 %collective-permute-start.2 = (bf16[3072,128]{1,0:T(8,128)(2,1)S(1)}, bf16[3072,128]{1,0:T(8,128)(2,1)}, u32[]{:S(2)}, u32[]{:S(2)}) collective-permute-start(bf16[3072,128]{1,0:T(8,128)(2,1)S(1)} %collective-permute-done.1.first_ref.refs_2_), channel_id=1, source_target_pairs={{0,1},{1,0},{2,3},{3,2},{4,5},{5,4},{6,7},{7,6},{8,9},{9,8},{10,11... | collective-permute-start | bytes 2359304 | tf_op jit(solution)/shard_map/ppermute | solution.py:149
  37.0 3.0 %collective-permute-start.7 = (bf16[1536,128]{1,0:T(8,128)(2,1)}, bf16[1536,128]{1,0:T(8,128)(2,1)}, u32[]{:S(2)}, u32[]{:S(2)}) collective-permute-start(bf16[1536,128]{1,0:T(8,128)(2,1)} %collective-permute-done.5.refs_6_), channel_id=1, source_target_pairs={{0,1},{1,0},{2,3},{3,2},{4,5},{5,4},{6,7},{7,6},{8,9},{9,8},{10,11... | collective-permute-start | bytes 1179656 | tf_op jit(solution)/shard_map/ppermute | solution.py:149
  39.8 2.1 %collective-permute-start.8 = (bf16[1536,128]{1,0:T(8,128)(2,1)}, bf16[1536,128]{1,0:T(8,128)(2,1)}, u32[]{:S(2)}, u32[]{:S(2)}) collective-permute-start(bf16[1536,128]{1,0:T(8,128)(2,1)} %collective-permute-done.6.refs_7_), channel_id=1, source_target_pairs={{0,1},{1,0},{2,3},{3,2},{4,5},{5,4},{6,7},{7,6},{8,9},{9,8},{10,11... | collective-permute-start | bytes 1179656 | tf_op jit(solution)/shard_map/ppermute | solution.py:149
  40.0 23.6 %copy-start.2 = (f32[4,4]{1,0:T(4,128)S(1)}, f32[4,4]{1,0:T(4,128)}, u32[]{:S(2)}) copy-start(f32[4,4]{1,0:T(4,128)} %weights_ref.1) | copy-start | bytes 196
  53.9 4.4 %collective-permute-start.9 = (f32[24,128]{1,0:T(8,128)S(1)}, f32[24,128]{1,0:T(8,128)S(1)}, u32[]{:S(2)}, u32[]{:S(2)}) collective-permute-start(f32[24,128]{1,0:T(8,128)S(1)} %get-tuple-element.12), channel_id=1, source_target_pairs={{0,8},{8,0},{16,24},{24,16},{1,9},{9,1},{17,25},{25,17},{2,10},{10... | collective-permute-start | bytes 36872 | tf_op jit(solution)/shard_map/ppermute | solution.py:192
  55.5 4.6 %collective-permute-start.10 = (f32[24,128]{1,0:T(8,128)S(1)}, f32[24,128]{1,0:T(8,128)S(1)}, u32[]{:S(2)}, u32[]{:S(2)}) collective-permute-start(f32[24,128]{1,0:T(8,128)S(1)} %get-tuple-element.13), channel_id=1, source_target_pairs={{0,16},{8,24},{16,0},{24,8},{1,17},{9,25},{17,1},{25,9},{2,18},{10... | collective-permute-start | bytes 36872 | tf_op jit(solution)/shard_map/ppermute | solution.py:192
  58.1 5.5 %collective-permute-start.11 = (f32[24,128]{1,0:T(8,128)S(1)}, f32[24,128]{1,0:T(8,128)S(1)}, u32[]{:S(2)}, u32[]{:S(2)}) collective-permute-start(f32[24,128]{1,0:T(8,128)S(1)} %get-tuple-element.14), channel_id=1, source_target_pairs={{0,24},{8,16},{16,8},{24,0},{1,25},{9,17},{17,9},{25,1},{2,26},{10... | collective-permute-start | bytes 36872 | tf_op jit(solution)/shard_map/ppermute | solution.py:192

commit v3 on v2

--- a/solution.py
+++ b/solution.py
@@ -16,44 +16,68 @@
     return [(rank, rank ^ distance) for rank in range(ranks)]
 
 
-def pack_pieces(projectors_ref, columns_ref, out_ref):
-    ranks = out_ref.shape[0]
-    rows, width = projectors_ref.shape
-    blocks, held = rows // width, width // ranks
+def pack_pieces(row_ref, panel_ref, projectors_ref, columns_ref, after_ref, *refs):
+    out_refs, turned = refs[:-1], refs[-1]
+    ranks, rows, width = turned.shape
+    held = width // ranks
+    blocks = rows // held
     for block in range(blocks):
-        turned = projectors_ref[block * width : (block + 1) * width].T
-        for device in range(ranks):
-            out_ref[device, block * held : (block + 1) * held] = turned[device * held : (device + 1) * held]
-    for device in range(ranks):
-        out_ref[device, blocks * held :] = columns_ref[...]
-
-
-def cut_halves(first_ref, second_ref, after_ref, low_ref, high_ref):
-    low_ref[...] = first_ref[: low_ref.shape[0]]
-    high_ref[...] = second_ref[low_ref.shape[0] :]
-
-
-def all_steps(ranks, primes, stored, columns_ref, place_ref, pieces_ref, *refs):
-    refs, panels = refs[:-ITERS], refs[-ITERS:]
+        turned[:, block * held : (block + 1) * held] = projectors_ref[block * width : (block + 1) * width].T.reshape(
+            ranks, held, width
+        )
+    first = panel_ref.shape[0]
+    for chip, out in enumerate(out_refs):
+        out[:first] = panel_ref[...]
+        for core in range(2):
+            at = first + core * rows
+            out[at : at + rows] = turned[row_ref[0] ^ (2 * chip + core)]
+        out[first + 2 * rows :] = columns_ref[...]
+
+
+def cut_halves(first_ref, second_ref, same_first_ref, same_second_ref, low_ref, high_ref, arrived):
+    rows = low_ref.shape[0]
+    copies = [
+        pltpu.make_async_copy(first_ref.at[:rows], low_ref, arrived.at[0]),
+        pltpu.make_async_copy(second_ref.at[rows : 2 * rows], high_ref, arrived.at[1]),
+    ]
+    for copy in copies:
+        copy.start()
+    for copy in copies:
+        copy.wait()
+
+
+def join_pieces(*refs):
+    pieces, out_ref = refs[:-2], refs[-1]
+    rows = pieces[0].shape[0]
+    for at, piece in enumerate(pieces):
+        out_ref[at * rows : (at + 1) * rows] = piece[...]
+
+
+def arrive(*refs):
+    pass
+
+
+def all_steps(ranks, primes, stored, columns_ref, place_ref, *refs):
+    chips = ranks // 2
+    near, joined, refs, panels = refs[:chips], refs[chips], refs[chips + 1 : -ITERS], refs[-ITERS:]
     refs, terms_refs, last_ref, terms = refs[: -primes - 2], refs[-primes - 2 : -2], refs[-2], refs[-1]
-    middle = refs[-1].shape[0]
-    refs = [whole.at[part] for whole in refs[:-4] for part in (slice(middle), slice(middle, 2 * middle))] + [*refs[-4:]]
     count, size, width = panels[0].shape
     blocks = count // ranks
     half = blocks // 2
-    depth = half * stored * size
+    rows, piece_rows = refs[-1].shape[0], near[0].shape[0]
+    far = [joined.at[at * piece_rows : (at + 1) * piece_rows] for at in range(chips)]
+    refs = [whole.at[at : at + rows] for whole in refs[:-4] for at in (0, rows)] + [*refs[-4:]]
     first_of = [(place_ref[1] ^ distance) * blocks for distance in range(ranks)]
     for distance, first in enumerate(first_of):
+        piece = (near, far)[distance % 2][distance // 2]
         for row in range(blocks):
-            source = refs[2 * distance + row // half]
-            at = depth + row % half * size
-            panels[0][first + row] = source[at : at + size]
+            panels[0][first + row] = piece[row * size : (row + 1) * size]
 
     def apply_row(old, distance, row):
         source = refs[2 * distance + row // half]
         at = row % half * stored * size
         tiles = [source[at + k * size : at + (k + 1) * size] for k in range(stored)]
-        slot = (first_of[distance] + row) * stored
+        slot = (distance * blocks + row) * stored
         needed = [old[columns_ref[slot + k]] for k in range(stored)]
         return jnp.dot(
             jnp.concatenate(tiles, axis=1), jnp.concatenate(needed, axis=0), preferred_element_type=jnp.float32
@@ -70,11 +94,12 @@
     parts = []
     for step in range(0, ITERS, 2):
         total = None
-        for device in range(ranks):
-            turned = [pieces_ref[device, block * held : (block + 1) * held] for block in range(blocks)]
+        for distance, first in enumerate(first_of):
+            piece = (near, far)[distance % 2][distance // 2]
+            at = blocks * size + distance % 2 * blocks * held
+            turned = [piece[at + block * held : at + (block + 1) * held] for block in range(blocks)]
             seen = [
-                jnp.concatenate([panels[step + j][device * blocks + block] for j in range(2)], axis=1)
-                for block in range(blocks)
+                jnp.concatenate([panels[step + j][first + block] for j in range(2)], axis=1) for block in range(blocks)
             ]
             part = jnp.dot(
                 jnp.concatenate(turned, axis=1), jnp.concatenate(seen, axis=0), preferred_element_type=jnp.float32
@@ -105,18 +130,36 @@
         out_ref[prime] = jnp.concatenate(groups, axis=0).reshape(steps, held, part)
 
 
-def on_chip(kernel, out_shape, smem, vmem, after=(), scratch=(), flops=0, name=None):
-    spaces = [pltpu.SMEM] * len(smem) + [pltpu.VMEM] * len(vmem) + [pl.ANY] * len(after)
+def on_chip(kernel, out_shape, smem, vmem, before=(), after=(), aliases=None, scratch=(), flops=0, name=None):
+    aliases = aliases or {}
+    spaces = [pl.ANY] * len(before) + [pltpu.SMEM] * len(smem) + [pltpu.VMEM] * len(vmem) + [pl.ANY] * len(after)
+    shapes, tree = jax.tree.flatten(out_shape)
+    outs = [pl.BlockSpec(memory_space=pl.ANY if at in aliases.values() else pltpu.VMEM) for at in range(len(shapes))]
     return pl.pallas_call(
         kernel,
         out_shape=out_shape,
         in_specs=[pl.BlockSpec(memory_space=space) for space in spaces],
-        out_specs=jax.tree.map(lambda _: pl.BlockSpec(memory_space=pltpu.VMEM), out_shape),
+        out_specs=jax.tree.unflatten(tree, outs),
         scratch_shapes=list(scratch),
+        input_output_aliases=aliases,
         compiler_params=pltpu.CompilerParams(vmem_limit_bytes=VMEM_BYTES),
         cost_estimate=pl.CostEstimate(flops=flops, bytes_accessed=sum(v.size * v.dtype.itemsize for v in vmem), transcendentals=0),
         name=name,
-    )(*smem, *vmem, *after)
+    )(*before, *smem, *vmem, *after)
+
+
+def arrived(arrays, others):
+    return on_chip(
+        arrive,
+        [jax.ShapeDtypeStruct(array.shape, array.dtype) for array in arrays],
+        [],
+        [],
+        before=arrays,
+        after=others,
+        aliases={at: at for at in range(len(arrays))},
+        flops=20_000_000_000,
+        name="arrive",
+    )
 
 
 def own_columns(tile_slots, requests, my_row, ranks):
@@ -148,41 +191,56 @@
     def to_core(array):
         return lax.ppermute(array, "row", bits_apart(ranks, 1))
 
-    half = blocks // 2
-    by_row = [tiles.reshape(blocks, stored * size, size), panel.reshape(blocks, size, width)]
-    own = jnp.concatenate(
-        [array[rows].reshape(-1, width) for rows in (slice(half), slice(half, blocks)) for array in by_row]
-    )
-    middle = own.shape[0] // 2
+    own = tiles.reshape(-1, width)
     from_x, from_y = to_chip(own, 1), to_chip(own, 2)
+    own_far = to_core(own)
     columns = own_columns(tile_slots[0], requests[0], my_row, ranks)
     columns = jnp.pad(columns.astype(jnp.bfloat16), ((0, held - blocks), (0, width - stored)))
+    chips = ranks // 2
+    last_rows = blocks * size + 2 * blocks * held
     pieces = on_chip(
         pack_pieces,
-        jax.ShapeDtypeStruct((ranks, (blocks + 1) * held, width), jnp.bfloat16),
-        [],
-        [projectors[0], columns],
+        [jax.ShapeDtypeStruct((last_rows + held, width), jnp.bfloat16)] * chips,
+        [my_row.reshape(1)],
+        [panel, projectors[0], columns],
+        after=[own_far],
+        scratch=[pltpu.VMEM((ranks, blocks * held, width), jnp.bfloat16)],
         name="pack_pieces",
     )
-    pieces = lax.all_to_all(pieces, "row", split_axis=0, concat_axis=0, tiled=True)
-    columns = pieces[:, blocks * held :][:, :blocks, :stored].astype(jnp.int32).reshape(-1)
-    low, high = on_chip(
+    pieces = [pieces[0]] + [to_chip(pieces[chip], chip) for chip in range(1, chips)]
+    half = jax.ShapeDtypeStruct((own.shape[0] // 2, width), jnp.bfloat16)
+    whole = jax.ShapeDtypeStruct(own.shape, own.dtype)
+    from_x, from_y, low, high = on_chip(
         cut_halves,
-        [jax.ShapeDtypeStruct((middle, width), jnp.bfloat16)] * 2,
-        [],
-        [from_x, from_y],
-        after=[pieces],
+        [whole, whole, half, half],
+        [],
+        [],
+        before=[from_x, from_y],
+        aliases={0: 0, 1: 1},
+        scratch=[pltpu.SemaphoreType.DMA((2,))],
         name="cut_halves",
     )
-    diagonal = [to_chip(low, 2), to_chip(high, 1)]
-    whole = [array for near in (own, from_x, from_y) for array in (near, to_core(near))]
-    halves = diagonal + [to_core(array) for array in diagonal]
+    diagonal = arrived([to_chip(low, 2), to_chip(high, 1)], [])
+    joined = on_chip(
+        join_pieces,
+        jax.ShapeDtypeStruct((chips * pieces[0].shape[0], width), jnp.bfloat16),
+        [],
+        pieces,
+        after=[low],
+        name="join_pieces",
+    )
+    other = to_core(joined)
+    columns = [piece[last_rows:][:blocks, :stored] for piece in pieces]
+    other_columns = other.reshape(chips, -1, width)[:, last_rows:][:, :blocks, :stored]
+    columns = jnp.stack([jnp.stack(columns), other_columns], axis=1).astype(jnp.int32).reshape(-1)
+    whole = [own, own_far] + [array for near in (from_x, from_y) for array in (near, to_core(near))]
+    halves = [*diagonal] + [to_core(array) for array in diagonal]
     piece = jax.ShapeDtypeStruct((ITERS * held // primes, width), jnp.float32)
     *terms, last = on_chip(
         functools.partial(all_steps, ranks, primes, stored),
         [piece] * primes + [jax.ShapeDtypeStruct((blocks * size, width), jnp.bfloat16)],
         [columns, place],
-        [pieces, *whole, *halves],
+        [*pieces, other, *whole, *halves],
         scratch=[pltpu.VMEM((primes, *piece.shape), jnp.float32)]
         + [pltpu.VMEM((ranks * blocks, size, width), jnp.bfloat16)] * ITERS,
         flops=2 * ITERS * ranks * tiles.size * width,

time: 65.2 us -> 61.7 us (0.946)
  waiting for transfers between devices: 31.1 us -> 27.1 us
  local copies, waits for them, and re-layouts: 2.5 us -> 3.99 us
  Pallas kernels: 14.3 us -> 13.6 us
    all_to_all x1 -> x0, waiting for transfers between devices: 13.9 us -> none  [whole_system(): lax.all_to_all(pieces, 'row', split_axis=0, concat_axis=0, tiled=True)]
    ppermute x4 -> x7, waiting for transfers between devices: 10.1 us -> 20 us  [to_chip(): return lax.ppermute(array, 'row', bits_apart(ranks, 2 * chip))]
    unnamed x8 -> x12, local copies, waits for them, and re-layouts: 0.03 us -> 3.51 us
    all_to_all x1 -> x0, starting transfers between devices: 3.38 us -> none  [whole_system(): lax.all_to_all(pieces, 'row', split_axis=0, concat_axis=0, tiled=True)]
    ppermute x4 -> x7, starting transfers between devices: 7.53 us -> 9.76 us  [to_chip(): return lax.ppermute(array, 'row', bits_apart(ranks, 2 * chip))]
    slice x1 -> x0, local copies, waits for them, and re-layouts: 1.12 us -> none  [whole_system(): array[rows].reshape(-1, width)]
    reshape x2 -> x0, local copies, waits for them, and re-layouts: 1 us -> none  [the longest x1 0.89 us: whole_system(): array[rows].reshape(-1, width)]
    ppermute x5 -> x6, starting transfers between devices: 0.64 us -> 1.61 us  [to_core(): return lax.ppermute(array, 'row', bits_apart(ranks, 1))]
  transfers between devices with their start and end apart: 13 -> 16, of which waited for: 6 -> 8; matrix products, arithmetic and copies ran while one was open for 1% -> 1% of each run, Pallas kernels for 1% -> 1%
where the time goes in v3:
time: 61.7 us; the launch traced here: 61.5 us
  waiting for transfers between devices  27.1 us (44%)
  starting transfers between devices  15.8 us (26%)
  Pallas kernels  13.6 us (22%)
  local copies, waits for them, and re-layouts  3.99 us (6%)
  between operations  0.72 us (1%)
    ppermute x7, waiting for transfers between devices, to_chip(): return lax.ppermute(array, 'row', bits_apart(ranks, 2 * chip))  20 us
    pallas_call x6, Pallas kernels, on_chip(): pl.pallas_call(kernel, out_shape=out_shape, in_specs=[pl.BlockSpec(memory...  13.6 us
    ppermute x7, starting transfers between devices, to_chip(): return lax.ppermute(array, 'row', bits_apart(ranks, 2 * chip))  9.76 us
    ppermute x3, waiting for transfers between devices, whole_system(): lax.ppermute(terms[bits], 'prime', bits_apart(primes, bits))  5.27 us
    ppermute x3, starting transfers between devices, whole_system(): lax.ppermute(terms[bits], 'prime', bits_apart(primes, bits))  4.39 us
    unnamed x12, local copies, waits for them, and re-layouts  3.51 us
    ppermute x6, waiting for transfers between devices, to_core(): return lax.ppermute(array, 'row', bits_apart(ranks, 1))  1.79 us
    ppermute x6, starting transfers between devices, to_core(): return lax.ppermute(array, 'row', bits_apart(ranks, 1))  1.61 us
  transfers between devices with their start and end apart: 16, of which 8 were waited for; matrix products, arithmetic and copies ran while one was open for 1% of the time, Pallas kernels for 1%

profile of v3, /device:TPU:0, one launch (start us, length us, event | category | flops | bytes accessed | tf_op | source)
XLA Modules:
  0.0 61.5 jit_solution(8466393541502748036)
XLA Ops:
  0.6 0.0 copy-start
  0.6 0.5 collective-permute-start
  1.2 2.6 %collective-permute-start.4 = (bf16[2560,128]{1,0:T(8,128)(2,1)}, bf16[2560,128]{1,0:T(8,128)(2,1)S(1)}, u32[]{:S(2)}, u32[]{:S(2)}) collective-permute-start(bf16[2560,128]{1,0:T(8,128)(2,1)} %bitcast.27), channel_id=1, source_target_pairs={{0,2},{1,3},{2,0},{3,1},{4,6},{5,7},{6,4},{7,5},{8,10},{9,11},{10,... | collective-permute-start | bytes 1966088 | tf_op jit(solution)/shard_map/ppermute | solution.py:189
  3.7 1.5 %collective-permute-start.5 = (bf16[2560,128]{1,0:T(8,128)(2,1)}, bf16[2560,128]{1,0:T(8,128)(2,1)S(1)}, u32[]{:S(2)}, u32[]{:S(2)}) collective-permute-start(bf16[2560,128]{1,0:T(8,128)(2,1)} %bitcast.28), channel_id=1, source_target_pairs={{0,4},{1,5},{2,6},{3,7},{4,0},{5,1},{6,2},{7,3},{8,12},{9,13},{10,... | collective-permute-start | bytes 1966088 | tf_op jit(solution)/shard_map/ppermute | solution.py:189
  5.2 0.0 copy-done
  5.3 0.1 copy.16
  5.3 0.0 copy-start.5
  5.3 0.1 broadcast_in_dim.17
  5.4 0.6 copy-done.5
  6.0 0.1 copy.15
  6.1 0.2 select_reduce_fusion
  6.4 0.1 copy.17
  6.5 0.1 pad_add_fusion.place_ref
  6.6 0.0 collective-permute-done.after_ref.refs_6_
  6.6 0.0 copy-start.1
  6.6 0.9 %copy-done.1 = bf16[1,512,128]{2,1,0:T(8,128)(2,1)S(1)} copy-done((bf16[1,512,128]{2,1,0:T(8,128)(2,1)S(1)}, bf16[1,512,128]{2,1,0:T(8,128)(2,1)}, u32[]{:S(2)}) %copy-start.1) | copy-done | bytes 131096
  7.5 0.0 copy-start.2
  7.5 0.9 %copy-done.2 = bf16[1,512,128]{2,1,0:T(8,128)(2,1)S(1)} copy-done((bf16[1,512,128]{2,1,0:T(8,128)(2,1)S(1)}, bf16[1,512,128]{2,1,0:T(8,128)(2,1)}, u32[]{:S(2)}) %copy-start.2) | copy-done | bytes 131096
  8.4 0.1 pack_pieces.1
  8.5 0.6 collective-permute-start.1
  9.1 0.4 collective-permute-start.2
  9.5 2.6 %collective-permute-start.3 = (bf16[656,128]{1,0:T(8,128)(2,1)S(1)}, bf16[656,128]{1,0:T(8,128)(2,1)S(1)}, u32[]{:S(2)}, u32[]{:S(2)}) collective-permute-start(bf16[656,128]{1,0:T(8,128)(2,1)S(1)} %get-tuple-element.20), channel_id=1, source_target_pairs={{0,6},{1,7},{2,4},{3,5},{4,2},{5,3},{6,0},{7,1},{8,14},{9,15},{10,... | collective-permute-start | bytes 503816 | tf_op jit(solution)/shard_map/ppermute | solution.py:189
  12.0 7.5 %collective-permute-done.4.first_ref = bf16[2560,128]{1,0:T(8,128)(2,1)S(1)} collective-permute-done((bf16[2560,128]{1,0:T(8,128)(2,1)}, bf16[2560,128]{1,0:T(8,128)(2,1)S(1)}, u32[]{:S(2)}, u32[]{:S(2)}) %collective-permute-start.4) | collective-permute-done | bytes 655392 | tf_op jit(solution)/shard_map/ppermute | solution.py:189
  19.5 2.0 %collective-permute-done.5.second_ref = bf16[2560,128]{1,0:T(8,128)(2,1)S(1)} collective-permute-done((bf16[2560,128]{1,0:T(8,128)(2,1)}, bf16[2560,128]{1,0:T(8,128)(2,1)S(1)}, u32[]{:S(2)}, u32[]{:S(2)}) %collective-permute-start.5) | collective-permute-done | bytes 655392 | tf_op jit(solution)/shard_map/ppermute | solution.py:189
  21.5 0.2 cut_halves.1
  21.7 1.6 %collective-permute-start.9 = (bf16[1280,128]{1,0:T(8,128)(2,1)S(1)}, bf16[1280,128]{1,0:T(8,128)(2,1)}, u32[]{:S(2)}, u32[]{:S(2)}) collective-permute-start(bf16[1280,128]{1,0:T(8,128)(2,1)S(1)} %get-tuple-element.21.refs_4_), channel_id=1, source_target_pairs={{0,4},{1,5},{2,6},{3,7},{4,0},{5,1},{6,2},{7,3},{8,12},{9,13},{10,... | collective-permute-start | bytes 983048 | tf_op jit(solution)/shard_map/ppermute | solution.py:189
  23.3 0.5 collective-permute-start.10
  23.9 0.0 collective-permute-done.1.refs_1_
  23.9 0.0 collective-permute-start.7
  23.9 4.8 %collective-permute-done.2.refs_2_ = bf16[656,128]{1,0:T(8,128)(2,1)S(1)} collective-permute-done((bf16[656,128]{1,0:T(8,128)(2,1)S(1)}, bf16[656,128]{1,0:T(8,128)(2,1)S(1)}, u32[]{:S(2)}, u32[]{:S(2)}) %collective-permute-start.2) | collective-permute-done | bytes 167968 | tf_op jit(solution)/shard_map/ppermute | solution.py:189
  28.7 0.0 collective-permute-start.8
  28.7 0.0 collective-permute-done.3.refs_3_
  28.8 0.6 collective-permute-start.6
  29.4 5.7 %collective-permute-done.9.refs_0_ = bf16[1280,128]{1,0:T(8,128)(2,1)} collective-permute-done((bf16[1280,128]{1,0:T(8,128)(2,1)S(1)}, bf16[1280,128]{1,0:T(8,128)(2,1)}, u32[]{:S(2)}, u32[]{:S(2)}) %collective-permute-start.9) | collective-permute-done | bytes 327712 | tf_op jit(solution)/shard_map/ppermute | solution.py:189
  35.1 0.0 collective-permute-done.10.refs_1_
  35.1 0.0 collective-permute-start.11
  35.1 0.5 collective-permute-start.12
  35.6 0.0 collective-permute-done.6.refs_4_
  35.6 0.1 reshape.18.columns_ref
  35.7 1.3 %collective-permute-done.11.refs_13_ = bf16[1280,128]{1,0:T(8,128)(2,1)} collective-permute-done((bf16[1280,128]{1,0:T(8,128)(2,1)}, bf16[1280,128]{1,0:T(8,128)(2,1)}, u32[]{:S(2)}, u32[]{:S(2)}) %collective-permute-start.11) | collective-permute-done | bytes 327712 | tf_op jit(solution)/shard_map/ppermute | solution.py:192
  37.0 0.5 collective-permute-done.12.refs_14_
  37.5 0.0 collective-permute-done.7.refs_8_
  37.5 0.0 collective-permute-done.8.refs_10_
  37.5 0.0 copy-start.4
  37.5 1.1 %copy-done.4 = bf16[1,4,5,128,128]{4,3,2,1,0:T(8,128)(2,1)S(1)} copy-done((bf16[1,4,5,128,128]{4,3,2,1,0:T(8,128)(2,1)S(1)}, bf16[1,4,5,128,128]{4,3,2,1,0:T(8,128)(2,1)}, u32[]{:S(2)}) %copy-start.4) | copy-done | bytes 655384
  38.6 11.8 %all_steps.1 = (f32[24,128]{1,0:T(8,128)S(1)}, f32[24,128]{1,0:T(8,128)S(1)}, f32[24,128]{1,0:T(8,128)S(1)}, f32[24,128]{1,0:T(8,128)S(1)}, bf16[512,128]{1,0:T(8,128)(2,1)}) custom-call(s32[160]{0:T(256)S(1)} %reshape.18.columns_ref, s32[2]{0:T(128)S(1)} %pad_add_fusion.place_ref, bf16[656,128]{1,0:T(8,128)(2,1)S(1)} %get-tuple-element.17.refs_0_, ...), custom_call_target="tpu_custom_call" | custom-call | flops 4026531840 | bytes 6586368 | tf_op jit(solution)/shard_map/all_steps/pallas_call | solution.py:138
  50.5 1.6 %collective-permute-start.13 = (f32[24,128]{1,0:T(8,128)S(1)}, f32[24,128]{1,0:T(8,128)S(1)}, u32[]{:S(2)}, u32[]{:S(2)}) collective-permute-start(f32[24,128]{1,0:T(8,128)S(1)} %get-tuple-element.28), channel_id=1, source_target_pairs={{0,8},{8,0},{16,24},{24,16},{1,9},{9,1},{17,25},{25,17},{2,10},{10... | collective-permute-start | bytes 36872 | tf_op jit(solution)/shard_map/ppermute | solution.py:250
  52.0 0.0 copy-start.3
  52.0 2.6 %collective-permute-start.14 = (f32[24,128]{1,0:T(8,128)S(1)}, f32[24,128]{1,0:T(8,128)S(1)}, u32[]{:S(2)}, u32[]{:S(2)}) collective-permute-start(f32[24,128]{1,0:T(8,128)S(1)} %get-tuple-element.29), channel_id=1, source_target_pairs={{0,16},{8,24},{16,0},{24,8},{1,17},{9,25},{17,1},{25,9},{2,18},{10... | collective-permute-start | bytes 36872 | tf_op jit(solution)/shard_map/ppermute | solution.py:250
  54.6 0.2 collective-permute-start.15
  54.9 0.0 collective-permute-done.13.refs_1_
  54.9 1.8 %collective-permute-done.14.refs_2_ = f32[24,128]{1,0:T(8,128)S(1)} collective-permute-done((f32[24,128]{1,0:T(8,128)S(1)}, f32[24,128]{1,0:T(8,128)S(1)}, u32[]{:S(2)}, u32[]{:S(2)}) %collective-permute-start.14) | collective-permute-done | bytes 12320 | tf_op jit(solution)/shard_map/ppermute | solution.py:250
  56.7 3.5 %collective-permute-done.15.refs_3_ = f32[24,128]{1,0:T(8,128)S(1)} collective-permute-done((f32[24,128]{1,0:T(8,128)S(1)}, f32[24,128]{1,0:T(8,128)S(1)}, u32[]{:S(2)}, u32[]{:S(2)}) %collective-permute-start.15) | collective-permute-done | bytes 12320 | tf_op jit(solution)/shard_map/ppermute | solution.py:250
  60.1 0.0 copy-done.3
  60.1 1.4 %mix_terms.1 = f32[4,6,16,32]{3,2,1,0:T(8,128)} custom-call(s32[2]{0:T(128)S(1)} %pad_add_fusion.place_ref, f32[4,4]{1,0:T(4,128)S(1)} %copy-done.3, f32[24,128]{1,0:T(8,128)S(1)} %get-tuple-element.27.refs_0_, f32[24,128]{1,0:T(8,128)S(1)} %collective-permute-done.13.refs_1_, f32[24,128]{1,0:T(8,128)S(1)} %collective-permute-done.14.refs_2_, ...), custom_call_target="tpu_custom_call" | custom-call | bytes 49152 | tf_op jit(solution)/shard_map/mix_terms/pallas_call | solution.py:138
  (13 shorter events, 0.1 us)
Async XLA Ops:
  0.6 4.6 %copy-start = (s32[1,8,8,2]{2,3,1,0:T(2,128)S(1)}, s32[1,8,8,2]{2,3,1,0:T(2,128)}, u32[]{:S(2)}) copy-start(s32[1,8,8,2]{2,3,1,0:T(2,128)} %param.8) | copy-start | bytes 1540
  0.6 5.9 %collective-permute-start = (bf16[2560,128]{1,0:T(8,128)(2,1)}, bf16[2560,128]{1,0:T(8,128)(2,1)S(1)}, u32[]{:S(2)}, u32[]{:S(2)}) collective-permute-start(bf16[2560,128]{1,0:T(8,128)(2,1)} %bitcast.26), channel_id=1, source_target_pairs={{0,1},{1,0},{2,3},{3,2},{4,5},{5,4},{6,7},{7,6},{8,9},{9,8},{10,11... | collective-permute-start | bytes 1966088 | tf_op jit(solution)/shard_map/ppermute | solution.py:192
  1.2 18.4 %collective-permute-start.4 = (bf16[2560,128]{1,0:T(8,128)(2,1)}, bf16[2560,128]{1,0:T(8,128)(2,1)S(1)}, u32[]{:S(2)}, u32[]{:S(2)}) collective-permute-start(bf16[2560,128]{1,0:T(8,128)(2,1)} %bitcast.27), channel_id=1, source_target_pairs={{0,2},{1,3},{2,0},{3,1},{4,6},{5,7},{6,4},{7,5},{8,10},{9,11},{10,... | collective-permute-start | bytes 1966088 | tf_op jit(solution)/shard_map/ppermute | solution.py:189
  3.7 17.8 %collective-permute-start.5 = (bf16[2560,128]{1,0:T(8,128)(2,1)}, bf16[2560,128]{1,0:T(8,128)(2,1)S(1)}, u32[]{:S(2)}, u32[]{:S(2)}) collective-permute-start(bf16[2560,128]{1,0:T(8,128)(2,1)} %bitcast.28), channel_id=1, source_target_pairs={{0,4},{1,5},{2,6},{3,7},{4,0},{5,1},{6,2},{7,3},{8,12},{9,13},{10,... | collective-permute-start | bytes 1966088 | tf_op jit(solution)/shard_map/ppermute | solution.py:189
  5.3 0.7 %copy-start.5 = (s32[1,4,5]{2,1,0:T(4,128)S(1)}, s32[1,4,5]{2,1,0:T(4,128)}, u32[]{:S(2)}) copy-start(s32[1,4,5]{2,1,0:T(4,128)} %param.7) | copy-start | bytes 244
  6.6 0.9 %copy-start.1 = (bf16[1,512,128]{2,1,0:T(8,128)(2,1)S(1)}, bf16[1,512,128]{2,1,0:T(8,128)(2,1)}, u32[]{:S(2)}) copy-start(bf16[1,512,128]{2,1,0:T(8,128)(2,1)} %param.9) | copy-start | bytes 393220
  7.5 0.9 %copy-start.2 = (bf16[1,512,128]{2,1,0:T(8,128)(2,1)S(1)}, bf16[1,512,128]{2,1,0:T(8,128)(2,1)}, u32[]{:S(2)}) copy-start(bf16[1,512,128]{2,1,0:T(8,128)(2,1)} %param.10) | copy-start | bytes 393220
  8.5 15.4 %collective-permute-start.1 = (bf16[656,128]{1,0:T(8,128)(2,1)S(1)}, bf16[656,128]{1,0:T(8,128)(2,1)S(1)}, u32[]{:S(2)}, u32[]{:S(2)}) collective-permute-start(bf16[656,128]{1,0:T(8,128)(2,1)S(1)} %get-tuple-element.18), channel_id=1, source_target_pairs={{0,2},{1,3},{2,0},{3,1},{4,6},{5,7},{6,4},{7,5},{8,10},{9,11},{10,... | collective-permute-start | bytes 503816 | tf_op jit(solution)/shard_map/ppermute | solution.py:189
  9.1 19.6 %collective-permute-start.2 = (bf16[656,128]{1,0:T(8,128)(2,1)S(1)}, bf16[656,128]{1,0:T(8,128)(2,1)S(1)}, u32[]{:S(2)}, u32[]{:S(2)}) collective-permute-start(bf16[656,128]{1,0:T(8,128)(2,1)S(1)} %get-tuple-element.19), channel_id=1, source_target_pairs={{0,4},{1,5},{2,6},{3,7},{4,0},{5,1},{6,2},{7,3},{8,12},{9,13},{10,... | collective-permute-start | bytes 503816 | tf_op jit(solution)/shard_map/ppermute | solution.py:189
  9.5 19.3 %collective-permute-start.3 = (bf16[656,128]{1,0:T(8,128)(2,1)S(1)}, bf16[656,128]{1,0:T(8,128)(2,1)S(1)}, u32[]{:S(2)}, u32[]{:S(2)}) collective-permute-start(bf16[656,128]{1,0:T(8,128)(2,1)S(1)} %get-tuple-element.20), channel_id=1, source_target_pairs={{0,6},{1,7},{2,4},{3,5},{4,2},{5,3},{6,0},{7,1},{8,14},{9,15},{10,... | collective-permute-start | bytes 503816 | tf_op jit(solution)/shard_map/ppermute | solution.py:189
  21.7 13.3 %collective-permute-start.9 = (bf16[1280,128]{1,0:T(8,128)(2,1)S(1)}, bf16[1280,128]{1,0:T(8,128)(2,1)}, u32[]{:S(2)}, u32[]{:S(2)}) collective-permute-start(bf16[1280,128]{1,0:T(8,128)(2,1)S(1)} %get-tuple-element.21.refs_4_), channel_id=1, source_target_pairs={{0,4},{1,5},{2,6},{3,7},{4,0},{5,1},{6,2},{7,3},{8,12},{9,13},{10,... | collective-permute-start | bytes 983048 | tf_op jit(solution)/shard_map/ppermute | solution.py:189
  23.3 11.7 %collective-permute-start.10 = (bf16[1280,128]{1,0:T(8,128)(2,1)S(1)}, bf16[1280,128]{1,0:T(8,128)(2,1)}, u32[]{:S(2)}, u32[]{:S(2)}) collective-permute-start(bf16[1280,128]{1,0:T(8,128)(2,1)S(1)} %get-tuple-element.24), channel_id=1, source_target_pairs={{0,2},{1,3},{2,0},{3,1},{4,6},{5,7},{6,4},{7,5},{8,10},{9,11},{10,... | collective-permute-start | bytes 983048 | tf_op jit(solution)/shard_map/ppermute | solution.py:189
  23.9 13.6 %collective-permute-start.7 = (bf16[2560,128]{1,0:T(8,128)(2,1)S(1)}, bf16[2560,128]{1,0:T(8,128)(2,1)}, u32[]{:S(2)}, u32[]{:S(2)}) collective-permute-start(bf16[2560,128]{1,0:T(8,128)(2,1)S(1)} %get-tuple-element.22.refs_7_), channel_id=1, source_target_pairs={{0,1},{1,0},{2,3},{3,2},{4,5},{5,4},{6,7},{7,6},{8,9},{9,8},{10,11... | collective-permute-start | bytes 1966088 | tf_op jit(solution)/shard_map/ppermute | solution.py:192
  28.7 8.8 %collective-permute-start.8 = (bf16[2560,128]{1,0:T(8,128)(2,1)S(1)}, bf16[2560,128]{1,0:T(8,128)(2,1)}, u32[]{:S(2)}, u32[]{:S(2)}) collective-permute-start(bf16[2560,128]{1,0:T(8,128)(2,1)S(1)} %get-tuple-element.23.refs_9_), channel_id=1, source_target_pairs={{0,1},{1,0},{2,3},{3,2},{4,5},{5,4},{6,7},{7,6},{8,9},{9,8},{10,11... | collective-permute-start | bytes 1966088 | tf_op jit(solution)/shard_map/ppermute | solution.py:192
  28.8 6.8 %collective-permute-start.6 = (bf16[2624,128]{1,0:T(8,128)(2,1)S(1)}, bf16[2624,128]{1,0:T(8,128)(2,1)S(1)}, u32[]{:S(2)}, u32[]{:S(2)}) collective-permute-start(bf16[2624,128]{1,0:T(8,128)(2,1)S(1)} %join_pieces.1), channel_id=1, source_target_pairs={{0,1},{1,0},{2,3},{3,2},{4,5},{5,4},{6,7},{7,6},{8,9},{9,8},{10,11... | collective-permute-start | bytes 2015240 | tf_op jit(solution)/shard_map/ppermute | solution.py:192
  35.1 2.0 %collective-permute-start.11 = (bf16[1280,128]{1,0:T(8,128)(2,1)}, bf16[1280,128]{1,0:T(8,128)(2,1)}, u32[]{:S(2)}, u32[]{:S(2)}) collective-permute-start(bf16[1280,128]{1,0:T(8,128)(2,1)} %get-tuple-element.25.refs_11_), channel_id=1, source_target_pairs={{0,1},{1,0},{2,3},{3,2},{4,5},{5,4},{6,7},{7,6},{8,9},{9,8},{10,11... | collective-permute-start | bytes 983048 | tf_op jit(solution)/shard_map/ppermute | solution.py:192
  35.1 2.4 %collective-permute-start.12 = (bf16[1280,128]{1,0:T(8,128)(2,1)}, bf16[1280,128]{1,0:T(8,128)(2,1)}, u32[]{:S(2)}, u32[]{:S(2)}) collective-permute-start(bf16[1280,128]{1,0:T(8,128)(2,1)} %get-tuple-element.26.refs_12_), channel_id=1, source_target_pairs={{0,1},{1,0},{2,3},{3,2},{4,5},{5,4},{6,7},{7,6},{8,9},{9,8},{10,11... | collective-permute-start | bytes 983048 | tf_op jit(solution)/shard_map/ppermute | solution.py:192
  37.5 1.1 %copy-start.4 = (bf16[1,4,5,128,128]{4,3,2,1,0:T(8,128)(2,1)S(1)}, bf16[1,4,5,128,128]{4,3,2,1,0:T(8,128)(2,1)}, u32[]{:S(2)}) copy-start(bf16[1,4,5,128,128]{4,3,2,1,0:T(8,128)(2,1)} %param.6) | copy-start | bytes 1966084
  50.5 4.4 %collective-permute-start.13 = (f32[24,128]{1,0:T(8,128)S(1)}, f32[24,128]{1,0:T(8,128)S(1)}, u32[]{:S(2)}, u32[]{:S(2)}) collective-permute-start(f32[24,128]{1,0:T(8,128)S(1)} %get-tuple-element.28), channel_id=1, source_target_pairs={{0,8},{8,0},{16,24},{24,16},{1,9},{9,1},{17,25},{25,17},{2,10},{10... | collective-permute-start | bytes 36872 | tf_op jit(solution)/shard_map/ppermute | solution.py:250
  52.0 8.1 %copy-start.3 = (f32[4,4]{1,0:T(4,128)S(1)}, f32[4,4]{1,0:T(4,128)}, u32[]{:S(2)}) copy-start(f32[4,4]{1,0:T(4,128)} %weights_ref.1) | copy-start | bytes 196
  52.0 4.6 %collective-permute-start.14 = (f32[24,128]{1,0:T(8,128)S(1)}, f32[24,128]{1,0:T(8,128)S(1)}, u32[]{:S(2)}, u32[]{:S(2)}) collective-permute-start(f32[24,128]{1,0:T(8,128)S(1)} %get-tuple-element.29), channel_id=1, source_target_pairs={{0,16},{8,24},{16,0},{24,8},{1,17},{9,25},{17,1},{25,9},{2,18},{10... | collective-permute-start | bytes 36872 | tf_op jit(solution)/shard_map/ppermute | solution.py:250
  54.6 5.5 %collective-permute-start.15 = (f32[24,128]{1,0:T(8,128)S(1)}, f32[24,128]{1,0:T(8,128)S(1)}, u32[]{:S(2)}, u32[]{:S(2)}) collective-permute-start(f32[24,128]{1,0:T(8,128)S(1)} %get-tuple-element.30), channel_id=1, source_target_pairs={{0,24},{8,16},{16,8},{24,0},{1,25},{9,17},{17,9},{25,1},{2,26},{10... | collective-permute-start | bytes 36872 | tf_op jit(solution)/shard_map/ppermute | solution.py:250

commit v4 on v3

--- a/solution.py
+++ b/solution.py
@@ -34,7 +34,7 @@
         out[first + 2 * rows :] = columns_ref[...]
 
 
-def cut_halves(first_ref, second_ref, same_first_ref, same_second_ref, low_ref, high_ref, arrived):
+def cut_halves(first_ref, second_ref, after_ref, same_first_ref, same_second_ref, low_ref, high_ref, arrived):
     rows = low_ref.shape[0]
     copies = [
         pltpu.make_async_copy(first_ref.at[:rows], low_ref, arrived.at[0]),
@@ -57,47 +57,73 @@
     pass
 
 
+def apply_row(columns_ref, old, slot, stored, source, at):
+    size = old.shape[1]
+    tiles = [source[at + k * size : at + (k + 1) * size] for k in range(stored)]
+    needed = [old[columns_ref[slot + k]] for k in range(stored)]
+    return jnp.dot(
+        jnp.concatenate(tiles, axis=1), jnp.concatenate(needed, axis=0), preferred_element_type=jnp.float32
+    ).astype(jnp.bfloat16)
+
+
+def first_step(ranks, stored, columns_ref, place_ref, *refs):
+    chips = ranks // 2
+    near, joined, tiles, (start_ref, part_ref, turned_ref) = refs[:chips], refs[chips], refs[chips + 1 : -3], refs[-3:]
+    held_rows = turned_ref.shape[1]
+    count, size, width = start_ref.shape
+    blocks = count // ranks
+    piece_rows = near[0].shape[0]
+    for distance in range(ranks):
+        first = (place_ref[1] ^ distance) * blocks
+        piece = near[distance // 2]
+        if distance % 2:
+            piece = joined.at[distance // 2 * piece_rows : (distance // 2 + 1) * piece_rows]
+        for row in range(blocks):
+            start_ref[first + row] = piece[row * size : (row + 1) * size]
+        at = blocks * size + distance % 2 * held_rows
+        turned_ref[distance] = piece[at : at + held_rows]
+    for row in range(part_ref.shape[0]):
+        part_ref[row] = apply_row(
+            columns_ref, start_ref, row * stored, stored, tiles[row // blocks], row % blocks * stored * size
+        )
+
+
 def all_steps(ranks, primes, stored, columns_ref, place_ref, *refs):
-    chips = ranks // 2
-    near, joined, refs, panels = refs[:chips], refs[chips], refs[chips + 1 : -ITERS], refs[-ITERS:]
+    (start, part, projectors), refs, panels = refs[:3], refs[3 : 1 - ITERS], refs[1 - ITERS :]
     refs, terms_refs, last_ref, terms = refs[: -primes - 2], refs[-primes - 2 : -2], refs[-2], refs[-1]
-    count, size, width = panels[0].shape
+    count, size, width = start.shape
     blocks = count // ranks
-    half = blocks // 2
-    rows, piece_rows = refs[-1].shape[0], near[0].shape[0]
-    far = [joined.at[at * piece_rows : (at + 1) * piece_rows] for at in range(chips)]
+    rows = refs[-1].shape[0]
     refs = [whole.at[at : at + rows] for whole in refs[:-4] for at in (0, rows)] + [*refs[-4:]]
     first_of = [(place_ref[1] ^ distance) * blocks for distance in range(ranks)]
-    for distance, first in enumerate(first_of):
-        piece = (near, far)[distance % 2][distance // 2]
-        for row in range(blocks):
-            panels[0][first + row] = piece[row * size : (row + 1) * size]
-
-    def apply_row(old, distance, row):
-        source = refs[2 * distance + row // half]
-        at = row % half * stored * size
-        tiles = [source[at + k * size : at + (k + 1) * size] for k in range(stored)]
-        slot = (distance * blocks + row) * stored
-        needed = [old[columns_ref[slot + k]] for k in range(stored)]
-        return jnp.dot(
-            jnp.concatenate(tiles, axis=1), jnp.concatenate(needed, axis=0), preferred_element_type=jnp.float32
-        ).astype(jnp.bfloat16)
-
-    for old, new in zip(panels[:-1], panels[1:]):
+    half = blocks // 2
+
+    def apply(old, distance, row):
+        return apply_row(
+            columns_ref,
+            old,
+            (distance * blocks + row) * stored,
+            stored,
+            refs[2 * distance + row // half],
+            row % half * stored * size,
+        )
+
+    panels = [start, *panels]
+    for step, (old, new) in enumerate(zip(panels[:-1], panels[1:])):
         for distance, first in enumerate(first_of):
             for row in range(blocks):
-                new[first + row] = apply_row(old, distance, row)
+                given = distance * blocks + row
+                known = step == 0 and given < part.shape[0]
+                new[first + row] = part[given] if known else apply(old, distance, row)
     for row in range(blocks):
-        last_ref[row * size : (row + 1) * size] = apply_row(panels[-1], 0, row)
+        last_ref[row * size : (row + 1) * size] = apply(panels[-1], 0, row)
 
     held = width // ranks
     parts = []
     for step in range(0, ITERS, 2):
         total = None
         for distance, first in enumerate(first_of):
-            piece = (near, far)[distance % 2][distance // 2]
-            at = blocks * size + distance % 2 * blocks * held
-            turned = [piece[at + block * held : at + (block + 1) * held] for block in range(blocks)]
+            turned = [projectors[distance, block * held : (block + 1) * held] for block in range(blocks)]
             seen = [
                 jnp.concatenate([panels[step + j][first + block] for j in range(2)], axis=1) for block in range(blocks)
             ]
@@ -216,11 +242,12 @@
         [],
         [],
         before=[from_x, from_y],
+        after=pieces[:1],
         aliases={0: 0, 1: 1},
         scratch=[pltpu.SemaphoreType.DMA((2,))],
         name="cut_halves",
     )
-    diagonal = arrived([to_chip(low, 2), to_chip(high, 1)], [])
+    diagonal = [to_chip(low, 2), to_chip(high, 1)]
     joined = on_chip(
         join_pieces,
         jax.ShapeDtypeStruct((chips * pieces[0].shape[0], width), jnp.bfloat16),
@@ -234,15 +261,29 @@
     other_columns = other.reshape(chips, -1, width)[:, last_rows:][:, :blocks, :stored]
     columns = jnp.stack([jnp.stack(columns), other_columns], axis=1).astype(jnp.int32).reshape(-1)
     whole = [own, own_far] + [array for near in (from_x, from_y) for array in (near, to_core(near))]
+    piece = jax.ShapeDtypeStruct((ITERS * held // primes, width), jnp.float32)
+    shape = (ranks * blocks, size, width)
+    given = on_chip(
+        functools.partial(first_step, ranks, stored),
+        [
+            jax.ShapeDtypeStruct(shape, jnp.bfloat16),
+            jax.ShapeDtypeStruct(((ranks - 2) * blocks, size, width), jnp.bfloat16),
+            jax.ShapeDtypeStruct((ranks, blocks * held, width), jnp.bfloat16),
+        ],
+        [columns, place],
+        [*pieces, other, *whole],
+        flops=2 * (ranks - 2) * tiles.size * width,
+        name="first_step",
+    )
+    diagonal = arrived(diagonal, given[2:])
     halves = [*diagonal] + [to_core(array) for array in diagonal]
-    piece = jax.ShapeDtypeStruct((ITERS * held // primes, width), jnp.float32)
     *terms, last = on_chip(
         functools.partial(all_steps, ranks, primes, stored),
         [piece] * primes + [jax.ShapeDtypeStruct((blocks * size, width), jnp.bfloat16)],
         [columns, place],
-        [*pieces, other, *whole, *halves],
+        [*given, *whole, *halves],
         scratch=[pltpu.VMEM((primes, *piece.shape), jnp.float32)]
-        + [pltpu.VMEM((ranks * blocks, size, width), jnp.bfloat16)] * ITERS,
+        + [pltpu.VMEM(shape, jnp.bfloat16)] * (ITERS - 1),
         flops=2 * ITERS * ranks * tiles.size * width,
         name="all_steps",
     )

time: 61.7 us -> 59.3 us (0.961)
  waiting for transfers between devices: 27.1 us -> 22.5 us
  Pallas kernels: 13.6 us -> 15.7 us
    ppermute x7, waiting for transfers between devices: 20 us -> 13.4 us  [to_chip(): return lax.ppermute(array, 'row', bits_apart(ranks, 2 * chip))]
    pallas_call x6 -> x7, Pallas kernels: 13.6 us -> 15.7 us  [on_chip(): pl.pallas_call(kernel, out_shape=out_shape, in_specs=[pl.BlockSpec(memory...]
    ppermute x6, waiting for transfers between devices: 1.79 us -> 3.86 us  [to_core(): return lax.ppermute(array, 'row', bits_apart(ranks, 1))]
    unnamed x12 -> x14, local copies, waits for them, and re-layouts: 3.51 us -> 3.51 us
  transfers between devices with their start and end apart: 16 -> 16, of which waited for: 8 -> 10; matrix products, arithmetic and copies ran while one was open for 1% -> 1% of each run, Pallas kernels for 1% -> 6%
where the time goes in v4:
time: 59.3 us; the launch traced here: 59.1 us
  waiting for transfers between devices  22.5 us (38%)
  starting transfers between devices  15.7 us (26%)
  Pallas kernels  15.7 us (26%)
  local copies, waits for them, and re-layouts  3.99 us (7%)
  between operations  0.78 us (1%)
    pallas_call x7, Pallas kernels, on_chip(): pl.pallas_call(kernel, out_shape=out_shape, in_specs=[pl.BlockSpec(memory...  15.7 us
    ppermute x7, waiting for transfers between devices, to_chip(): return lax.ppermute(array, 'row', bits_apart(ranks, 2 * chip))  13.4 us
    ppermute x7, starting transfers between devices, to_chip(): return lax.ppermute(array, 'row', bits_apart(ranks, 2 * chip))  9.7 us
    ppermute x3, waiting for transfers between devices, whole_system(): lax.ppermute(terms[bits], 'prime', bits_apart(primes, bits))  5.27 us
    ppermute x3, starting transfers between devices, whole_system(): lax.ppermute(terms[bits], 'prime', bits_apart(primes, bits))  4.39 us
    ppermute x6, waiting for transfers between devices, to_core(): return lax.ppermute(array, 'row', bits_apart(ranks, 1))  3.86 us
    unnamed x14, local copies, waits for them, and re-layouts  3.51 us
    ppermute x6, starting transfers between devices, to_core(): return lax.ppermute(array, 'row', bits_apart(ranks, 1))  1.6 us
  transfers between devices with their start and end apart: 16, of which 10 were waited for; matrix products, arithmetic and copies ran while one was open for 1% of the time, Pallas kernels for 6%

profile of v4, /device:TPU:0, one launch (start us, length us, event | category | flops | bytes accessed | tf_op | source)
XLA Modules:
  0.0 59.1 jit_solution(17134370445812907004)
XLA Ops:
  0.6 0.0 copy-start
  0.6 0.5 collective-permute-start
  1.2 2.6 %collective-permute-start.5 = (bf16[2560,128]{1,0:T(8,128)(2,1)}, bf16[2560,128]{1,0:T(8,128)(2,1)S(1)}, u32[]{:S(2)}, u32[]{:S(2)}) collective-permute-start(bf16[2560,128]{1,0:T(8,128)(2,1)} %bitcast.25), channel_id=1, source_target_pairs={{0,4},{1,5},{2,6},{3,7},{4,0},{5,1},{6,2},{7,3},{8,12},{9,13},{10,... | collective-permute-start | bytes 1966088 | tf_op jit(solution)/shard_map/ppermute | solution.py:215
  3.8 1.5 %collective-permute-start.4 = (bf16[2560,128]{1,0:T(8,128)(2,1)}, bf16[2560,128]{1,0:T(8,128)(2,1)S(1)}, u32[]{:S(2)}, u32[]{:S(2)}) collective-permute-start(bf16[2560,128]{1,0:T(8,128)(2,1)} %bitcast.26), channel_id=1, source_target_pairs={{0,2},{1,3},{2,0},{3,1},{4,6},{5,7},{6,4},{7,5},{8,10},{9,11},{10,... | collective-permute-start | bytes 1966088 | tf_op jit(solution)/shard_map/ppermute | solution.py:215
  5.2 0.0 copy-done
  5.3 0.1 copy.16
  5.3 0.0 copy-start.6
  5.3 0.1 broadcast_in_dim.17
  5.4 0.6 %copy-done.6 = s32[1,4,5]{2,1,0:T(4,128)S(1)} copy-done((s32[1,4,5]{2,1,0:T(4,128)S(1)}, s32[1,4,5]{2,1,0:T(4,128)}, u32[]{:S(2)}) %copy-start.6) | copy-done | bytes 104
  6.0 0.1 copy.15
  6.1 0.2 select_reduce_fusion
  6.4 0.1 copy.17
  6.5 0.1 pad_add_fusion.place_ref
  6.6 0.0 collective-permute-done.after_ref.refs_6_.refs_4_
  6.6 0.0 copy-start.3
  6.6 0.9 %copy-done.3 = bf16[1,512,128]{2,1,0:T(8,128)(2,1)S(1)} copy-done((bf16[1,512,128]{2,1,0:T(8,128)(2,1)S(1)}, bf16[1,512,128]{2,1,0:T(8,128)(2,1)}, u32[]{:S(2)}) %copy-start.3) | copy-done | bytes 131096
  7.5 0.0 copy-start.4
  7.5 0.9 %copy-done.4 = bf16[1,512,128]{2,1,0:T(8,128)(2,1)S(1)} copy-done((bf16[1,512,128]{2,1,0:T(8,128)(2,1)S(1)}, bf16[1,512,128]{2,1,0:T(8,128)(2,1)}, u32[]{:S(2)}) %copy-start.4) | copy-done | bytes 131096
  8.4 0.1 pack_pieces.1
  8.5 0.6 %collective-permute-start.1 = (bf16[656,128]{1,0:T(8,128)(2,1)S(1)}, bf16[656,128]{1,0:T(8,128)(2,1)S(1)}, u32[]{:S(2)}, u32[]{:S(2)}) collective-permute-start(bf16[656,128]{1,0:T(8,128)(2,1)S(1)} %get-tuple-element.21), channel_id=1, source_target_pairs={{0,2},{1,3},{2,0},{3,1},{4,6},{5,7},{6,4},{7,5},{8,10},{9,11},{10,... | collective-permute-start | bytes 503816 | tf_op jit(solution)/shard_map/ppermute | solution.py:215
  9.1 0.4 collective-permute-start.2
  9.5 2.6 %collective-permute-start.3 = (bf16[656,128]{1,0:T(8,128)(2,1)S(1)}, bf16[656,128]{1,0:T(8,128)(2,1)S(1)}, u32[]{:S(2)}, u32[]{:S(2)}) collective-permute-start(bf16[656,128]{1,0:T(8,128)(2,1)S(1)} %get-tuple-element.23), channel_id=1, source_target_pairs={{0,6},{1,7},{2,4},{3,5},{4,2},{5,3},{6,0},{7,1},{8,14},{9,15},{10,... | collective-permute-start | bytes 503816 | tf_op jit(solution)/shard_map/ppermute | solution.py:215
  12.0 7.5 %collective-permute-done.5.second_ref = bf16[2560,128]{1,0:T(8,128)(2,1)S(1)} collective-permute-done((bf16[2560,128]{1,0:T(8,128)(2,1)}, bf16[2560,128]{1,0:T(8,128)(2,1)S(1)}, u32[]{:S(2)}, u32[]{:S(2)}) %collective-permute-start.5) | collective-permute-done | bytes 655392 | tf_op jit(solution)/shard_map/ppermute | solution.py:215
  19.6 2.0 %collective-permute-done.4.first_ref = bf16[2560,128]{1,0:T(8,128)(2,1)S(1)} collective-permute-done((bf16[2560,128]{1,0:T(8,128)(2,1)}, bf16[2560,128]{1,0:T(8,128)(2,1)S(1)}, u32[]{:S(2)}, u32[]{:S(2)}) %collective-permute-start.4) | collective-permute-done | bytes 655392 | tf_op jit(solution)/shard_map/ppermute | solution.py:215
  21.5 1.1 %cut_halves.1 = (bf16[2560,128]{1,0:T(8,128)(2,1)S(1)}, bf16[2560,128]{1,0:T(8,128)(2,1)S(1)}, bf16[1280,128]{1,0:T(8,128)(2,1)}, bf16[1280,128]{1,0:T(8,128)(2,1)}) custom-call(bf16[2560,128]{1,0:T(8,128)(2,1)S(1)} %collective-permute-done.4.first_ref, ...), custom_call_target="tpu_custom_call", output_to_operand_aliasing={{0}: (0, {}), {1}: (1, {})} | custom-call | tf_op jit(solution)/shard_map/cut_halves/pallas_call | solution.py:164
  22.6 1.6 %collective-permute-start.10 = (bf16[1280,128]{1,0:T(8,128)(2,1)}, bf16[1280,128]{1,0:T(8,128)(2,1)}, u32[]{:S(2)}, u32[]{:S(2)}) collective-permute-start(bf16[1280,128]{1,0:T(8,128)(2,1)} %get-tuple-element.30), channel_id=1, source_target_pairs={{0,2},{1,3},{2,0},{3,1},{4,6},{5,7},{6,4},{7,5},{8,10},{9,11},{10,... | collective-permute-start | bytes 983048 | tf_op jit(solution)/shard_map/ppermute | solution.py:215
  24.2 0.5 collective-permute-start.9
  24.7 0.5 collective-permute-done.1.refs_1_
  25.1 0.0 collective-permute-start.7
  25.1 0.0 collective-permute-done.2.refs_2_
  25.1 0.5 collective-permute-start.8
  25.7 2.6 %collective-permute-done.3.refs_3_ = bf16[656,128]{1,0:T(8,128)(2,1)S(1)} collective-permute-done((bf16[656,128]{1,0:T(8,128)(2,1)S(1)}, bf16[656,128]{1,0:T(8,128)(2,1)S(1)}, u32[]{:S(2)}, u32[]{:S(2)}) %collective-permute-start.3) | collective-permute-done | bytes 167968 | tf_op jit(solution)/shard_map/ppermute | solution.py:215
  28.3 0.1 collective-permute-start.6
  28.5 2.1 %collective-permute-done.6.refs_4_ = bf16[2624,128]{1,0:T(8,128)(2,1)S(1)} collective-permute-done((bf16[2624,128]{1,0:T(8,128)(2,1)S(1)}, bf16[2624,128]{1,0:T(8,128)(2,1)S(1)}, u32[]{:S(2)}, u32[]{:S(2)}) %collective-permute-start.6) | collective-permute-done | bytes 671776 | tf_op jit(solution)/shard_map/ppermute | solution.py:218
  30.5 0.1 reshape.18.columns_ref
  30.7 0.0 collective-permute-done.7.refs_8_.refs_6_
  30.7 0.0 collective-permute-done.8.refs_10_.refs_8_
  30.7 0.0 copy-start.1
  30.7 1.1 %copy-done.1 = bf16[1,4,5,128,128]{4,3,2,1,0:T(8,128)(2,1)S(1)} copy-done((bf16[1,4,5,128,128]{4,3,2,1,0:T(8,128)(2,1)S(1)}, bf16[1,4,5,128,128]{4,3,2,1,0:T(8,128)(2,1)}, u32[]{:S(2)}) %copy-start.1) | copy-done | bytes 655384
  31.8 2.6 %first_step.1 = (bf16[32,128,128]{2,1,0:T(8,128)(2,1)S(1)}, bf16[24,128,128]{2,1,0:T(8,128)(2,1)S(1)}, bf16[8,64,128]{2,1,0:T(8,128)(2,1)S(1)}) custom-call(s32[160]{0:T(256)S(1)} %reshape.18.columns_ref, s32[2]{0:T(128)S(1)} %pad_add_fusion.place_ref, bf16[656,128]{1,0:T(8,128)(2,1)S(1)} %get-tuple-element.20.after_ref.refs_0_, ...), custom_call_target="tpu_custom_call" | custom-call | flops 503316480 | bytes 5275648 | tf_op jit(solution)/shard_map/first_step/pallas_call | solution.py:164
  34.4 0.8 %collective-permute-done.10.refs_1_ = bf16[1280,128]{1,0:T(8,128)(2,1)} collective-permute-done((bf16[1280,128]{1,0:T(8,128)(2,1)}, bf16[1280,128]{1,0:T(8,128)(2,1)}, u32[]{:S(2)}, u32[]{:S(2)}) %collective-permute-start.10) | collective-permute-done | bytes 327712 | tf_op jit(solution)/shard_map/ppermute | solution.py:215
  35.1 0.0 collective-permute-done.9.refs_0_
  35.1 0.0 copy-start.2
  35.1 0.0 collective-permute-start.11
  35.2 0.5 collective-permute-start.12
  35.7 1.3 %collective-permute-done.11.refs_11_ = bf16[1280,128]{1,0:T(8,128)(2,1)S(1)} collective-permute-done((bf16[1280,128]{1,0:T(8,128)(2,1)}, bf16[1280,128]{1,0:T(8,128)(2,1)S(1)}, u32[]{:S(2)}, u32[]{:S(2)}) %collective-permute-start.11) | collective-permute-done | bytes 327712 | tf_op jit(solution)/shard_map/ppermute | solution.py:218
  37.0 0.5 collective-permute-done.12.refs_12_
  37.5 0.0 copy-done.2
  37.5 10.6 %all_steps.1 = (f32[24,128]{1,0:T(8,128)S(1)}, f32[24,128]{1,0:T(8,128)S(1)}, f32[24,128]{1,0:T(8,128)S(1)}, f32[24,128]{1,0:T(8,128)S(1)}, bf16[512,128]{1,0:T(8,128)(2,1)}) custom-call(s32[160]{0:T(256)S(1)} %reshape.18.columns_ref, s32[2]{0:T(128)S(1)} %pad_add_fusion.place_ref, bf16[32,128,128]{2,1,0:T(8,128)(2,1)S(1)} %get-tuple-element.27.refs_0_, ...), custom_call_target="tpu_custom_call" | custom-call | flops 4026531840 | bytes 7208960 | tf_op jit(solution)/shard_map/all_steps/pallas_call | solution.py:164
  48.0 1.6 %collective-permute-start.13 = (f32[24,128]{1,0:T(8,128)S(1)}, f32[24,128]{1,0:T(8,128)S(1)}, u32[]{:S(2)}, u32[]{:S(2)}) collective-permute-start(f32[24,128]{1,0:T(8,128)S(1)} %get-tuple-element.34), channel_id=1, source_target_pairs={{0,8},{8,0},{16,24},{24,16},{1,9},{9,1},{17,25},{25,17},{2,10},{10... | collective-permute-start | bytes 36872 | tf_op jit(solution)/shard_map/ppermute | solution.py:291
  49.6 0.0 copy-start.5
  49.6 2.6 %collective-permute-start.14 = (f32[24,128]{1,0:T(8,128)S(1)}, f32[24,128]{1,0:T(8,128)S(1)}, u32[]{:S(2)}, u32[]{:S(2)}) collective-permute-start(f32[24,128]{1,0:T(8,128)S(1)} %get-tuple-element.35), channel_id=1, source_target_pairs={{0,16},{8,24},{16,0},{24,8},{1,17},{9,25},{17,1},{25,9},{2,18},{10... | collective-permute-start | bytes 36872 | tf_op jit(solution)/shard_map/ppermute | solution.py:291
  52.2 0.2 collective-permute-start.15
  52.4 0.0 collective-permute-done.13.refs_1_
  52.4 1.8 %collective-permute-done.14.refs_2_ = f32[24,128]{1,0:T(8,128)S(1)} collective-permute-done((f32[24,128]{1,0:T(8,128)S(1)}, f32[24,128]{1,0:T(8,128)S(1)}, u32[]{:S(2)}, u32[]{:S(2)}) %collective-permute-start.14) | collective-permute-done | bytes 12320 | tf_op jit(solution)/shard_map/ppermute | solution.py:291
  54.2 3.5 %collective-permute-done.15.refs_3_ = f32[24,128]{1,0:T(8,128)S(1)} collective-permute-done((f32[24,128]{1,0:T(8,128)S(1)}, f32[24,128]{1,0:T(8,128)S(1)}, u32[]{:S(2)}, u32[]{:S(2)}) %collective-permute-start.15) | collective-permute-done | bytes 12320 | tf_op jit(solution)/shard_map/ppermute | solution.py:291
  57.7 0.0 copy-done.5
  57.7 1.4 %mix_terms.1 = f32[4,6,16,32]{3,2,1,0:T(8,128)} custom-call(s32[2]{0:T(128)S(1)} %pad_add_fusion.place_ref, f32[4,4]{1,0:T(4,128)S(1)} %copy-done.5, f32[24,128]{1,0:T(8,128)S(1)} %get-tuple-element.33.refs_0_, f32[24,128]{1,0:T(8,128)S(1)} %collective-permute-done.13.refs_1_, f32[24,128]{1,0:T(8,128)S(1)} %collective-permute-done.14.refs_2_, ...), custom_call_target="tpu_custom_call" | custom-call | bytes 49152 | tf_op jit(solution)/shard_map/mix_terms/pallas_call | solution.py:164
  (13 shorter events, 0.1 us)
Async XLA Ops:
  0.6 4.6 %copy-start = (s32[1,8,8,2]{2,3,1,0:T(2,128)S(1)}, s32[1,8,8,2]{2,3,1,0:T(2,128)}, u32[]{:S(2)}) copy-start(s32[1,8,8,2]{2,3,1,0:T(2,128)} %param.8) | copy-start | bytes 1540
  0.6 5.9 %collective-permute-start = (bf16[2560,128]{1,0:T(8,128)(2,1)}, bf16[2560,128]{1,0:T(8,128)(2,1)S(1)}, u32[]{:S(2)}, u32[]{:S(2)}) collective-permute-start(bf16[2560,128]{1,0:T(8,128)(2,1)} %bitcast.24), channel_id=1, source_target_pairs={{0,1},{1,0},{2,3},{3,2},{4,5},{5,4},{6,7},{7,6},{8,9},{9,8},{10,11... | collective-permute-start | bytes 1966088 | tf_op jit(solution)/shard_map/ppermute | solution.py:218
  1.2 18.4 %collective-permute-start.5 = (bf16[2560,128]{1,0:T(8,128)(2,1)}, bf16[2560,128]{1,0:T(8,128)(2,1)S(1)}, u32[]{:S(2)}, u32[]{:S(2)}) collective-permute-start(bf16[2560,128]{1,0:T(8,128)(2,1)} %bitcast.25), channel_id=1, source_target_pairs={{0,4},{1,5},{2,6},{3,7},{4,0},{5,1},{6,2},{7,3},{8,12},{9,13},{10,... | collective-permute-start | bytes 1966088 | tf_op jit(solution)/shard_map/ppermute | solution.py:215
  3.8 17.8 %collective-permute-start.4 = (bf16[2560,128]{1,0:T(8,128)(2,1)}, bf16[2560,128]{1,0:T(8,128)(2,1)S(1)}, u32[]{:S(2)}, u32[]{:S(2)}) collective-permute-start(bf16[2560,128]{1,0:T(8,128)(2,1)} %bitcast.26), channel_id=1, source_target_pairs={{0,2},{1,3},{2,0},{3,1},{4,6},{5,7},{6,4},{7,5},{8,10},{9,11},{10,... | collective-permute-start | bytes 1966088 | tf_op jit(solution)/shard_map/ppermute | solution.py:215
  5.3 0.7 %copy-start.6 = (s32[1,4,5]{2,1,0:T(4,128)S(1)}, s32[1,4,5]{2,1,0:T(4,128)}, u32[]{:S(2)}) copy-start(s32[1,4,5]{2,1,0:T(4,128)} %param.7) | copy-start | bytes 244
  6.6 0.9 %copy-start.3 = (bf16[1,512,128]{2,1,0:T(8,128)(2,1)S(1)}, bf16[1,512,128]{2,1,0:T(8,128)(2,1)}, u32[]{:S(2)}) copy-start(bf16[1,512,128]{2,1,0:T(8,128)(2,1)} %param.9) | copy-start | bytes 393220
  7.5 0.9 %copy-start.4 = (bf16[1,512,128]{2,1,0:T(8,128)(2,1)S(1)}, bf16[1,512,128]{2,1,0:T(8,128)(2,1)}, u32[]{:S(2)}) copy-start(bf16[1,512,128]{2,1,0:T(8,128)(2,1)} %param.10) | copy-start | bytes 393220
  8.5 16.7 %collective-permute-start.1 = (bf16[656,128]{1,0:T(8,128)(2,1)S(1)}, bf16[656,128]{1,0:T(8,128)(2,1)S(1)}, u32[]{:S(2)}, u32[]{:S(2)}) collective-permute-start(bf16[656,128]{1,0:T(8,128)(2,1)S(1)} %get-tuple-element.21), channel_id=1, source_target_pairs={{0,2},{1,3},{2,0},{3,1},{4,6},{5,7},{6,4},{7,5},{8,10},{9,11},{10,... | collective-permute-start | bytes 503816 | tf_op jit(solution)/shard_map/ppermute | solution.py:215
  9.1 16.1 %collective-permute-start.2 = (bf16[656,128]{1,0:T(8,128)(2,1)S(1)}, bf16[656,128]{1,0:T(8,128)(2,1)S(1)}, u32[]{:S(2)}, u32[]{:S(2)}) collective-permute-start(bf16[656,128]{1,0:T(8,128)(2,1)S(1)} %get-tuple-element.22), channel_id=1, source_target_pairs={{0,4},{1,5},{2,6},{3,7},{4,0},{5,1},{6,2},{7,3},{8,12},{9,13},{10,... | collective-permute-start | bytes 503816 | tf_op jit(solution)/shard_map/ppermute | solution.py:215
  9.5 18.8 %collective-permute-start.3 = (bf16[656,128]{1,0:T(8,128)(2,1)S(1)}, bf16[656,128]{1,0:T(8,128)(2,1)S(1)}, u32[]{:S(2)}, u32[]{:S(2)}) collective-permute-start(bf16[656,128]{1,0:T(8,128)(2,1)S(1)} %get-tuple-element.23), channel_id=1, source_target_pairs={{0,6},{1,7},{2,4},{3,5},{4,2},{5,3},{6,0},{7,1},{8,14},{9,15},{10,... | collective-permute-start | bytes 503816 | tf_op jit(solution)/shard_map/ppermute | solution.py:215
  22.6 12.5 %collective-permute-start.10 = (bf16[1280,128]{1,0:T(8,128)(2,1)}, bf16[1280,128]{1,0:T(8,128)(2,1)}, u32[]{:S(2)}, u32[]{:S(2)}) collective-permute-start(bf16[1280,128]{1,0:T(8,128)(2,1)} %get-tuple-element.30), channel_id=1, source_target_pairs={{0,2},{1,3},{2,0},{3,1},{4,6},{5,7},{6,4},{7,5},{8,10},{9,11},{10,... | collective-permute-start | bytes 983048 | tf_op jit(solution)/shard_map/ppermute | solution.py:215
  24.2 11.0 %collective-permute-start.9 = (bf16[1280,128]{1,0:T(8,128)(2,1)}, bf16[1280,128]{1,0:T(8,128)(2,1)}, u32[]{:S(2)}, u32[]{:S(2)}) collective-permute-start(bf16[1280,128]{1,0:T(8,128)(2,1)} %get-tuple-element.24.refs_4_), channel_id=1, source_target_pairs={{0,4},{1,5},{2,6},{3,7},{4,0},{5,1},{6,2},{7,3},{8,12},{9,13},{10,... | collective-permute-start | bytes 983048 | tf_op jit(solution)/shard_map/ppermute | solution.py:215
  25.1 5.5 %collective-permute-start.7 = (bf16[2560,128]{1,0:T(8,128)(2,1)S(1)}, bf16[2560,128]{1,0:T(8,128)(2,1)}, u32[]{:S(2)}, u32[]{:S(2)}) collective-permute-start(bf16[2560,128]{1,0:T(8,128)(2,1)S(1)} %get-tuple-element.25.refs_7_.refs_5_), channel_id=1, source_target_pairs={{0,1},{1,0},{2,3},{3,2},{4,5},{5,4},{6,7},{7,6},{8,9},{9,8},{10,11... | collective-permute-start | bytes 1966088 | tf_op jit(solution)/shard_map/ppermute | solution.py:218
  25.1 5.5 %collective-permute-start.8 = (bf16[2560,128]{1,0:T(8,128)(2,1)S(1)}, bf16[2560,128]{1,0:T(8,128)(2,1)}, u32[]{:S(2)}, u32[]{:S(2)}) collective-permute-start(bf16[2560,128]{1,0:T(8,128)(2,1)S(1)} %get-tuple-element.26.refs_9_.refs_7_), channel_id=1, source_target_pairs={{0,1},{1,0},{2,3},{3,2},{4,5},{5,4},{6,7},{7,6},{8,9},{9,8},{10,11... | collective-permute-start | bytes 1966088 | tf_op jit(solution)/shard_map/ppermute | solution.py:218
  28.3 2.2 %collective-permute-start.6 = (bf16[2624,128]{1,0:T(8,128)(2,1)S(1)}, bf16[2624,128]{1,0:T(8,128)(2,1)S(1)}, u32[]{:S(2)}, u32[]{:S(2)}) collective-permute-start(bf16[2624,128]{1,0:T(8,128)(2,1)S(1)} %join_pieces.1), channel_id=1, source_target_pairs={{0,1},{1,0},{2,3},{3,2},{4,5},{5,4},{6,7},{7,6},{8,9},{9,8},{10,11... | collective-permute-start | bytes 2015240 | tf_op jit(solution)/shard_map/ppermute | solution.py:218
  30.7 1.1 %copy-start.1 = (bf16[1,4,5,128,128]{4,3,2,1,0:T(8,128)(2,1)S(1)}, bf16[1,4,5,128,128]{4,3,2,1,0:T(8,128)(2,1)}, u32[]{:S(2)}) copy-start(bf16[1,4,5,128,128]{4,3,2,1,0:T(8,128)(2,1)} %param.6) | copy-start | bytes 1966084
  35.1 2.3 %copy-start.2 = (bf16[1,4,5,128,128]{4,3,2,1,0:T(8,128)(2,1)S(1)}, bf16[1,4,5,128,128]{4,3,2,1,0:T(8,128)(2,1)}, u32[]{:S(2)}) copy-start(bf16[1,4,5,128,128]{4,3,2,1,0:T(8,128)(2,1)} %param.6) | copy-start | bytes 1966084
  35.1 1.8 %collective-permute-start.11 = (bf16[1280,128]{1,0:T(8,128)(2,1)}, bf16[1280,128]{1,0:T(8,128)(2,1)S(1)}, u32[]{:S(2)}, u32[]{:S(2)}) collective-permute-start(bf16[1280,128]{1,0:T(8,128)(2,1)} %get-tuple-element.31.refs_9_), channel_id=1, source_target_pairs={{0,1},{1,0},{2,3},{3,2},{4,5},{5,4},{6,7},{7,6},{8,9},{9,8},{10,11... | collective-permute-start | bytes 983048 | tf_op jit(solution)/shard_map/ppermute | solution.py:218
  35.2 2.3 %collective-permute-start.12 = (bf16[1280,128]{1,0:T(8,128)(2,1)}, bf16[1280,128]{1,0:T(8,128)(2,1)S(1)}, u32[]{:S(2)}, u32[]{:S(2)}) collective-permute-start(bf16[1280,128]{1,0:T(8,128)(2,1)} %get-tuple-element.32.refs_10_), channel_id=1, source_target_pairs={{0,1},{1,0},{2,3},{3,2},{4,5},{5,4},{6,7},{7,6},{8,9},{9,8},{10,11... | collective-permute-start | bytes 983048 | tf_op jit(solution)/shard_map/ppermute | solution.py:218
  48.0 4.4 %collective-permute-start.13 = (f32[24,128]{1,0:T(8,128)S(1)}, f32[24,128]{1,0:T(8,128)S(1)}, u32[]{:S(2)}, u32[]{:S(2)}) collective-permute-start(f32[24,128]{1,0:T(8,128)S(1)} %get-tuple-element.34), channel_id=1, source_target_pairs={{0,8},{8,0},{16,24},{24,16},{1,9},{9,1},{17,25},{25,17},{2,10},{10... | collective-permute-start | bytes 36872 | tf_op jit(solution)/shard_map/ppermute | solution.py:291
  49.6 8.1 %copy-start.5 = (f32[4,4]{1,0:T(4,128)S(1)}, f32[4,4]{1,0:T(4,128)}, u32[]{:S(2)}) copy-start(f32[4,4]{1,0:T(4,128)} %weights_ref.1) | copy-start | bytes 196
  49.6 4.6 %collective-permute-start.14 = (f32[24,128]{1,0:T(8,128)S(1)}, f32[24,128]{1,0:T(8,128)S(1)}, u32[]{:S(2)}, u32[]{:S(2)}) collective-permute-start(f32[24,128]{1,0:T(8,128)S(1)} %get-tuple-element.35), channel_id=1, source_target_pairs={{0,16},{8,24},{16,0},{24,8},{1,17},{9,25},{17,1},{25,9},{2,18},{10... | collective-permute-start | bytes 36872 | tf_op jit(solution)/shard_map/ppermute | solution.py:291
  52.2 5.5 %collective-permute-start.15 = (f32[24,128]{1,0:T(8,128)S(1)}, f32[24,128]{1,0:T(8,128)S(1)}, u32[]{:S(2)}, u32[]{:S(2)}) collective-permute-start(f32[24,128]{1,0:T(8,128)S(1)} %get-tuple-element.36), channel_id=1, source_target_pairs={{0,24},{8,16},{16,8},{24,0},{1,25},{9,17},{17,9},{25,1},{2,26},{10... | collective-permute-start | bytes 36872 | tf_op jit(solution)/shard_map/ppermute | solution.py:291

commit v5 on v4

--- a/solution.py
+++ b/solution.py
@@ -90,7 +90,7 @@
 
 def all_steps(ranks, primes, stored, columns_ref, place_ref, *refs):
     (start, part, projectors), refs, panels = refs[:3], refs[3 : 1 - ITERS], refs[1 - ITERS :]
-    refs, terms_refs, last_ref, terms = refs[: -primes - 2], refs[-primes - 2 : -2], refs[-2], refs[-1]
+    refs, terms_refs, (last_ref, terms, result, sent) = refs[: -primes - 4], refs[-primes - 4 : -4], refs[-4:]
     count, size, width = start.shape
     blocks = count // ranks
     rows = refs[-1].shape[0]
@@ -116,7 +116,9 @@
                 known = step == 0 and given < part.shape[0]
                 new[first + row] = part[given] if known else apply(old, distance, row)
     for row in range(blocks):
-        last_ref[row * size : (row + 1) * size] = apply(panels[-1], 0, row)
+        result[row * size : (row + 1) * size] = apply(panels[-1], 0, row)
+    leaving = pltpu.make_async_copy(result, last_ref, sent.at[0])
+    leaving.start()
 
     held = width // ranks
     parts = []
@@ -144,6 +146,7 @@
         )
     for bits in range(primes):
         terms_refs[bits][...] = terms[place_ref[0] ^ bits]
+    leaving.wait()
 
 
 def mix_terms(place_ref, weights_ref, *refs):
@@ -156,11 +159,12 @@
         out_ref[prime] = jnp.concatenate(groups, axis=0).reshape(steps, held, part)
 
 
-def on_chip(kernel, out_shape, smem, vmem, before=(), after=(), aliases=None, scratch=(), flops=0, name=None):
+def on_chip(kernel, out_shape, smem, vmem, before=(), after=(), aliases=None, far_outs=(), scratch=(), flops=0, name=None):
     aliases = aliases or {}
     spaces = [pl.ANY] * len(before) + [pltpu.SMEM] * len(smem) + [pltpu.VMEM] * len(vmem) + [pl.ANY] * len(after)
     shapes, tree = jax.tree.flatten(out_shape)
-    outs = [pl.BlockSpec(memory_space=pl.ANY if at in aliases.values() else pltpu.VMEM) for at in range(len(shapes))]
+    far_outs = {*aliases.values(), *far_outs}
+    outs = [pl.BlockSpec(memory_space=pl.ANY if at in far_outs else pltpu.VMEM) for at in range(len(shapes))]
     return pl.pallas_call(
         kernel,
         out_shape=out_shape,
@@ -282,7 +286,12 @@
         [piece] * primes + [jax.ShapeDtypeStruct((blocks * size, width), jnp.bfloat16)],
         [columns, place],
         [*given, *whole, *halves],
-        scratch=[pltpu.VMEM((primes, *piece.shape), jnp.float32)]
+        far_outs=[primes],
+        scratch=[
+            pltpu.VMEM((primes, *piece.shape), jnp.float32),
+            pltpu.VMEM((blocks * size, width), jnp.bfloat16),
+            pltpu.SemaphoreType.DMA((1,)),
+        ]
         + [pltpu.VMEM(shape, jnp.bfloat16)] * (ITERS - 1),
         flops=2 * ITERS * ranks * tiles.size * width,
         name="all_steps",

time: 59.3 us -> 59.2 us (level)
  no operation moved by 1% of the time
where the time goes in v5:
time: 59.2 us; the launch traced here: 59 us
  waiting for transfers between devices  22.5 us (38%)
  starting transfers between devices  15.8 us (27%)
  Pallas kernels  15.6 us (26%)
  local copies, waits for them, and re-layouts  3.99 us (7%)
  between operations  0.79 us (1%)
    pallas_call x7, Pallas kernels, on_chip(): pl.pallas_call(kernel, out_shape=out_shape, in_specs=[pl.BlockSpec(memory...  15.6 us
    ppermute x7, waiting for transfers between devices, to_chip(): return lax.ppermute(array, 'row', bits_apart(ranks, 2 * chip))  13.4 us
    ppermute x7, starting transfers between devices, to_chip(): return lax.ppermute(array, 'row', bits_apart(ranks, 2 * chip))  9.7 us
    ppermute x3, waiting for transfers between devices, whole_system(): lax.ppermute(terms[bits], 'prime', bits_apart(primes, bits))  5.27 us
    ppermute x3, starting transfers between devices, whole_system(): lax.ppermute(terms[bits], 'prime', bits_apart(primes, bits))  4.45 us
    ppermute x6, waiting for transfers between devices, to_core(): return lax.ppermute(array, 'row', bits_apart(ranks, 1))  3.86 us
    unnamed x14, local copies, waits for them, and re-layouts  3.51 us
    ppermute x6, starting transfers between devices, to_core(): return lax.ppermute(array, 'row', bits_apart(ranks, 1))  1.6 us
  transfers between devices with their start and end apart: 16, of which 10 were waited for; matrix products, arithmetic and copies ran while one was open for 1% of the time, Pallas kernels for 6%

profile of v5, /device:TPU:0, one launch (start us, length us, event | category | flops | bytes accessed | tf_op | source)
XLA Modules:
  0.0 59.0 jit_solution(13546317807406937732)
XLA Ops:
  0.6 0.0 copy-start
  0.6 0.5 collective-permute-start
  1.2 2.6 %collective-permute-start.5 = (bf16[2560,128]{1,0:T(8,128)(2,1)}, bf16[2560,128]{1,0:T(8,128)(2,1)S(1)}, u32[]{:S(2)}, u32[]{:S(2)}) collective-permute-start(bf16[2560,128]{1,0:T(8,128)(2,1)} %bitcast.25), channel_id=1, source_target_pairs={{0,4},{1,5},{2,6},{3,7},{4,0},{5,1},{6,2},{7,3},{8,12},{9,13},{10,... | collective-permute-start | bytes 1966088 | tf_op jit(solution)/shard_map/ppermute | solution.py:219
  3.8 1.5 %collective-permute-start.4 = (bf16[2560,128]{1,0:T(8,128)(2,1)}, bf16[2560,128]{1,0:T(8,128)(2,1)S(1)}, u32[]{:S(2)}, u32[]{:S(2)}) collective-permute-start(bf16[2560,128]{1,0:T(8,128)(2,1)} %bitcast.26), channel_id=1, source_target_pairs={{0,2},{1,3},{2,0},{3,1},{4,6},{5,7},{6,4},{7,5},{8,10},{9,11},{10,... | collective-permute-start | bytes 1966088 | tf_op jit(solution)/shard_map/ppermute | solution.py:219
  5.2 0.0 copy-done
  5.3 0.1 copy.16
  5.3 0.0 copy-start.6
  5.3 0.1 broadcast_in_dim.17
  5.4 0.6 %copy-done.6 = s32[1,4,5]{2,1,0:T(4,128)S(1)} copy-done((s32[1,4,5]{2,1,0:T(4,128)S(1)}, s32[1,4,5]{2,1,0:T(4,128)}, u32[]{:S(2)}) %copy-start.6) | copy-done | bytes 104
  6.0 0.1 copy.15
  6.1 0.2 select_reduce_fusion
  6.4 0.1 copy.17
  6.5 0.1 pad_add_fusion.place_ref
  6.6 0.0 collective-permute-done.after_ref.refs_6_.refs_4_
  6.6 0.0 copy-start.3
  6.6 0.9 %copy-done.3 = bf16[1,512,128]{2,1,0:T(8,128)(2,1)S(1)} copy-done((bf16[1,512,128]{2,1,0:T(8,128)(2,1)S(1)}, bf16[1,512,128]{2,1,0:T(8,128)(2,1)}, u32[]{:S(2)}) %copy-start.3) | copy-done | bytes 131096
  7.5 0.0 copy-start.4
  7.5 0.9 %copy-done.4 = bf16[1,512,128]{2,1,0:T(8,128)(2,1)S(1)} copy-done((bf16[1,512,128]{2,1,0:T(8,128)(2,1)S(1)}, bf16[1,512,128]{2,1,0:T(8,128)(2,1)}, u32[]{:S(2)}) %copy-start.4) | copy-done | bytes 131096
  8.4 0.1 pack_pieces.1
  8.5 0.6 %collective-permute-start.1 = (bf16[656,128]{1,0:T(8,128)(2,1)S(1)}, bf16[656,128]{1,0:T(8,128)(2,1)S(1)}, u32[]{:S(2)}, u32[]{:S(2)}) collective-permute-start(bf16[656,128]{1,0:T(8,128)(2,1)S(1)} %get-tuple-element.21), channel_id=1, source_target_pairs={{0,2},{1,3},{2,0},{3,1},{4,6},{5,7},{6,4},{7,5},{8,10},{9,11},{10,... | collective-permute-start | bytes 503816 | tf_op jit(solution)/shard_map/ppermute | solution.py:219
  9.1 0.4 collective-permute-start.2
  9.5 2.6 %collective-permute-start.3 = (bf16[656,128]{1,0:T(8,128)(2,1)S(1)}, bf16[656,128]{1,0:T(8,128)(2,1)S(1)}, u32[]{:S(2)}, u32[]{:S(2)}) collective-permute-start(bf16[656,128]{1,0:T(8,128)(2,1)S(1)} %get-tuple-element.23), channel_id=1, source_target_pairs={{0,6},{1,7},{2,4},{3,5},{4,2},{5,3},{6,0},{7,1},{8,14},{9,15},{10,... | collective-permute-start | bytes 503816 | tf_op jit(solution)/shard_map/ppermute | solution.py:219
  12.0 7.5 %collective-permute-done.5.second_ref = bf16[2560,128]{1,0:T(8,128)(2,1)S(1)} collective-permute-done((bf16[2560,128]{1,0:T(8,128)(2,1)}, bf16[2560,128]{1,0:T(8,128)(2,1)S(1)}, u32[]{:S(2)}, u32[]{:S(2)}) %collective-permute-start.5) | collective-permute-done | bytes 655392 | tf_op jit(solution)/shard_map/ppermute | solution.py:219
  19.6 2.0 %collective-permute-done.4.first_ref = bf16[2560,128]{1,0:T(8,128)(2,1)S(1)} collective-permute-done((bf16[2560,128]{1,0:T(8,128)(2,1)}, bf16[2560,128]{1,0:T(8,128)(2,1)S(1)}, u32[]{:S(2)}, u32[]{:S(2)}) %collective-permute-start.4) | collective-permute-done | bytes 655392 | tf_op jit(solution)/shard_map/ppermute | solution.py:219
  21.5 1.1 %cut_halves.1 = (bf16[2560,128]{1,0:T(8,128)(2,1)S(1)}, bf16[2560,128]{1,0:T(8,128)(2,1)S(1)}, bf16[1280,128]{1,0:T(8,128)(2,1)}, bf16[1280,128]{1,0:T(8,128)(2,1)}) custom-call(bf16[2560,128]{1,0:T(8,128)(2,1)S(1)} %collective-permute-done.4.first_ref, ...), custom_call_target="tpu_custom_call", output_to_operand_aliasing={{0}: (0, {}), {1}: (1, {})} | custom-call | tf_op jit(solution)/shard_map/cut_halves/pallas_call | solution.py:168
  22.6 1.6 %collective-permute-start.10 = (bf16[1280,128]{1,0:T(8,128)(2,1)}, bf16[1280,128]{1,0:T(8,128)(2,1)}, u32[]{:S(2)}, u32[]{:S(2)}) collective-permute-start(bf16[1280,128]{1,0:T(8,128)(2,1)} %get-tuple-element.30), channel_id=1, source_target_pairs={{0,2},{1,3},{2,0},{3,1},{4,6},{5,7},{6,4},{7,5},{8,10},{9,11},{10,... | collective-permute-start | bytes 983048 | tf_op jit(solution)/shard_map/ppermute | solution.py:219
  24.2 0.5 collective-permute-start.9
  24.7 0.5 collective-permute-done.1.refs_1_
  25.1 0.0 collective-permute-start.7
  25.1 0.0 collective-permute-done.2.refs_2_
  25.1 0.5 collective-permute-start.8
  25.7 2.6 %collective-permute-done.3.refs_3_ = bf16[656,128]{1,0:T(8,128)(2,1)S(1)} collective-permute-done((bf16[656,128]{1,0:T(8,128)(2,1)S(1)}, bf16[656,128]{1,0:T(8,128)(2,1)S(1)}, u32[]{:S(2)}, u32[]{:S(2)}) %collective-permute-start.3) | collective-permute-done | bytes 167968 | tf_op jit(solution)/shard_map/ppermute | solution.py:219
  28.3 0.1 collective-permute-start.6
  28.5 2.1 %collective-permute-done.6.refs_4_ = bf16[2624,128]{1,0:T(8,128)(2,1)S(1)} collective-permute-done((bf16[2624,128]{1,0:T(8,128)(2,1)S(1)}, bf16[2624,128]{1,0:T(8,128)(2,1)S(1)}, u32[]{:S(2)}, u32[]{:S(2)}) %collective-permute-start.6) | collective-permute-done | bytes 671776 | tf_op jit(solution)/shard_map/ppermute | solution.py:222
  30.5 0.1 reshape.18.columns_ref
  30.7 0.0 collective-permute-done.7.refs_8_.refs_6_
  30.7 0.0 collective-permute-done.8.refs_10_.refs_8_
  30.7 0.0 copy-start.1
  30.7 1.1 %copy-done.1 = bf16[1,4,5,128,128]{4,3,2,1,0:T(8,128)(2,1)S(1)} copy-done((bf16[1,4,5,128,128]{4,3,2,1,0:T(8,128)(2,1)S(1)}, bf16[1,4,5,128,128]{4,3,2,1,0:T(8,128)(2,1)}, u32[]{:S(2)}) %copy-start.1) | copy-done | bytes 655384
  31.8 2.6 %first_step.1 = (bf16[32,128,128]{2,1,0:T(8,128)(2,1)S(1)}, bf16[24,128,128]{2,1,0:T(8,128)(2,1)S(1)}, bf16[8,64,128]{2,1,0:T(8,128)(2,1)S(1)}) custom-call(s32[160]{0:T(256)S(1)} %reshape.18.columns_ref, s32[2]{0:T(128)S(1)} %pad_add_fusion.place_ref, bf16[656,128]{1,0:T(8,128)(2,1)S(1)} %get-tuple-element.20.after_ref.refs_0_, ...), custom_call_target="tpu_custom_call" | custom-call | flops 503316480 | bytes 5275648 | tf_op jit(solution)/shard_map/first_step/pallas_call | solution.py:168
  34.4 0.8 %collective-permute-done.10.refs_1_ = bf16[1280,128]{1,0:T(8,128)(2,1)} collective-permute-done((bf16[1280,128]{1,0:T(8,128)(2,1)}, bf16[1280,128]{1,0:T(8,128)(2,1)}, u32[]{:S(2)}, u32[]{:S(2)}) %collective-permute-start.10) | collective-permute-done | bytes 327712 | tf_op jit(solution)/shard_map/ppermute | solution.py:219
  35.1 0.0 collective-permute-done.9.refs_0_
  35.1 0.0 copy-start.2
  35.1 0.0 collective-permute-start.11
  35.2 0.5 collective-permute-start.12
  35.7 1.3 %collective-permute-done.11.refs_11_ = bf16[1280,128]{1,0:T(8,128)(2,1)S(1)} collective-permute-done((bf16[1280,128]{1,0:T(8,128)(2,1)}, bf16[1280,128]{1,0:T(8,128)(2,1)S(1)}, u32[]{:S(2)}, u32[]{:S(2)}) %collective-permute-start.11) | collective-permute-done | bytes 327712 | tf_op jit(solution)/shard_map/ppermute | solution.py:222
  37.0 0.5 collective-permute-done.12.refs_12_
  37.5 0.0 copy-done.2
  37.5 10.4 %all_steps.1 = (f32[24,128]{1,0:T(8,128)S(1)}, f32[24,128]{1,0:T(8,128)S(1)}, f32[24,128]{1,0:T(8,128)S(1)}, f32[24,128]{1,0:T(8,128)S(1)}, bf16[512,128]{1,0:T(8,128)(2,1)}) custom-call(s32[160]{0:T(256)S(1)} %reshape.18.columns_ref, s32[2]{0:T(128)S(1)} %pad_add_fusion.place_ref, bf16[32,128,128]{2,1,0:T(8,128)(2,1)S(1)} %get-tuple-element.27.refs_0_, ...), custom_call_target="tpu_custom_call" | custom-call | flops 4026531840 | bytes 7208960 | tf_op jit(solution)/shard_map/all_steps/pallas_call | solution.py:168
  47.9 1.6 %collective-permute-start.13 = (f32[24,128]{1,0:T(8,128)S(1)}, f32[24,128]{1,0:T(8,128)S(1)}, u32[]{:S(2)}, u32[]{:S(2)}) collective-permute-start(f32[24,128]{1,0:T(8,128)S(1)} %get-tuple-element.34), channel_id=1, source_target_pairs={{0,8},{8,0},{16,24},{24,16},{1,9},{9,1},{17,25},{25,17},{2,10},{10... | collective-permute-start | bytes 36872 | tf_op jit(solution)/shard_map/ppermute | solution.py:300
  49.5 0.0 copy-start.5
  49.5 2.6 %collective-permute-start.14 = (f32[24,128]{1,0:T(8,128)S(1)}, f32[24,128]{1,0:T(8,128)S(1)}, u32[]{:S(2)}, u32[]{:S(2)}) collective-permute-start(f32[24,128]{1,0:T(8,128)S(1)} %get-tuple-element.35), channel_id=1, source_target_pairs={{0,16},{8,24},{16,0},{24,8},{1,17},{9,25},{17,1},{25,9},{2,18},{10... | collective-permute-start | bytes 36872 | tf_op jit(solution)/shard_map/ppermute | solution.py:300
  52.1 0.2 collective-permute-start.15
  52.3 0.0 collective-permute-done.13.refs_1_
  52.3 1.8 %collective-permute-done.14.refs_2_ = f32[24,128]{1,0:T(8,128)S(1)} collective-permute-done((f32[24,128]{1,0:T(8,128)S(1)}, f32[24,128]{1,0:T(8,128)S(1)}, u32[]{:S(2)}, u32[]{:S(2)}) %collective-permute-start.14) | collective-permute-done | bytes 12320 | tf_op jit(solution)/shard_map/ppermute | solution.py:300
  54.1 3.5 %collective-permute-done.15.refs_3_ = f32[24,128]{1,0:T(8,128)S(1)} collective-permute-done((f32[24,128]{1,0:T(8,128)S(1)}, f32[24,128]{1,0:T(8,128)S(1)}, u32[]{:S(2)}, u32[]{:S(2)}) %collective-permute-start.15) | collective-permute-done | bytes 12320 | tf_op jit(solution)/shard_map/ppermute | solution.py:300
  57.6 0.0 copy-done.5
  57.6 1.4 %mix_terms.1 = f32[4,6,16,32]{3,2,1,0:T(8,128)} custom-call(s32[2]{0:T(128)S(1)} %pad_add_fusion.place_ref, f32[4,4]{1,0:T(4,128)S(1)} %copy-done.5, f32[24,128]{1,0:T(8,128)S(1)} %get-tuple-element.33.refs_0_, f32[24,128]{1,0:T(8,128)S(1)} %collective-permute-done.13.refs_1_, f32[24,128]{1,0:T(8,128)S(1)} %collective-permute-done.14.refs_2_, ...), custom_call_target="tpu_custom_call" | custom-call | bytes 49152 | tf_op jit(solution)/shard_map/mix_terms/pallas_call | solution.py:168
  (13 shorter events, 0.1 us)
Async XLA Ops:
  0.6 4.6 %copy-start = (s32[1,8,8,2]{2,3,1,0:T(2,128)S(1)}, s32[1,8,8,2]{2,3,1,0:T(2,128)}, u32[]{:S(2)}) copy-start(s32[1,8,8,2]{2,3,1,0:T(2,128)} %param.8) | copy-start | bytes 1540
  0.6 5.9 %collective-permute-start = (bf16[2560,128]{1,0:T(8,128)(2,1)}, bf16[2560,128]{1,0:T(8,128)(2,1)S(1)}, u32[]{:S(2)}, u32[]{:S(2)}) collective-permute-start(bf16[2560,128]{1,0:T(8,128)(2,1)} %bitcast.24), channel_id=1, source_target_pairs={{0,1},{1,0},{2,3},{3,2},{4,5},{5,4},{6,7},{7,6},{8,9},{9,8},{10,11... | collective-permute-start | bytes 1966088 | tf_op jit(solution)/shard_map/ppermute | solution.py:222
  1.2 18.4 %collective-permute-start.5 = (bf16[2560,128]{1,0:T(8,128)(2,1)}, bf16[2560,128]{1,0:T(8,128)(2,1)S(1)}, u32[]{:S(2)}, u32[]{:S(2)}) collective-permute-start(bf16[2560,128]{1,0:T(8,128)(2,1)} %bitcast.25), channel_id=1, source_target_pairs={{0,4},{1,5},{2,6},{3,7},{4,0},{5,1},{6,2},{7,3},{8,12},{9,13},{10,... | collective-permute-start | bytes 1966088 | tf_op jit(solution)/shard_map/ppermute | solution.py:219
  3.8 17.8 %collective-permute-start.4 = (bf16[2560,128]{1,0:T(8,128)(2,1)}, bf16[2560,128]{1,0:T(8,128)(2,1)S(1)}, u32[]{:S(2)}, u32[]{:S(2)}) collective-permute-start(bf16[2560,128]{1,0:T(8,128)(2,1)} %bitcast.26), channel_id=1, source_target_pairs={{0,2},{1,3},{2,0},{3,1},{4,6},{5,7},{6,4},{7,5},{8,10},{9,11},{10,... | collective-permute-start | bytes 1966088 | tf_op jit(solution)/shard_map/ppermute | solution.py:219
  5.3 0.7 %copy-start.6 = (s32[1,4,5]{2,1,0:T(4,128)S(1)}, s32[1,4,5]{2,1,0:T(4,128)}, u32[]{:S(2)}) copy-start(s32[1,4,5]{2,1,0:T(4,128)} %param.7) | copy-start | bytes 244
  6.6 0.9 %copy-start.3 = (bf16[1,512,128]{2,1,0:T(8,128)(2,1)S(1)}, bf16[1,512,128]{2,1,0:T(8,128)(2,1)}, u32[]{:S(2)}) copy-start(bf16[1,512,128]{2,1,0:T(8,128)(2,1)} %param.9) | copy-start | bytes 393220
  7.5 0.9 %copy-start.4 = (bf16[1,512,128]{2,1,0:T(8,128)(2,1)S(1)}, bf16[1,512,128]{2,1,0:T(8,128)(2,1)}, u32[]{:S(2)}) copy-start(bf16[1,512,128]{2,1,0:T(8,128)(2,1)} %param.10) | copy-start | bytes 393220
  8.5 16.7 %collective-permute-start.1 = (bf16[656,128]{1,0:T(8,128)(2,1)S(1)}, bf16[656,128]{1,0:T(8,128)(2,1)S(1)}, u32[]{:S(2)}, u32[]{:S(2)}) collective-permute-start(bf16[656,128]{1,0:T(8,128)(2,1)S(1)} %get-tuple-element.21), channel_id=1, source_target_pairs={{0,2},{1,3},{2,0},{3,1},{4,6},{5,7},{6,4},{7,5},{8,10},{9,11},{10,... | collective-permute-start | bytes 503816 | tf_op jit(solution)/shard_map/ppermute | solution.py:219
  9.1 16.1 %collective-permute-start.2 = (bf16[656,128]{1,0:T(8,128)(2,1)S(1)}, bf16[656,128]{1,0:T(8,128)(2,1)S(1)}, u32[]{:S(2)}, u32[]{:S(2)}) collective-permute-start(bf16[656,128]{1,0:T(8,128)(2,1)S(1)} %get-tuple-element.22), channel_id=1, source_target_pairs={{0,4},{1,5},{2,6},{3,7},{4,0},{5,1},{6,2},{7,3},{8,12},{9,13},{10,... | collective-permute-start | bytes 503816 | tf_op jit(solution)/shard_map/ppermute | solution.py:219
  9.5 18.8 %collective-permute-start.3 = (bf16[656,128]{1,0:T(8,128)(2,1)S(1)}, bf16[656,128]{1,0:T(8,128)(2,1)S(1)}, u32[]{:S(2)}, u32[]{:S(2)}) collective-permute-start(bf16[656,128]{1,0:T(8,128)(2,1)S(1)} %get-tuple-element.23), channel_id=1, source_target_pairs={{0,6},{1,7},{2,4},{3,5},{4,2},{5,3},{6,0},{7,1},{8,14},{9,15},{10,... | collective-permute-start | bytes 503816 | tf_op jit(solution)/shard_map/ppermute | solution.py:219
  22.6 12.5 %collective-permute-start.10 = (bf16[1280,128]{1,0:T(8,128)(2,1)}, bf16[1280,128]{1,0:T(8,128)(2,1)}, u32[]{:S(2)}, u32[]{:S(2)}) collective-permute-start(bf16[1280,128]{1,0:T(8,128)(2,1)} %get-tuple-element.30), channel_id=1, source_target_pairs={{0,2},{1,3},{2,0},{3,1},{4,6},{5,7},{6,4},{7,5},{8,10},{9,11},{10,... | collective-permute-start | bytes 983048 | tf_op jit(solution)/shard_map/ppermute | solution.py:219
  24.2 11.0 %collective-permute-start.9 = (bf16[1280,128]{1,0:T(8,128)(2,1)}, bf16[1280,128]{1,0:T(8,128)(2,1)}, u32[]{:S(2)}, u32[]{:S(2)}) collective-permute-start(bf16[1280,128]{1,0:T(8,128)(2,1)} %get-tuple-element.24.refs_4_), channel_id=1, source_target_pairs={{0,4},{1,5},{2,6},{3,7},{4,0},{5,1},{6,2},{7,3},{8,12},{9,13},{10,... | collective-permute-start | bytes 983048 | tf_op jit(solution)/shard_map/ppermute | solution.py:219
  25.1 5.5 %collective-permute-start.7 = (bf16[2560,128]{1,0:T(8,128)(2,1)S(1)}, bf16[2560,128]{1,0:T(8,128)(2,1)}, u32[]{:S(2)}, u32[]{:S(2)}) collective-permute-start(bf16[2560,128]{1,0:T(8,128)(2,1)S(1)} %get-tuple-element.25.refs_7_.refs_5_), channel_id=1, source_target_pairs={{0,1},{1,0},{2,3},{3,2},{4,5},{5,4},{6,7},{7,6},{8,9},{9,8},{10,11... | collective-permute-start | bytes 1966088 | tf_op jit(solution)/shard_map/ppermute | solution.py:222
  25.1 5.5 %collective-permute-start.8 = (bf16[2560,128]{1,0:T(8,128)(2,1)S(1)}, bf16[2560,128]{1,0:T(8,128)(2,1)}, u32[]{:S(2)}, u32[]{:S(2)}) collective-permute-start(bf16[2560,128]{1,0:T(8,128)(2,1)S(1)} %get-tuple-element.26.refs_9_.refs_7_), channel_id=1, source_target_pairs={{0,1},{1,0},{2,3},{3,2},{4,5},{5,4},{6,7},{7,6},{8,9},{9,8},{10,11... | collective-permute-start | bytes 1966088 | tf_op jit(solution)/shard_map/ppermute | solution.py:222
  28.3 2.2 %collective-permute-start.6 = (bf16[2624,128]{1,0:T(8,128)(2,1)S(1)}, bf16[2624,128]{1,0:T(8,128)(2,1)S(1)}, u32[]{:S(2)}, u32[]{:S(2)}) collective-permute-start(bf16[2624,128]{1,0:T(8,128)(2,1)S(1)} %join_pieces.1), channel_id=1, source_target_pairs={{0,1},{1,0},{2,3},{3,2},{4,5},{5,4},{6,7},{7,6},{8,9},{9,8},{10,11... | collective-permute-start | bytes 2015240 | tf_op jit(solution)/shard_map/ppermute | solution.py:222
  30.7 1.1 %copy-start.1 = (bf16[1,4,5,128,128]{4,3,2,1,0:T(8,128)(2,1)S(1)}, bf16[1,4,5,128,128]{4,3,2,1,0:T(8,128)(2,1)}, u32[]{:S(2)}) copy-start(bf16[1,4,5,128,128]{4,3,2,1,0:T(8,128)(2,1)} %param.6) | copy-start | bytes 1966084
  35.1 2.3 %copy-start.2 = (bf16[1,4,5,128,128]{4,3,2,1,0:T(8,128)(2,1)S(1)}, bf16[1,4,5,128,128]{4,3,2,1,0:T(8,128)(2,1)}, u32[]{:S(2)}) copy-start(bf16[1,4,5,128,128]{4,3,2,1,0:T(8,128)(2,1)} %param.6) | copy-start | bytes 1966084
  35.1 1.8 %collective-permute-start.11 = (bf16[1280,128]{1,0:T(8,128)(2,1)}, bf16[1280,128]{1,0:T(8,128)(2,1)S(1)}, u32[]{:S(2)}, u32[]{:S(2)}) collective-permute-start(bf16[1280,128]{1,0:T(8,128)(2,1)} %get-tuple-element.31.refs_9_), channel_id=1, source_target_pairs={{0,1},{1,0},{2,3},{3,2},{4,5},{5,4},{6,7},{7,6},{8,9},{9,8},{10,11... | collective-permute-start | bytes 983048 | tf_op jit(solution)/shard_map/ppermute | solution.py:222
  35.2 2.3 %collective-permute-start.12 = (bf16[1280,128]{1,0:T(8,128)(2,1)}, bf16[1280,128]{1,0:T(8,128)(2,1)S(1)}, u32[]{:S(2)}, u32[]{:S(2)}) collective-permute-start(bf16[1280,128]{1,0:T(8,128)(2,1)} %get-tuple-element.32.refs_10_), channel_id=1, source_target_pairs={{0,1},{1,0},{2,3},{3,2},{4,5},{5,4},{6,7},{7,6},{8,9},{9,8},{10,11... | collective-permute-start | bytes 983048 | tf_op jit(solution)/shard_map/ppermute | solution.py:222
  47.9 4.5 %collective-permute-start.13 = (f32[24,128]{1,0:T(8,128)S(1)}, f32[24,128]{1,0:T(8,128)S(1)}, u32[]{:S(2)}, u32[]{:S(2)}) collective-permute-start(f32[24,128]{1,0:T(8,128)S(1)} %get-tuple-element.34), channel_id=1, source_target_pairs={{0,8},{8,0},{16,24},{24,16},{1,9},{9,1},{17,25},{25,17},{2,10},{10... | collective-permute-start | bytes 36872 | tf_op jit(solution)/shard_map/ppermute | solution.py:300
  49.5 8.1 %copy-start.5 = (f32[4,4]{1,0:T(4,128)S(1)}, f32[4,4]{1,0:T(4,128)}, u32[]{:S(2)}) copy-start(f32[4,4]{1,0:T(4,128)} %weights_ref.1) | copy-start | bytes 196
  49.5 4.6 %collective-permute-start.14 = (f32[24,128]{1,0:T(8,128)S(1)}, f32[24,128]{1,0:T(8,128)S(1)}, u32[]{:S(2)}, u32[]{:S(2)}) collective-permute-start(f32[24,128]{1,0:T(8,128)S(1)} %get-tuple-element.35), channel_id=1, source_target_pairs={{0,16},{8,24},{16,0},{24,8},{1,17},{9,25},{17,1},{25,9},{2,18},{10... | collective-permute-start | bytes 36872 | tf_op jit(solution)/shard_map/ppermute | solution.py:300
  52.1 5.5 %collective-permute-start.15 = (f32[24,128]{1,0:T(8,128)S(1)}, f32[24,128]{1,0:T(8,128)S(1)}, u32[]{:S(2)}, u32[]{:S(2)}) collective-permute-start(f32[24,128]{1,0:T(8,128)S(1)} %get-tuple-element.36), channel_id=1, source_target_pairs={{0,24},{8,16},{16,8},{24,0},{1,25},{9,17},{17,9},{25,1},{2,26},{10... | collective-permute-start | bytes 36872 | tf_op jit(solution)/shard_map/ppermute | solution.py:300

commit v6 on v5

--- a/solution.py
+++ b/solution.py
@@ -150,13 +150,18 @@
 
 
 def mix_terms(place_ref, weights_ref, *refs):
-    terms_refs, out_ref = refs[:-1], refs[-1]
-    primes, steps, held, part = out_ref.shape
+    terms_refs, (out_ref, mixture, sent) = refs[:-3], refs[-3:]
+    primes, steps, held, part = mixture.shape
+    copies = []
     parts = [terms[...] for terms in terms_refs]
     for prime in range(primes):
         mixed = sum(weights_ref[prime, place_ref[0] ^ bits] * terms for bits, terms in enumerate(parts))
         groups = [mixed[:, group * part : (group + 1) * part] for group in range(primes)]
-        out_ref[prime] = jnp.concatenate(groups, axis=0).reshape(steps, held, part)
+        mixture[prime] = jnp.concatenate(groups, axis=0).reshape(steps, held, part)
+        copies.append(pltpu.make_async_copy(mixture.at[prime], out_ref.at[prime], sent.at[prime]))
+        copies[-1].start()
+    for copy in copies:
+        copy.wait()
 
 
 def on_chip(kernel, out_shape, smem, vmem, before=(), after=(), aliases=None, far_outs=(), scratch=(), flops=0, name=None):
@@ -304,6 +309,11 @@
         jax.ShapeDtypeStruct((primes, ITERS, held, width // primes), jnp.float32),
         [place, combine_weights],
         terms,
+        far_outs=[0],
+        scratch=[
+            pltpu.VMEM((primes, ITERS, held, width // primes), jnp.float32),
+            pltpu.SemaphoreType.DMA((primes,)),
+        ],
         name="mix_terms",
     )
     return mixed, last[None]

time: 59.2 us -> 59.2 us (level)
  no operation moved by 1% of the time
where the time goes in v6:
time: 59.2 us; the launch traced here: 59 us
  waiting for transfers between devices  22.5 us (38%)
  starting transfers between devices  15.8 us (27%)
  Pallas kernels  15.6 us (26%)
  local copies, waits for them, and re-layouts  3.99 us (7%)
  between operations  0.79 us (1%)
    pallas_call x7, Pallas kernels, on_chip(): pl.pallas_call(kernel, out_shape=out_shape, in_specs=[pl.BlockSpec(memory...  15.6 us
    ppermute x7, waiting for transfers between devices, to_chip(): return lax.ppermute(array, 'row', bits_apart(ranks, 2 * chip))  13.4 us
    ppermute x7, starting transfers between devices, to_chip(): return lax.ppermute(array, 'row', bits_apart(ranks, 2 * chip))  9.7 us
    ppermute x3, waiting for transfers between devices, whole_system(): lax.ppermute(terms[bits], 'prime', bits_apart(primes, bits))  5.27 us
    ppermute x3, starting transfers between devices, whole_system(): lax.ppermute(terms[bits], 'prime', bits_apart(primes, bits))  4.45 us
    ppermute x6, waiting for transfers between devices, to_core(): return lax.ppermute(array, 'row', bits_apart(ranks, 1))  3.86 us
    unnamed x14, local copies, waits for them, and re-layouts  3.51 us
    ppermute x6, starting transfers between devices, to_core(): return lax.ppermute(array, 'row', bits_apart(ranks, 1))  1.6 us
  transfers between devices with their start and end apart: 16, of which 10 were waited for; matrix products, arithmetic and copies ran while one was open for 1% of the time, Pallas kernels for 6%

profile of v6, /device:TPU:0, one launch (start us, length us, event | category | flops | bytes accessed | tf_op | source)
XLA Modules:
  0.0 59.0 jit_solution(5452702940144119125)
XLA Ops:
  0.6 0.0 copy-start
  0.6 0.5 collective-permute-start
  1.2 2.6 %collective-permute-start.5 = (bf16[2560,128]{1,0:T(8,128)(2,1)}, bf16[2560,128]{1,0:T(8,128)(2,1)S(1)}, u32[]{:S(2)}, u32[]{:S(2)}) collective-permute-start(bf16[2560,128]{1,0:T(8,128)(2,1)} %bitcast.25), channel_id=1, source_target_pairs={{0,4},{1,5},{2,6},{3,7},{4,0},{5,1},{6,2},{7,3},{8,12},{9,13},{10,... | collective-permute-start | bytes 1966088 | tf_op jit(solution)/shard_map/ppermute | solution.py:224
  3.8 1.5 %collective-permute-start.4 = (bf16[2560,128]{1,0:T(8,128)(2,1)}, bf16[2560,128]{1,0:T(8,128)(2,1)S(1)}, u32[]{:S(2)}, u32[]{:S(2)}) collective-permute-start(bf16[2560,128]{1,0:T(8,128)(2,1)} %bitcast.26), channel_id=1, source_target_pairs={{0,2},{1,3},{2,0},{3,1},{4,6},{5,7},{6,4},{7,5},{8,10},{9,11},{10,... | collective-permute-start | bytes 1966088 | tf_op jit(solution)/shard_map/ppermute | solution.py:224
  5.2 0.0 copy-done
  5.3 0.1 copy.16
  5.3 0.0 copy-start.6
  5.3 0.1 broadcast_in_dim.17
  5.4 0.6 %copy-done.6 = s32[1,4,5]{2,1,0:T(4,128)S(1)} copy-done((s32[1,4,5]{2,1,0:T(4,128)S(1)}, s32[1,4,5]{2,1,0:T(4,128)}, u32[]{:S(2)}) %copy-start.6) | copy-done | bytes 104
  6.0 0.1 copy.15
  6.1 0.2 select_reduce_fusion
  6.4 0.1 copy.17
  6.5 0.1 pad_add_fusion.place_ref
  6.6 0.0 collective-permute-done.after_ref.refs_6_.refs_4_
  6.6 0.0 copy-start.3
  6.6 0.9 %copy-done.3 = bf16[1,512,128]{2,1,0:T(8,128)(2,1)S(1)} copy-done((bf16[1,512,128]{2,1,0:T(8,128)(2,1)S(1)}, bf16[1,512,128]{2,1,0:T(8,128)(2,1)}, u32[]{:S(2)}) %copy-start.3) | copy-done | bytes 131096
  7.5 0.0 copy-start.4
  7.5 0.9 %copy-done.4 = bf16[1,512,128]{2,1,0:T(8,128)(2,1)S(1)} copy-done((bf16[1,512,128]{2,1,0:T(8,128)(2,1)S(1)}, bf16[1,512,128]{2,1,0:T(8,128)(2,1)}, u32[]{:S(2)}) %copy-start.4) | copy-done | bytes 131096
  8.4 0.1 pack_pieces.1
  8.5 0.6 %collective-permute-start.1 = (bf16[656,128]{1,0:T(8,128)(2,1)S(1)}, bf16[656,128]{1,0:T(8,128)(2,1)S(1)}, u32[]{:S(2)}, u32[]{:S(2)}) collective-permute-start(bf16[656,128]{1,0:T(8,128)(2,1)S(1)} %get-tuple-element.21), channel_id=1, source_target_pairs={{0,2},{1,3},{2,0},{3,1},{4,6},{5,7},{6,4},{7,5},{8,10},{9,11},{10,... | collective-permute-start | bytes 503816 | tf_op jit(solution)/shard_map/ppermute | solution.py:224
  9.1 0.4 collective-permute-start.2
  9.5 2.6 %collective-permute-start.3 = (bf16[656,128]{1,0:T(8,128)(2,1)S(1)}, bf16[656,128]{1,0:T(8,128)(2,1)S(1)}, u32[]{:S(2)}, u32[]{:S(2)}) collective-permute-start(bf16[656,128]{1,0:T(8,128)(2,1)S(1)} %get-tuple-element.23), channel_id=1, source_target_pairs={{0,6},{1,7},{2,4},{3,5},{4,2},{5,3},{6,0},{7,1},{8,14},{9,15},{10,... | collective-permute-start | bytes 503816 | tf_op jit(solution)/shard_map/ppermute | solution.py:224
  12.0 7.5 %collective-permute-done.5.second_ref = bf16[2560,128]{1,0:T(8,128)(2,1)S(1)} collective-permute-done((bf16[2560,128]{1,0:T(8,128)(2,1)}, bf16[2560,128]{1,0:T(8,128)(2,1)S(1)}, u32[]{:S(2)}, u32[]{:S(2)}) %collective-permute-start.5) | collective-permute-done | bytes 655392 | tf_op jit(solution)/shard_map/ppermute | solution.py:224
  19.6 2.0 %collective-permute-done.4.first_ref = bf16[2560,128]{1,0:T(8,128)(2,1)S(1)} collective-permute-done((bf16[2560,128]{1,0:T(8,128)(2,1)}, bf16[2560,128]{1,0:T(8,128)(2,1)S(1)}, u32[]{:S(2)}, u32[]{:S(2)}) %collective-permute-start.4) | collective-permute-done | bytes 655392 | tf_op jit(solution)/shard_map/ppermute | solution.py:224
  21.5 1.1 %cut_halves.1 = (bf16[2560,128]{1,0:T(8,128)(2,1)S(1)}, bf16[2560,128]{1,0:T(8,128)(2,1)S(1)}, bf16[1280,128]{1,0:T(8,128)(2,1)}, bf16[1280,128]{1,0:T(8,128)(2,1)}) custom-call(bf16[2560,128]{1,0:T(8,128)(2,1)S(1)} %collective-permute-done.4.first_ref, ...), custom_call_target="tpu_custom_call", output_to_operand_aliasing={{0}: (0, {}), {1}: (1, {})} | custom-call | tf_op jit(solution)/shard_map/cut_halves/pallas_call | solution.py:173
  22.6 1.6 %collective-permute-start.10 = (bf16[1280,128]{1,0:T(8,128)(2,1)}, bf16[1280,128]{1,0:T(8,128)(2,1)}, u32[]{:S(2)}, u32[]{:S(2)}) collective-permute-start(bf16[1280,128]{1,0:T(8,128)(2,1)} %get-tuple-element.30), channel_id=1, source_target_pairs={{0,2},{1,3},{2,0},{3,1},{4,6},{5,7},{6,4},{7,5},{8,10},{9,11},{10,... | collective-permute-start | bytes 983048 | tf_op jit(solution)/shard_map/ppermute | solution.py:224
  24.2 0.5 collective-permute-start.9
  24.7 0.5 collective-permute-done.1.refs_1_
  25.1 0.0 collective-permute-start.7
  25.1 0.0 collective-permute-done.2.refs_2_
  25.1 0.5 collective-permute-start.8
  25.7 2.6 %collective-permute-done.3.refs_3_ = bf16[656,128]{1,0:T(8,128)(2,1)S(1)} collective-permute-done((bf16[656,128]{1,0:T(8,128)(2,1)S(1)}, bf16[656,128]{1,0:T(8,128)(2,1)S(1)}, u32[]{:S(2)}, u32[]{:S(2)}) %collective-permute-start.3) | collective-permute-done | bytes 167968 | tf_op jit(solution)/shard_map/ppermute | solution.py:224
  28.3 0.1 collective-permute-start.6
  28.5 2.1 %collective-permute-done.6.refs_4_ = bf16[2624,128]{1,0:T(8,128)(2,1)S(1)} collective-permute-done((bf16[2624,128]{1,0:T(8,128)(2,1)S(1)}, bf16[2624,128]{1,0:T(8,128)(2,1)S(1)}, u32[]{:S(2)}, u32[]{:S(2)}) %collective-permute-start.6) | collective-permute-done | bytes 671776 | tf_op jit(solution)/shard_map/ppermute | solution.py:227
  30.5 0.1 reshape.18.columns_ref
  30.7 0.0 collective-permute-done.7.refs_8_.refs_6_
  30.7 0.0 collective-permute-done.8.refs_10_.refs_8_
  30.7 0.0 copy-start.1
  30.7 1.1 %copy-done.1 = bf16[1,4,5,128,128]{4,3,2,1,0:T(8,128)(2,1)S(1)} copy-done((bf16[1,4,5,128,128]{4,3,2,1,0:T(8,128)(2,1)S(1)}, bf16[1,4,5,128,128]{4,3,2,1,0:T(8,128)(2,1)}, u32[]{:S(2)}) %copy-start.1) | copy-done | bytes 655384
  31.8 2.6 %first_step.1 = (bf16[32,128,128]{2,1,0:T(8,128)(2,1)S(1)}, bf16[24,128,128]{2,1,0:T(8,128)(2,1)S(1)}, bf16[8,64,128]{2,1,0:T(8,128)(2,1)S(1)}) custom-call(s32[160]{0:T(256)S(1)} %reshape.18.columns_ref, s32[2]{0:T(128)S(1)} %pad_add_fusion.place_ref, bf16[656,128]{1,0:T(8,128)(2,1)S(1)} %get-tuple-element.20.after_ref.refs_0_, ...), custom_call_target="tpu_custom_call" | custom-call | flops 503316480 | bytes 5275648 | tf_op jit(solution)/shard_map/first_step/pallas_call | solution.py:173
  34.4 0.8 %collective-permute-done.10.refs_1_ = bf16[1280,128]{1,0:T(8,128)(2,1)} collective-permute-done((bf16[1280,128]{1,0:T(8,128)(2,1)}, bf16[1280,128]{1,0:T(8,128)(2,1)}, u32[]{:S(2)}, u32[]{:S(2)}) %collective-permute-start.10) | collective-permute-done | bytes 327712 | tf_op jit(solution)/shard_map/ppermute | solution.py:224
  35.1 0.0 collective-permute-done.9.refs_0_
  35.1 0.0 copy-start.2
  35.1 0.0 collective-permute-start.11
  35.2 0.5 collective-permute-start.12
  35.7 1.3 %collective-permute-done.11.refs_11_ = bf16[1280,128]{1,0:T(8,128)(2,1)S(1)} collective-permute-done((bf16[1280,128]{1,0:T(8,128)(2,1)}, bf16[1280,128]{1,0:T(8,128)(2,1)S(1)}, u32[]{:S(2)}, u32[]{:S(2)}) %collective-permute-start.11) | collective-permute-done | bytes 327712 | tf_op jit(solution)/shard_map/ppermute | solution.py:227
  37.0 0.5 collective-permute-done.12.refs_12_
  37.5 0.0 copy-done.2
  37.5 10.4 %all_steps.1 = (f32[24,128]{1,0:T(8,128)S(1)}, f32[24,128]{1,0:T(8,128)S(1)}, f32[24,128]{1,0:T(8,128)S(1)}, f32[24,128]{1,0:T(8,128)S(1)}, bf16[512,128]{1,0:T(8,128)(2,1)}) custom-call(s32[160]{0:T(256)S(1)} %reshape.18.columns_ref, s32[2]{0:T(128)S(1)} %pad_add_fusion.place_ref, bf16[32,128,128]{2,1,0:T(8,128)(2,1)S(1)} %get-tuple-element.27.refs_0_, ...), custom_call_target="tpu_custom_call" | custom-call | flops 4026531840 | bytes 7208960 | tf_op jit(solution)/shard_map/all_steps/pallas_call | solution.py:173
  47.9 1.6 %collective-permute-start.13 = (f32[24,128]{1,0:T(8,128)S(1)}, f32[24,128]{1,0:T(8,128)S(1)}, u32[]{:S(2)}, u32[]{:S(2)}) collective-permute-start(f32[24,128]{1,0:T(8,128)S(1)} %get-tuple-element.34), channel_id=1, source_target_pairs={{0,8},{8,0},{16,24},{24,16},{1,9},{9,1},{17,25},{25,17},{2,10},{10... | collective-permute-start | bytes 36872 | tf_op jit(solution)/shard_map/ppermute | solution.py:305
  49.5 0.0 copy-start.5
  49.5 2.6 %collective-permute-start.14 = (f32[24,128]{1,0:T(8,128)S(1)}, f32[24,128]{1,0:T(8,128)S(1)}, u32[]{:S(2)}, u32[]{:S(2)}) collective-permute-start(f32[24,128]{1,0:T(8,128)S(1)} %get-tuple-element.35), channel_id=1, source_target_pairs={{0,16},{8,24},{16,0},{24,8},{1,17},{9,25},{17,1},{25,9},{2,18},{10... | collective-permute-start | bytes 36872 | tf_op jit(solution)/shard_map/ppermute | solution.py:305
  52.1 0.2 collective-permute-start.15
  52.3 0.0 collective-permute-done.13.refs_1_
  52.3 1.8 %collective-permute-done.14.refs_2_ = f32[24,128]{1,0:T(8,128)S(1)} collective-permute-done((f32[24,128]{1,0:T(8,128)S(1)}, f32[24,128]{1,0:T(8,128)S(1)}, u32[]{:S(2)}, u32[]{:S(2)}) %collective-permute-start.14) | collective-permute-done | bytes 12320 | tf_op jit(solution)/shard_map/ppermute | solution.py:305
  54.1 3.5 %collective-permute-done.15.refs_3_ = f32[24,128]{1,0:T(8,128)S(1)} collective-permute-done((f32[24,128]{1,0:T(8,128)S(1)}, f32[24,128]{1,0:T(8,128)S(1)}, u32[]{:S(2)}, u32[]{:S(2)}) %collective-permute-start.15) | collective-permute-done | bytes 12320 | tf_op jit(solution)/shard_map/ppermute | solution.py:305
  57.6 0.0 copy-done.5
  57.6 1.4 %mix_terms.1 = f32[4,6,16,32]{3,2,1,0:T(8,128)} custom-call(s32[2]{0:T(128)S(1)} %pad_add_fusion.place_ref, f32[4,4]{1,0:T(4,128)S(1)} %copy-done.5, f32[24,128]{1,0:T(8,128)S(1)} %get-tuple-element.33.refs_0_, f32[24,128]{1,0:T(8,128)S(1)} %collective-permute-done.13.refs_1_, f32[24,128]{1,0:T(8,128)S(1)} %collective-permute-done.14.refs_2_, ...), custom_call_target="tpu_custom_call" | custom-call | bytes 49152 | tf_op jit(solution)/shard_map/mix_terms/pallas_call | solution.py:173
  (13 shorter events, 0.1 us)
Async XLA Ops:
  0.6 4.6 %copy-start = (s32[1,8,8,2]{2,3,1,0:T(2,128)S(1)}, s32[1,8,8,2]{2,3,1,0:T(2,128)}, u32[]{:S(2)}) copy-start(s32[1,8,8,2]{2,3,1,0:T(2,128)} %param.8) | copy-start | bytes 1540
  0.6 5.9 %collective-permute-start = (bf16[2560,128]{1,0:T(8,128)(2,1)}, bf16[2560,128]{1,0:T(8,128)(2,1)S(1)}, u32[]{:S(2)}, u32[]{:S(2)}) collective-permute-start(bf16[2560,128]{1,0:T(8,128)(2,1)} %bitcast.24), channel_id=1, source_target_pairs={{0,1},{1,0},{2,3},{3,2},{4,5},{5,4},{6,7},{7,6},{8,9},{9,8},{10,11... | collective-permute-start | bytes 1966088 | tf_op jit(solution)/shard_map/ppermute | solution.py:227
  1.2 18.4 %collective-permute-start.5 = (bf16[2560,128]{1,0:T(8,128)(2,1)}, bf16[2560,128]{1,0:T(8,128)(2,1)S(1)}, u32[]{:S(2)}, u32[]{:S(2)}) collective-permute-start(bf16[2560,128]{1,0:T(8,128)(2,1)} %bitcast.25), channel_id=1, source_target_pairs={{0,4},{1,5},{2,6},{3,7},{4,0},{5,1},{6,2},{7,3},{8,12},{9,13},{10,... | collective-permute-start | bytes 1966088 | tf_op jit(solution)/shard_map/ppermute | solution.py:224
  3.8 17.8 %collective-permute-start.4 = (bf16[2560,128]{1,0:T(8,128)(2,1)}, bf16[2560,128]{1,0:T(8,128)(2,1)S(1)}, u32[]{:S(2)}, u32[]{:S(2)}) collective-permute-start(bf16[2560,128]{1,0:T(8,128)(2,1)} %bitcast.26), channel_id=1, source_target_pairs={{0,2},{1,3},{2,0},{3,1},{4,6},{5,7},{6,4},{7,5},{8,10},{9,11},{10,... | collective-permute-start | bytes 1966088 | tf_op jit(solution)/shard_map/ppermute | solution.py:224
  5.3 0.7 %copy-start.6 = (s32[1,4,5]{2,1,0:T(4,128)S(1)}, s32[1,4,5]{2,1,0:T(4,128)}, u32[]{:S(2)}) copy-start(s32[1,4,5]{2,1,0:T(4,128)} %param.7) | copy-start | bytes 244
  6.6 0.9 %copy-start.3 = (bf16[1,512,128]{2,1,0:T(8,128)(2,1)S(1)}, bf16[1,512,128]{2,1,0:T(8,128)(2,1)}, u32[]{:S(2)}) copy-start(bf16[1,512,128]{2,1,0:T(8,128)(2,1)} %param.9) | copy-start | bytes 393220
  7.5 0.9 %copy-start.4 = (bf16[1,512,128]{2,1,0:T(8,128)(2,1)S(1)}, bf16[1,512,128]{2,1,0:T(8,128)(2,1)}, u32[]{:S(2)}) copy-start(bf16[1,512,128]{2,1,0:T(8,128)(2,1)} %param.10) | copy-start | bytes 393220
  8.5 16.7 %collective-permute-start.1 = (bf16[656,128]{1,0:T(8,128)(2,1)S(1)}, bf16[656,128]{1,0:T(8,128)(2,1)S(1)}, u32[]{:S(2)}, u32[]{:S(2)}) collective-permute-start(bf16[656,128]{1,0:T(8,128)(2,1)S(1)} %get-tuple-element.21), channel_id=1, source_target_pairs={{0,2},{1,3},{2,0},{3,1},{4,6},{5,7},{6,4},{7,5},{8,10},{9,11},{10,... | collective-permute-start | bytes 503816 | tf_op jit(solution)/shard_map/ppermute | solution.py:224
  9.1 16.1 %collective-permute-start.2 = (bf16[656,128]{1,0:T(8,128)(2,1)S(1)}, bf16[656,128]{1,0:T(8,128)(2,1)S(1)}, u32[]{:S(2)}, u32[]{:S(2)}) collective-permute-start(bf16[656,128]{1,0:T(8,128)(2,1)S(1)} %get-tuple-element.22), channel_id=1, source_target_pairs={{0,4},{1,5},{2,6},{3,7},{4,0},{5,1},{6,2},{7,3},{8,12},{9,13},{10,... | collective-permute-start | bytes 503816 | tf_op jit(solution)/shard_map/ppermute | solution.py:224
  9.5 18.8 %collective-permute-start.3 = (bf16[656,128]{1,0:T(8,128)(2,1)S(1)}, bf16[656,128]{1,0:T(8,128)(2,1)S(1)}, u32[]{:S(2)}, u32[]{:S(2)}) collective-permute-start(bf16[656,128]{1,0:T(8,128)(2,1)S(1)} %get-tuple-element.23), channel_id=1, source_target_pairs={{0,6},{1,7},{2,4},{3,5},{4,2},{5,3},{6,0},{7,1},{8,14},{9,15},{10,... | collective-permute-start | bytes 503816 | tf_op jit(solution)/shard_map/ppermute | solution.py:224
  22.6 12.5 %collective-permute-start.10 = (bf16[1280,128]{1,0:T(8,128)(2,1)}, bf16[1280,128]{1,0:T(8,128)(2,1)}, u32[]{:S(2)}, u32[]{:S(2)}) collective-permute-start(bf16[1280,128]{1,0:T(8,128)(2,1)} %get-tuple-element.30), channel_id=1, source_target_pairs={{0,2},{1,3},{2,0},{3,1},{4,6},{5,7},{6,4},{7,5},{8,10},{9,11},{10,... | collective-permute-start | bytes 983048 | tf_op jit(solution)/shard_map/ppermute | solution.py:224
  24.2 11.0 %collective-permute-start.9 = (bf16[1280,128]{1,0:T(8,128)(2,1)}, bf16[1280,128]{1,0:T(8,128)(2,1)}, u32[]{:S(2)}, u32[]{:S(2)}) collective-permute-start(bf16[1280,128]{1,0:T(8,128)(2,1)} %get-tuple-element.24.refs_4_), channel_id=1, source_target_pairs={{0,4},{1,5},{2,6},{3,7},{4,0},{5,1},{6,2},{7,3},{8,12},{9,13},{10,... | collective-permute-start | bytes 983048 | tf_op jit(solution)/shard_map/ppermute | solution.py:224
  25.1 5.5 %collective-permute-start.7 = (bf16[2560,128]{1,0:T(8,128)(2,1)S(1)}, bf16[2560,128]{1,0:T(8,128)(2,1)}, u32[]{:S(2)}, u32[]{:S(2)}) collective-permute-start(bf16[2560,128]{1,0:T(8,128)(2,1)S(1)} %get-tuple-element.25.refs_7_.refs_5_), channel_id=1, source_target_pairs={{0,1},{1,0},{2,3},{3,2},{4,5},{5,4},{6,7},{7,6},{8,9},{9,8},{10,11... | collective-permute-start | bytes 1966088 | tf_op jit(solution)/shard_map/ppermute | solution.py:227
  25.1 5.5 %collective-permute-start.8 = (bf16[2560,128]{1,0:T(8,128)(2,1)S(1)}, bf16[2560,128]{1,0:T(8,128)(2,1)}, u32[]{:S(2)}, u32[]{:S(2)}) collective-permute-start(bf16[2560,128]{1,0:T(8,128)(2,1)S(1)} %get-tuple-element.26.refs_9_.refs_7_), channel_id=1, source_target_pairs={{0,1},{1,0},{2,3},{3,2},{4,5},{5,4},{6,7},{7,6},{8,9},{9,8},{10,11... | collective-permute-start | bytes 1966088 | tf_op jit(solution)/shard_map/ppermute | solution.py:227
  28.3 2.2 %collective-permute-start.6 = (bf16[2624,128]{1,0:T(8,128)(2,1)S(1)}, bf16[2624,128]{1,0:T(8,128)(2,1)S(1)}, u32[]{:S(2)}, u32[]{:S(2)}) collective-permute-start(bf16[2624,128]{1,0:T(8,128)(2,1)S(1)} %join_pieces.1), channel_id=1, source_target_pairs={{0,1},{1,0},{2,3},{3,2},{4,5},{5,4},{6,7},{7,6},{8,9},{9,8},{10,11... | collective-permute-start | bytes 2015240 | tf_op jit(solution)/shard_map/ppermute | solution.py:227
  30.7 1.1 %copy-start.1 = (bf16[1,4,5,128,128]{4,3,2,1,0:T(8,128)(2,1)S(1)}, bf16[1,4,5,128,128]{4,3,2,1,0:T(8,128)(2,1)}, u32[]{:S(2)}) copy-start(bf16[1,4,5,128,128]{4,3,2,1,0:T(8,128)(2,1)} %param.6) | copy-start | bytes 1966084
  35.1 2.3 %copy-start.2 = (bf16[1,4,5,128,128]{4,3,2,1,0:T(8,128)(2,1)S(1)}, bf16[1,4,5,128,128]{4,3,2,1,0:T(8,128)(2,1)}, u32[]{:S(2)}) copy-start(bf16[1,4,5,128,128]{4,3,2,1,0:T(8,128)(2,1)} %param.6) | copy-start | bytes 1966084
  35.1 1.8 %collective-permute-start.11 = (bf16[1280,128]{1,0:T(8,128)(2,1)}, bf16[1280,128]{1,0:T(8,128)(2,1)S(1)}, u32[]{:S(2)}, u32[]{:S(2)}) collective-permute-start(bf16[1280,128]{1,0:T(8,128)(2,1)} %get-tuple-element.31.refs_9_), channel_id=1, source_target_pairs={{0,1},{1,0},{2,3},{3,2},{4,5},{5,4},{6,7},{7,6},{8,9},{9,8},{10,11... | collective-permute-start | bytes 983048 | tf_op jit(solution)/shard_map/ppermute | solution.py:227
  35.2 2.3 %collective-permute-start.12 = (bf16[1280,128]{1,0:T(8,128)(2,1)}, bf16[1280,128]{1,0:T(8,128)(2,1)S(1)}, u32[]{:S(2)}, u32[]{:S(2)}) collective-permute-start(bf16[1280,128]{1,0:T(8,128)(2,1)} %get-tuple-element.32.refs_10_), channel_id=1, source_target_pairs={{0,1},{1,0},{2,3},{3,2},{4,5},{5,4},{6,7},{7,6},{8,9},{9,8},{10,11... | collective-permute-start | bytes 983048 | tf_op jit(solution)/shard_map/ppermute | solution.py:227
  47.9 4.5 %collective-permute-start.13 = (f32[24,128]{1,0:T(8,128)S(1)}, f32[24,128]{1,0:T(8,128)S(1)}, u32[]{:S(2)}, u32[]{:S(2)}) collective-permute-start(f32[24,128]{1,0:T(8,128)S(1)} %get-tuple-element.34), channel_id=1, source_target_pairs={{0,8},{8,0},{16,24},{24,16},{1,9},{9,1},{17,25},{25,17},{2,10},{10... | collective-permute-start | bytes 36872 | tf_op jit(solution)/shard_map/ppermute | solution.py:305
  49.5 8.1 %copy-start.5 = (f32[4,4]{1,0:T(4,128)S(1)}, f32[4,4]{1,0:T(4,128)}, u32[]{:S(2)}) copy-start(f32[4,4]{1,0:T(4,128)} %weights_ref.1) | copy-start | bytes 196
  49.5 4.6 %collective-permute-start.14 = (f32[24,128]{1,0:T(8,128)S(1)}, f32[24,128]{1,0:T(8,128)S(1)}, u32[]{:S(2)}, u32[]{:S(2)}) collective-permute-start(f32[24,128]{1,0:T(8,128)S(1)} %get-tuple-element.35), channel_id=1, source_target_pairs={{0,16},{8,24},{16,0},{24,8},{1,17},{9,25},{17,1},{25,9},{2,18},{10... | collective-permute-start | bytes 36872 | tf_op jit(solution)/shard_map/ppermute | solution.py:305
  52.1 5.5 %collective-permute-start.15 = (f32[24,128]{1,0:T(8,128)S(1)}, f32[24,128]{1,0:T(8,128)S(1)}, u32[]{:S(2)}, u32[]{:S(2)}) collective-permute-start(f32[24,128]{1,0:T(8,128)S(1)} %get-tuple-element.36), channel_id=1, source_target_pairs={{0,24},{8,16},{16,8},{24,0},{1,25},{9,17},{17,9},{25,1},{2,26},{10... | collective-permute-start | bytes 36872 | tf_op jit(solution)/shard_map/ppermute | solution.py:305
